TPU v7x, 32 devices: a whole 2x2x4 slice. The times are simulated.
32 devices in a mesh: gx: 4 (over x, core), gy: 2 (over y), gz: 4 (over z).
Axes of the slice: x: 2, y: 2, z: 4, core: 2. Of those that a mesh axis runs over, the one named last changes fastest.
Arguments:
- positions: float32 [3, 4, 2, 8, 256], P(None, 'gx', 'gy', 'gz'), may hold values from 0 to 1
- velocities: float32 [3, 4, 2, 8, 256], P(None, 'gx', 'gy', 'gz'), may hold values from -2 to 2
- mass: float32 [4, 2, 8, 256], P('gx', 'gy', 'gz'), may hold values from 0.03 to 0.3
- counts: int32 [4, 2, 8], P('gx', 'gy', 'gz'), may hold values from 1 to 256, as said below
Outputs:
- new_positions: float32 [3, 4, 2, 8, 256], P(None, 'gx', 'gy', 'gz')
- new_velocities: float32 [3, 4, 2, 8, 256], P(None, 'gx', 'gy', 'gz')
Inputs may be any that keep to these rules, and one draw needn't show every extreme that they name: `counts`: particles of a bin fill its first slots; every bin holds at least 128 particles, and some bin holds exactly 256 particles in every draw.
All inputs are finite; a program needn't handle non-finite values.
Results may differ from a plain program's by a relative error of at most 0.0001.
Values sent between devices are 32-bit elements; how exact they have to be, the bound alone decides.
No kernel may reach another device: no remote copies, remote signals or barrier semaphores. Data moves between devices by JAX's collectives and lax.ppermute only.
A program may use at most 64 MiB of HBM per device.

v0:
```python
import functools

import jax
import jax.numpy as jnp
from jax import lax
from jax.experimental import pallas as pl
from jax.experimental.pallas import tpu as pltpu
from jax.sharding import PartitionSpec as P

SUBCYCLES = 2

time_step = 0.25

CENTRE = (0.5, 0.5, 1.0)
F32, BF16 = jnp.float32, jnp.bfloat16


def parts(value):
    high = value.astype(BF16).astype(F32)
    rest = value - high
    mid = rest.astype(BF16).astype(F32)
    return high, mid, rest - mid


def row_index(rows, slots):
    return lax.broadcasted_iota(jnp.int32, (rows, slots), 0)


def shifted(packed, offset):
    row = row_index(*packed.shape)
    x, y, z = [jnp.asarray(o, F32) - c for o, c in zip(offset, CENTRE)]
    move = jnp.where(row == 0, x, jnp.where(row == 1, y, jnp.where(row == 2, z, 0.0)))
    return packed + move


def source_rows(moved):
    row = row_index(*moved.shape)
    square = jnp.sum(jnp.where(row < 3, moved * moved, 0.0), axis=0, keepdims=True)
    head = jnp.where(row < 3, moved, square)
    tail = jnp.where(row == 0, 1.0, 0.0).astype(F32)
    high, mid, low = parts(jnp.concatenate([head, tail], axis=0))
    distance = jnp.concatenate([high, high, high, mid, mid, low], axis=0).astype(BF16)
    mass = moved[3:4]
    carried = jnp.where(row < 3, moved * mass, mass)
    high, mid, low = parts(jnp.concatenate([carried, jnp.zeros_like(carried)], axis=0))
    summed = jnp.concatenate([high, mid, low, jnp.zeros_like(low)], axis=0).astype(BF16)
    return distance, summed


def target_rows(moved):
    slots = moved.shape[-1]
    row = row_index(4, slots)
    square = jnp.sum(jnp.where(row < 3, moved * moved, 0.0), axis=0, keepdims=True)
    head = jnp.where(row < 3, 2.0 * moved, -1.0)
    tail = jnp.where(row == 0, 1.0 - square, 0.0)
    high, mid, low = parts(jnp.concatenate([head, tail], axis=0))
    return jnp.concatenate([high, mid, low, high, mid, high], axis=0).T.astype(BF16)


def pair_weight(target, source):
    near = jnp.maximum(jnp.dot(target, source, preferred_element_type=F32), 0.0)
    weight = near * near * near
    high = weight.astype(BF16)
    return high, (weight - high.astype(F32)).astype(BF16)


def contract(weights, rows):
    return lax.dot_general(weights, rows, (((1,), (1,)), ((), ())), preferred_element_type=F32)


def pack_kernel(counts_ref, place_ref, mass_ref, packed_ref, keep_ref):
    for z in range(2):
        mass = mass_ref[0, 0, z : z + 1, :]
        keep = lax.broadcasted_iota(jnp.int32, mass.shape, 1) < counts_ref[0, :, z : z + 1]
        rows = [place_ref[c, 0, 0, z : z + 1, :] for c in range(3)]
        packed_ref[z] = jnp.concatenate(rows + [jnp.where(keep, mass, 0.0)], axis=0)
        keep_ref[z] = jnp.broadcast_to(jnp.where(keep, 1.0, 0.0), keep_ref.shape[1:])


def ahead(axis):
    return 1 - 2 * lax.rem(lax.axis_index(axis), 2)


def y_shifts(size):
    if size == 2:
        return [[0], [-1, 1]]
    return [[0], [ahead("gy")], [-ahead("gy")]]


def list_chunk(list_ref, chunk):
    return jnp.concatenate([list_ref[2 * chunk], list_ref[2 * chunk + 1]], axis=1)[0:4]


def fill(near_ref, sum_ref, list_ref, entries):
    half = list_ref.shape[-1]
    lane = lax.broadcasted_iota(jnp.int32, (8, half), 1)
    list_ref[...] = jnp.zeros_like(list_ref)
    place = jnp.int32(0)
    held = {}
    for number, (ref, index, offset) in enumerate(entries):
        packed = ref[index]
        head, tail = shifted(packed[:, :half], offset), shifted(packed[:, half:], offset)
        if number == len(entries) - 1 and number % 2 == 0:
            list_ref[0] = jnp.concatenate([head, jnp.zeros_like(head)], axis=0)
        else:
            distance, summed = source_rows(head)
            near_ref[:, number * half : (number + 1) * half] = distance
            sum_ref[:, number * half : (number + 1) * half] = summed
        held[number] = tail
    if len(entries) % 2:
        place = place + half
    known = {}
    for number, (ref, index, offset) in enumerate(entries):
        tail = held[number]
        key = (id(ref),) + (index if isinstance(index, tuple) else (index,))
        if key not in known:
            present = jnp.where(tail[3:4] != 0.0, lane[0:1] + 1, 0).astype(F32)
            known[key] = jnp.max(present).astype(jnp.int32)
        length = known[key]
        tile, turn = lax.div(place, half), lax.rem(place, half)
        tail = jnp.where(lane < length, jnp.concatenate([tail, jnp.zeros_like(tail)], axis=0), 0.0)
        tail = pltpu.roll(tail, turn, 1)
        list_ref[tile] += jnp.where(lane >= turn, tail, 0.0)
        list_ref[tile + 1] += jnp.where(lane < turn, tail, 0.0)
        place = place + length
    done = (len(entries) // 2) * 2 * half
    for chunk in range((near_ref.shape[1] - done) // (2 * half)):
        distance, summed = source_rows(list_chunk(list_ref, chunk))
        near_ref[:, done + chunk * 2 * half : done + (chunk + 1) * 2 * half] = distance
        sum_ref[:, done + chunk * 2 * half : done + (chunk + 1) * 2 * half] = summed
    return place


def gathered(target, nears, sums):
    highs, lows = [], []
    for near in nears:
        high, low = pair_weight(target, near)
        highs.append(high)
        lows.append(low)
    rows = jnp.concatenate(sums, axis=1)
    return contract(jnp.concatenate(highs + lows, axis=1), jnp.concatenate([rows, rows], axis=1))


def sums_over(targets, totals, near_ref, sum_ref, list_ref, length, sources, tiles):
    wide = 2 * list_ref.shape[-1]
    steps = near_ref.shape[1] // (tiles * wide)

    def step(number, totals):
        nears, sums = [], []
        for tile in range(tiles):
            lanes = pl.ds(pl.multiple_of((number * tiles + tile) * wide, wide), wide)
            nears.append(near_ref[:, lanes])
            sums.append(sum_ref[:, lanes])
        return tuple(total + gathered(target, nears, sums) for target, total in zip(targets, totals))

    totals = step(0, totals) if steps == 1 else lax.fori_loop(0, steps, step, tuple(totals))
    done = steps * tiles - sources // 2

    def rest(number, totals):
        near, summed = source_rows(list_chunk(list_ref, number))
        return tuple(total + gathered(target, [near], [summed]) for target, total in zip(targets, totals))

    return lax.fori_loop(done, jnp.maximum(lax.div(length + (wide - 1), wide), done), rest, tuple(totals))


def plane_kernel(size_y, *refs):
    planes, (target_ref, total_ref, near_ref, sum_ref, list_ref) = refs[:-5], refs[-5:]
    own_ref = planes[0]
    for z in range(2):
        target_ref[z] = target_rows(shifted(own_ref[z], (0, 0, z)))
    entries = []
    for ref, shifts in zip(planes, y_shifts(size_y)):
        for y in shifts:
            entries += [(ref, z, (0, y, z)) for z in range(2)]
    length = fill(near_ref, sum_ref, list_ref, entries)
    zero = jnp.zeros(total_ref.shape[1:], F32)
    targets = [target_ref[z] for z in range(2)]
    totals = sums_over(targets, (zero, zero), near_ref, sum_ref, list_ref, length, len(entries), 5)
    for z in range(2):
        total_ref[z] = totals[z]


def slab_kernel(size_y, target_ref, before_ref, near_x_ref, far_x_ref, total_ref, near_ref, sum_ref, list_ref):
    entries = []
    for ref, x in ((near_x_ref, ahead("gx")), (far_x_ref, -ahead("gx"))):
        for plane, shifts in enumerate(y_shifts(size_y)):
            for y in shifts:
                entries += [(ref, (plane, z), (x, y, z)) for z in range(2)]
    length = fill(near_ref, sum_ref, list_ref, entries)
    targets = [target_ref[z] for z in range(2)]
    totals = sums_over(targets, (before_ref[0], before_ref[1]), near_ref, sum_ref, list_ref, length, len(entries), 3)
    for z in range(2):
        total_ref[z] = totals[z]


def complete(size_y, first, z, speed_ref, own_ref, target_ref, before_ref, source_ref, near_ref, sum_ref, list_ref):
    entries = []
    for column, x in enumerate((0, ahead("gx"), -ahead("gx"))):
        for plane, shifts in enumerate(y_shifts(size_y)):
            entries += [(source_ref, (column, plane), (x, y, 3 * z - 1)) for y in shifts]
    length = fill(near_ref, sum_ref, list_ref, entries)
    (total,) = sums_over([target_ref[z]], (before_ref[z],), near_ref, sum_ref, list_ref, length, len(entries), 7)
    total = total.T
    total = (total[0:8] + total[8:16] + total[16:24])[0:4]
    own = own_ref[z]
    accel = total - shifted(own, (0, 0, z)) * total[3:4]
    if first:
        rows = [jnp.where(z == 1, speed_ref[c, 0, 0, 1:2, :], speed_ref[c, 0, 0, 0:1, :]) for c in range(3)]
        speed = jnp.concatenate(rows + [jnp.zeros_like(rows[0])], axis=0)
    else:
        speed = speed_ref[z]
    speed = speed + time_step * accel
    place = jnp.clip(own + time_step * speed, 0.0, 1.0)
    return jnp.where(row_index(*own.shape) < 3, place, own), speed


def near_side():
    return (1 + ahead("gz")) // 2


def near_kernel(size_y, first, speed_ref, own_ref, target_ref, before_ref, source_ref, bin_ref, near_ref, sum_ref, list_ref):
    place, speed = complete(
        size_y, first, near_side(), speed_ref, own_ref, target_ref, before_ref, source_ref, near_ref, sum_ref, list_ref
    )
    bin_ref[0] = place
    bin_ref[1] = speed


def far_kernel(size_y, first, last, keep_ref, bin_ref, speed_ref, own_ref, target_ref, before_ref, source_ref, place_out, speed_out, near_ref, sum_ref, list_ref):
    other = near_side()
    z = 1 - other
    place, speed = complete(
        size_y, first, z, speed_ref, own_ref, target_ref, before_ref, source_ref, near_ref, sum_ref, list_ref
    )
    if not last:
        place_out[z] = place
        speed_out[z] = speed
        place_out[other] = bin_ref[0]
        speed_out[other] = bin_ref[1]
        return
    for side in range(2):
        keep = keep_ref[side, 0:1] > 0.0
        moved = jnp.where(z == side, place, bin_ref[0])
        kicked = jnp.where(z == side, speed, bin_ref[1])
        for c in range(3):
            place_out[c, 0, 0, side : side + 1, :] = jnp.where(keep, moved[c : c + 1], 0.0)
            speed_out[c, 0, 0, side : side + 1, :] = jnp.where(keep, kicked[c : c + 1], 0.0)


VMEM = pl.BlockSpec(memory_space=pltpu.VMEM)


def swaps(axis):
    size = lax.axis_size(axis)
    near = [(i, i ^ 1) for i in range(size)]
    far = [(i, (((i + 1) ^ 1) - 1) % size) for i in range(size)]
    return near, far


def call(kernel, inputs, outputs, sources, targets, slots, chunks):
    half = slots // 2
    heads = sources // 2 * 2
    return pl.pallas_call(
        kernel,
        out_shape=outputs,
        in_specs=[VMEM] * len(inputs),
        out_specs=tuple(VMEM for _ in outputs),
        scratch_shapes=[
            pltpu.VMEM((48, heads * half + chunks * slots), BF16),
            pltpu.VMEM((32, heads * half + chunks * slots), BF16),
            pltpu.VMEM((heads + 4, 8, half), F32),
        ],
        compiler_params=pltpu.CompilerParams(vmem_limit_bytes=24 * 1024 * 1024),
        cost_estimate=pl.CostEstimate(flops=sources * targets * slots * slots * 1000, bytes_accessed=1 << 18, transcendentals=0),
    )(*inputs)


def on_device(positions, velocities, mass, counts):
    slots = positions.shape[-1]
    size_y = lax.axis_size("gy")
    bins = jax.ShapeDtypeStruct((2, 4, slots), F32)
    full = jax.ShapeDtypeStruct(positions.shape, F32)
    running = jax.ShapeDtypeStruct((2, slots, 32), F32)
    packed, keep = pl.pallas_call(
        pack_kernel,
        out_shape=(bins, bins),
        in_specs=[VMEM] * 3,
        out_specs=(VMEM, VMEM),
    )(counts, positions, mass)
    speed = velocities
    upper = lax.rem(lax.axis_index("gz"), 2)
    for subcycle in range(SUBCYCLES):
        first, last = subcycle == 0, subcycle == SUBCYCLES - 1
        near, far = swaps("gy")
        planes = [packed]
        if size_y > 2:
            other = lax.ppermute(packed, "gy", far)
            planes += [lax.ppermute(packed, "gy", near), other]
        else:
            planes.append(lax.ppermute(packed, "gy", near))
        plane = jnp.stack(planes)
        near, far = swaps("gx")
        far_x = lax.ppermute(plane, "gx", far)
        near_x = lax.ppermute(plane, "gx", near)
        targets, total = call(
            functools.partial(plane_kernel, size_y),
            planes,
            (jax.ShapeDtypeStruct((2, slots, 48), BF16), running),
            6, 2, slots, 2,
        )
        slab = jnp.stack([plane, near_x, far_x])
        near, far = swaps("gz")
        far_z = lax.ppermute(lax.dynamic_index_in_dim(slab, upper, 2, False), "gz", far)
        near_z = lax.ppermute(lax.dynamic_index_in_dim(slab, 1 - upper, 2, False), "gz", near)
        (total,) = call(
            functools.partial(slab_kernel, size_y),
            [targets, total, near_x, far_x],
            (running,),
            12, 2, slots, 3,
        )
        state = [speed, packed, targets, total]
        (half_done,) = call(
            functools.partial(near_kernel, size_y, first),
            state + [near_z],
            (bins,),
            9, 1, slots, 3,
        )
        packed, speed = call(
            functools.partial(far_kernel, size_y, first, last),
            [keep, half_done] + state + [far_z],
            (full, full) if last else (bins, bins),
            9, 1, slots, 3,
        )
    return packed, speed


def solution(mesh):
    placed = (
        P(None, "gx", "gy", "gz", None),
        P(None, "gx", "gy", "gz", None),
        P("gx", "gy", "gz", None),
        P("gx", "gy", "gz"),
    )
    return jax.shard_map(
        on_device,
        mesh=mesh,
        in_specs=placed,
        out_specs=(P(None, "gx", "gy", "gz", None), P(None, "gx", "gy", "gz", None)),
        check_vma=False,
    )
```

profile of v0, /device:TPU:0, one launch (start us, length us, event | category | flops | bytes accessed | tf_op | source)
XLA Modules:
  0.0 35.3 jit_solution(14943751471646612534)
XLA Ops:
  0.6 1.4 %shard_map.59 = (f32[2,4,256]{2,1,0:T(4,128)}, f32[2,4,256]{2,1,0:T(4,128)}) custom-call(s32[1,1,2]{2,1,0:T(1,128)} %counts_ref.1, f32[3,1,1,2,256]{4,3,2,1,0:T(2,128)} %place_ref.1, f32[1,1,2,256]{3,2,1,0:T(2,128)} %mass_ref.1), custom_call_target="tpu_custom_call" | custom-call | tf_op jit(solution)/shard_map/pallas_call | solution.py:284
  2.0 3.0 %collective-permute-start = (f32[2,4,256]{2,1,0:T(4,128)}, f32[2,4,256]{2,1,0:T(4,128)S(1)}, u32[]{:S(2)}, u32[]{:S(2)}) collective-permute-start(f32[2,4,256]{2,1,0:T(4,128)} %get-tuple-element.11.refs_0_.own_ref), channel_id=1, source_target_pairs={{0,4},{4,0},{1,5},{5,1},{2,6},{6,2},{3,7},{7,3},{8,12},{12,8},{9,1... | collective-permute-start | bytes 24584 | tf_op jit(solution)/shard_map/ppermute | solution.py:300
  5.0 0.0 copy-start
  5.0 1.8 %collective-permute-done.refs_1_ = f32[2,4,256]{2,1,0:T(4,128)S(1)} collective-permute-done((f32[2,4,256]{2,1,0:T(4,128)}, f32[2,4,256]{2,1,0:T(4,128)S(1)}, u32[]{:S(2)}, u32[]{:S(2)}) %collective-permute-start) | collective-permute-done | bytes 8224 | tf_op jit(solution)/shard_map/ppermute | solution.py:300
  6.8 0.0 copy-done
  6.8 0.1 collective-permute-start.1
  6.9 2.1 %collective-permute-start.2 = (f32[2,2,4,256]{3,2,1,0:T(4,128)S(1)}, f32[2,2,4,256]{3,2,1,0:T(4,128)S(1)}, u32[]{:S(2)}, u32[]{:S(2)}) collective-permute-start(f32[2,2,4,256]{3,2,1,0:T(4,128)S(1)} %get-tuple-element.25), channel_id=1, source_target_pairs={{0,24},{8,16},{16,8},{24,0},{1,25},{9,17},{17,9},{25,1},{2,26},{10... | collective-permute-start | bytes 49160 | tf_op jit(solution)/shard_map/ppermute | solution.py:303
  9.0 1.4 %shard_map.60 = (bf16[2,256,48]{2,1,0:T(8,128)(2,1)S(1)}, f32[2,256,32]{2,1,0:T(8,128)S(1)}) custom-call(f32[2,4,256]{2,1,0:T(4,128)S(1)} %copy-done, f32[2,4,256]{2,1,0:T(4,128)S(1)} %collective-permute-done.refs_1_), custom_call_target="tpu_custom_call" | custom-call | flops 786432000 | bytes 262144 | tf_op jit(solution)/shard_map/pallas_call | solution.py:263
  10.4 0.0 collective-permute-done.1.near_x_ref
  10.4 0.1 collective-permute-done.2.far_x_ref
  10.5 1.8 %collective-permute-start.3 = (f32[3,2,4,256]{3,2,1,0:T(4,128)S(1)}, f32[3,2,4,256]{3,2,1,0:T(4,128)S(1)}, u32[]{:S(2)}, u32[]{:S(2)}) collective-permute-start(f32[3,2,4,256]{3,2,1,0:T(4,128)S(1)} %get-tuple-element.21), channel_id=1, source_target_pairs={{0,1},{1,0},{2,3},{3,2},{4,5},{5,4},{6,7},{7,6},{8,9},{9,8},{10,11... | collective-permute-start | bytes 73736 | tf_op jit(solution)/shard_map/ppermute | solution.py:314
  12.3 2.5 %collective-permute-start.4 = (f32[3,2,4,256]{3,2,1,0:T(4,128)S(1)}, f32[3,2,4,256]{3,2,1,0:T(4,128)S(1)}, u32[]{:S(2)}, u32[]{:S(2)}) collective-permute-start(f32[3,2,4,256]{3,2,1,0:T(4,128)S(1)} %get-tuple-element.20), channel_id=1, source_target_pairs={{0,3},{1,2},{2,1},{3,0},{4,7},{5,6},{6,5},{7,4},{8,11},{9,10},{10,... | collective-permute-start | bytes 73736 | tf_op jit(solution)/shard_map/ppermute | solution.py:313
  14.8 0.0 copy-start.2
  14.8 2.9 %shard_map.61.before_ref = f32[2,256,32]{2,1,0:T(8,128)S(1)} custom-call(bf16[2,256,48]{2,1,0:T(8,128)(2,1)S(1)} %get-tuple-element.12.target_ref, f32[2,256,32]{2,1,0:T(8,128)S(1)} %get-tuple-element.13.before_ref, f32[2,2,4,256]{3,2,1,0:T(4,128)S(1)} %collective-permute-done.1.near_x_ref, f32[2,2,4,256]{3,2,1,0:T(4,128)S(1)} %collective-permute-done.2.far_x_ref), custom_call_target="tpu_custom_call" | custom-call | flops 1572864000 | bytes 262144 | tf_op jit(solution)/shard_map/pallas_call | solution.py:263
  17.7 0.0 copy-start.1
  17.7 0.0 collective-permute-done.3.source_ref
  17.7 0.0 copy-done.2
  17.7 1.2 %shard_map.62.bin_ref = f32[2,4,256]{2,1,0:T(4,128)S(1)} custom-call(f32[3,1,1,2,256]{4,3,2,1,0:T(2,128)S(1)} %copy-done.2, f32[2,4,256]{2,1,0:T(4,128)S(1)} %copy-done, bf16[2,256,48]{2,1,0:T(8,128)(2,1)S(1)} %get-tuple-element.12.target_ref, f32[2,256,32]{2,1,0:T(8,128)S(1)} %shard_map.61.before_ref, f32[3,2,4,256]{3,2,1,0:T(4,128)S(1)} %collective-permute-done.3.source_ref), custom_call_target="tpu_custom_call" | custom-call | flops 589824000 | bytes 262144 | tf_op jit(solution)/shard_map/pallas_call | solution.py:263
  18.9 0.0 collective-permute-done.4.source_ref
  18.9 0.0 copy-done.1
  18.9 1.2 %shard_map.63 = (f32[2,4,256]{2,1,0:T(4,128)S(1)}, f32[2,4,256]{2,1,0:T(4,128)S(1)}) custom-call(f32[2,4,256]{2,1,0:T(4,128)S(1)} %copy-done.1, f32[2,4,256]{2,1,0:T(4,128)S(1)} %shard_map.62.bin_ref, f32[3,1,1,2,256]{4,3,2,1,0:T(2,128)S(1)} %copy-done.2, f32[2,4,256]{2,1,0:T(4,128)S(1)} %copy-done, bf16[2,256,48]{2,1,0:T(8,128)(2,1)S(1)} %get-tuple-element.12.target_ref, ...), custom_call_target="tpu_custom_call" | custom-call | flops 589824000 | bytes 262144 | tf_op jit(solution)/shard_map/pallas_call | solution.py:263
  20.1 1.6 %collective-permute-start.5 = (f32[2,4,256]{2,1,0:T(4,128)S(1)}, f32[2,4,256]{2,1,0:T(4,128)S(1)}, u32[]{:S(2)}, u32[]{:S(2)}) collective-permute-start(f32[2,4,256]{2,1,0:T(4,128)S(1)} %get-tuple-element.15.refs_0_.own_ref), channel_id=1, source_target_pairs={{0,4},{4,0},{1,5},{5,1},{2,6},{6,2},{3,7},{7,3},{8,12},{12,8},{9,1... | collective-permute-start | bytes 24584 | tf_op jit(solution)/shard_map/ppermute | solution.py:300
  21.7 2.1 %collective-permute-done.5.refs_1_ = f32[2,4,256]{2,1,0:T(4,128)S(1)} collective-permute-done((f32[2,4,256]{2,1,0:T(4,128)S(1)}, f32[2,4,256]{2,1,0:T(4,128)S(1)}, u32[]{:S(2)}, u32[]{:S(2)}) %collective-permute-start.5) | collective-permute-done | bytes 8224 | tf_op jit(solution)/shard_map/ppermute | solution.py:300
  23.8 0.1 collective-permute-start.6
  23.9 1.6 %collective-permute-start.7 = (f32[2,2,4,256]{3,2,1,0:T(4,128)S(1)}, f32[2,2,4,256]{3,2,1,0:T(4,128)S(1)}, u32[]{:S(2)}, u32[]{:S(2)}) collective-permute-start(f32[2,2,4,256]{3,2,1,0:T(4,128)S(1)} %get-tuple-element.23), channel_id=1, source_target_pairs={{0,24},{8,16},{16,8},{24,0},{1,25},{9,17},{17,9},{25,1},{2,26},{10... | collective-permute-start | bytes 49160 | tf_op jit(solution)/shard_map/ppermute | solution.py:303
  25.5 1.4 %shard_map.64 = (bf16[2,256,48]{2,1,0:T(8,128)(2,1)S(1)}, f32[2,256,32]{2,1,0:T(8,128)S(1)}) custom-call(f32[2,4,256]{2,1,0:T(4,128)S(1)} %get-tuple-element.15.refs_0_.own_ref, f32[2,4,256]{2,1,0:T(4,128)S(1)} %collective-permute-done.5.refs_1_), custom_call_target="tpu_custom_call" | custom-call | flops 786432000 | bytes 262144 | tf_op jit(solution)/shard_map/pallas_call | solution.py:263
  26.9 0.0 collective-permute-done.6.near_x_ref
  26.9 0.2 collective-permute-done.7.far_x_ref
  27.1 0.7 %collective-permute-start.8 = (f32[3,2,4,256]{3,2,1,0:T(4,128)S(1)}, f32[3,2,4,256]{3,2,1,0:T(4,128)S(1)}, u32[]{:S(2)}, u32[]{:S(2)}) collective-permute-start(f32[3,2,4,256]{3,2,1,0:T(4,128)S(1)} %get-tuple-element.19), channel_id=1, source_target_pairs={{0,1},{1,0},{2,3},{3,2},{4,5},{5,4},{6,7},{7,6},{8,9},{9,8},{10,11... | collective-permute-start | bytes 73736 | tf_op jit(solution)/shard_map/ppermute | solution.py:314
  27.9 0.9 %collective-permute-start.9 = (f32[3,2,4,256]{3,2,1,0:T(4,128)S(1)}, f32[3,2,4,256]{3,2,1,0:T(4,128)S(1)}, u32[]{:S(2)}, u32[]{:S(2)}) collective-permute-start(f32[3,2,4,256]{3,2,1,0:T(4,128)S(1)} %get-tuple-element.18), channel_id=1, source_target_pairs={{0,3},{1,2},{2,1},{3,0},{4,7},{5,6},{6,5},{7,4},{8,11},{9,10},{10,... | collective-permute-start | bytes 73736 | tf_op jit(solution)/shard_map/ppermute | solution.py:313
  28.8 2.9 %shard_map.65.before_ref = f32[2,256,32]{2,1,0:T(8,128)S(1)} custom-call(bf16[2,256,48]{2,1,0:T(8,128)(2,1)S(1)} %get-tuple-element.16.target_ref, f32[2,256,32]{2,1,0:T(8,128)S(1)} %get-tuple-element.17.before_ref, f32[2,2,4,256]{3,2,1,0:T(4,128)S(1)} %collective-permute-done.6.near_x_ref, f32[2,2,4,256]{3,2,1,0:T(4,128)S(1)} %collective-permute-done.7.far_x_ref), custom_call_target="tpu_custom_call" | custom-call | flops 1572864000 | bytes 262144 | tf_op jit(solution)/shard_map/pallas_call | solution.py:263
  31.7 0.0 collective-permute-done.8.source_ref
  31.7 1.2 %shard_map.66.bin_ref = f32[2,4,256]{2,1,0:T(4,128)S(1)} custom-call(f32[2,4,256]{2,1,0:T(4,128)S(1)} %get-tuple-element.14.speed_ref, f32[2,4,256]{2,1,0:T(4,128)S(1)} %get-tuple-element.15.refs_0_.own_ref, bf16[2,256,48]{2,1,0:T(8,128)(2,1)S(1)} %get-tuple-element.16.target_ref, f32[2,256,32]{2,1,0:T(8,128)S(1)} %shard_map.65.before_ref, ...), custom_call_target="tpu_custom_call" | custom-call | flops 589824000 | bytes 262144 | tf_op jit(solution)/shard_map/pallas_call | solution.py:263
  32.9 0.6 %collective-permute-done.9.source_ref = f32[3,2,4,256]{3,2,1,0:T(4,128)S(1)} collective-permute-done((f32[3,2,4,256]{3,2,1,0:T(4,128)S(1)}, f32[3,2,4,256]{3,2,1,0:T(4,128)S(1)}, u32[]{:S(2)}, u32[]{:S(2)}) %collective-permute-start.9) | collective-permute-done | bytes 24608 | tf_op jit(solution)/shard_map/ppermute | solution.py:313
  33.5 1.8 %shard_map.67 = (f32[3,1,1,2,256]{4,3,2,1,0:T(2,128)}, f32[3,1,1,2,256]{4,3,2,1,0:T(2,128)}) custom-call(f32[2,4,256]{2,1,0:T(4,128)S(1)} %copy-done.1, f32[2,4,256]{2,1,0:T(4,128)S(1)} %shard_map.66.bin_ref, f32[2,4,256]{2,1,0:T(4,128)S(1)} %get-tuple-element.14.speed_ref, f32[2,4,256]{2,1,0:T(4,128)S(1)} %get-tuple-element.15.refs_0_.own_ref, ...), custom_call_target="tpu_custom_call" | custom-call | flops 589824000 | bytes 262144 | tf_op jit(solution)/shard_map/pallas_call | solution.py:263
  (6 shorter events, 0.1 us)
Async XLA Ops:
  2.0 4.8 %collective-permute-start = (f32[2,4,256]{2,1,0:T(4,128)}, f32[2,4,256]{2,1,0:T(4,128)S(1)}, u32[]{:S(2)}, u32[]{:S(2)}) collective-permute-start(f32[2,4,256]{2,1,0:T(4,128)} %get-tuple-element.11.refs_0_.own_ref), channel_id=1, source_target_pairs={{0,4},{4,0},{1,5},{5,1},{2,6},{6,2},{3,7},{7,3},{8,12},{12,8},{9,1... | collective-permute-start | bytes 24584 | tf_op jit(solution)/shard_map/ppermute | solution.py:300
  5.0 1.8 %copy-start = (f32[2,4,256]{2,1,0:T(4,128)S(1)}, f32[2,4,256]{2,1,0:T(4,128)}, u32[]{:S(2)}) copy-start(f32[2,4,256]{2,1,0:T(4,128)} %get-tuple-element.11.refs_0_.own_ref) | copy-start | bytes 24580
  6.8 3.6 %collective-permute-start.1 = (f32[2,2,4,256]{3,2,1,0:T(4,128)S(1)}, f32[2,2,4,256]{3,2,1,0:T(4,128)S(1)}, u32[]{:S(2)}, u32[]{:S(2)}) collective-permute-start(f32[2,2,4,256]{3,2,1,0:T(4,128)S(1)} %get-tuple-element.25), channel_id=1, source_target_pairs={{0,8},{8,0},{16,24},{24,16},{1,9},{9,1},{17,25},{25,17},{2,10},{10... | collective-permute-start | bytes 49160 | tf_op jit(solution)/shard_map/ppermute | solution.py:304
  6.9 3.6 %collective-permute-start.2 = (f32[2,2,4,256]{3,2,1,0:T(4,128)S(1)}, f32[2,2,4,256]{3,2,1,0:T(4,128)S(1)}, u32[]{:S(2)}, u32[]{:S(2)}) collective-permute-start(f32[2,2,4,256]{3,2,1,0:T(4,128)S(1)} %get-tuple-element.25), channel_id=1, source_target_pairs={{0,24},{8,16},{16,8},{24,0},{1,25},{9,17},{17,9},{25,1},{2,26},{10... | collective-permute-start | bytes 49160 | tf_op jit(solution)/shard_map/ppermute | solution.py:303
  10.5 7.2 %collective-permute-start.3 = (f32[3,2,4,256]{3,2,1,0:T(4,128)S(1)}, f32[3,2,4,256]{3,2,1,0:T(4,128)S(1)}, u32[]{:S(2)}, u32[]{:S(2)}) collective-permute-start(f32[3,2,4,256]{3,2,1,0:T(4,128)S(1)} %get-tuple-element.21), channel_id=1, source_target_pairs={{0,1},{1,0},{2,3},{3,2},{4,5},{5,4},{6,7},{7,6},{8,9},{9,8},{10,11... | collective-permute-start | bytes 73736 | tf_op jit(solution)/shard_map/ppermute | solution.py:314
  12.3 6.5 %collective-permute-start.4 = (f32[3,2,4,256]{3,2,1,0:T(4,128)S(1)}, f32[3,2,4,256]{3,2,1,0:T(4,128)S(1)}, u32[]{:S(2)}, u32[]{:S(2)}) collective-permute-start(f32[3,2,4,256]{3,2,1,0:T(4,128)S(1)} %get-tuple-element.20), channel_id=1, source_target_pairs={{0,3},{1,2},{2,1},{3,0},{4,7},{5,6},{6,5},{7,4},{8,11},{9,10},{10,... | collective-permute-start | bytes 73736 | tf_op jit(solution)/shard_map/ppermute | solution.py:313
  14.8 2.9 %copy-start.2 = (f32[3,1,1,2,256]{4,3,2,1,0:T(2,128)S(1)}, f32[3,1,1,2,256]{4,3,2,1,0:T(2,128)}, u32[]{:S(2)}) copy-start(f32[3,1,1,2,256]{4,3,2,1,0:T(2,128)} %speed_ref.3) | copy-start | bytes 18436
  17.7 1.2 %copy-start.1 = (f32[2,4,256]{2,1,0:T(4,128)S(1)}, f32[2,4,256]{2,1,0:T(4,128)}, u32[]{:S(2)}) copy-start(f32[2,4,256]{2,1,0:T(4,128)} %get-tuple-element.10.keep_ref) | copy-start | bytes 24580
  20.1 3.7 %collective-permute-start.5 = (f32[2,4,256]{2,1,0:T(4,128)S(1)}, f32[2,4,256]{2,1,0:T(4,128)S(1)}, u32[]{:S(2)}, u32[]{:S(2)}) collective-permute-start(f32[2,4,256]{2,1,0:T(4,128)S(1)} %get-tuple-element.15.refs_0_.own_ref), channel_id=1, source_target_pairs={{0,4},{4,0},{1,5},{5,1},{2,6},{6,2},{3,7},{7,3},{8,12},{12,8},{9,1... | collective-permute-start | bytes 24584 | tf_op jit(solution)/shard_map/ppermute | solution.py:300
  23.8 3.1 %collective-permute-start.6 = (f32[2,2,4,256]{3,2,1,0:T(4,128)S(1)}, f32[2,2,4,256]{3,2,1,0:T(4,128)S(1)}, u32[]{:S(2)}, u32[]{:S(2)}) collective-permute-start(f32[2,2,4,256]{3,2,1,0:T(4,128)S(1)} %get-tuple-element.23), channel_id=1, source_target_pairs={{0,8},{8,0},{16,24},{24,16},{1,9},{9,1},{17,25},{25,17},{2,10},{10... | collective-permute-start | bytes 49160 | tf_op jit(solution)/shard_map/ppermute | solution.py:304
  23.9 3.2 %collective-permute-start.7 = (f32[2,2,4,256]{3,2,1,0:T(4,128)S(1)}, f32[2,2,4,256]{3,2,1,0:T(4,128)S(1)}, u32[]{:S(2)}, u32[]{:S(2)}) collective-permute-start(f32[2,2,4,256]{3,2,1,0:T(4,128)S(1)} %get-tuple-element.23), channel_id=1, source_target_pairs={{0,24},{8,16},{16,8},{24,0},{1,25},{9,17},{17,9},{25,1},{2,26},{10... | collective-permute-start | bytes 49160 | tf_op jit(solution)/shard_map/ppermute | solution.py:303
  27.1 4.6 %collective-permute-start.8 = (f32[3,2,4,256]{3,2,1,0:T(4,128)S(1)}, f32[3,2,4,256]{3,2,1,0:T(4,128)S(1)}, u32[]{:S(2)}, u32[]{:S(2)}) collective-permute-start(f32[3,2,4,256]{3,2,1,0:T(4,128)S(1)} %get-tuple-element.19), channel_id=1, source_target_pairs={{0,1},{1,0},{2,3},{3,2},{4,5},{5,4},{6,7},{7,6},{8,9},{9,8},{10,11... | collective-permute-start | bytes 73736 | tf_op jit(solution)/shard_map/ppermute | solution.py:314
  27.9 5.6 %collective-permute-start.9 = (f32[3,2,4,256]{3,2,1,0:T(4,128)S(1)}, f32[3,2,4,256]{3,2,1,0:T(4,128)S(1)}, u32[]{:S(2)}, u32[]{:S(2)}) collective-permute-start(f32[3,2,4,256]{3,2,1,0:T(4,128)S(1)} %get-tuple-element.18), channel_id=1, source_target_pairs={{0,3},{1,2},{2,1},{3,0},{4,7},{5,6},{6,5},{7,4},{8,11},{9,10},{10,... | collective-permute-start | bytes 73736 | tf_op jit(solution)/shard_map/ppermute | solution.py:313
where the time goes:
time: 35.5 us; the launch traced here: 35.3 us
  Pallas kernels  15.1 us (43%)
  starting transfers between devices  14.4 us (41%)
  waiting for transfers between devices  4.89 us (14%)
  between operations  0.8 us (2%)
    pallas_call x8, Pallas kernels, call(): pl.pallas_call(kernel, out_shape=outputs, in_specs=[VMEM] * len(inputs),...  13.7 us
    ppermute x2, starting transfers between devices, on_device(): planes.append(lax.ppermute(packed, 'gy', near))  4.55 us
    ppermute x2, waiting for transfers between devices, on_device(): planes.append(lax.ppermute(packed, 'gy', near))  3.97 us
    ppermute x2, starting transfers between devices, on_device(): far_x = lax.ppermute(plane, 'gx', far)  3.72 us
    ppermute x2, starting transfers between devices, on_device(): lax.ppermute(lax.dynamic_index_in_dim(slab, upper, 2, False), 'gz', far)  3.41 us
    ppermute x2, starting transfers between devices, on_device(): lax.ppermute(lax.dynamic_index_in_dim(slab, 1 - upper, 2, False), 'gz', n...  2.56 us
    pallas_call x1, Pallas kernels, on_device(): pl.pallas_call(pack_kernel, out_shape=(bins, bins), in_specs=[VMEM] * 3,...  1.39 us
  transfers between devices with their start and end apart: 10, of which 4 were waited for; matrix products, arithmetic and copies ran while one was open for 0% of the time, Pallas kernels for 31%

commit v1 on v0

--- a/solution.py
+++ b/solution.py
@@ -81,10 +81,11 @@
     return 1 - 2 * lax.rem(lax.axis_index(axis), 2)
 
 
-def y_shifts(size):
+def y_sources(size):
     if size == 2:
-        return [[0], [-1, 1]]
-    return [[0], [ahead("gy")], [-ahead("gy")]]
+        here = lax.axis_index("gy")
+        return [(here, 0, 0), (1 - here, -1, 1), (1 - here, 1, 1)]
+    return [(0, 0, 0), (1, ahead("gy"), 1), (2, -ahead("gy"), 2)]
 
 
 def list_chunk(list_ref, chunk):
@@ -97,7 +98,7 @@
     list_ref[...] = jnp.zeros_like(list_ref)
     place = jnp.int32(0)
     held = {}
-    for number, (ref, index, offset) in enumerate(entries):
+    for number, (ref, index, offset, _) in enumerate(entries):
         packed = ref[index]
         head, tail = shifted(packed[:, :half], offset), shifted(packed[:, half:], offset)
         if number == len(entries) - 1 and number % 2 == 0:
@@ -110,9 +111,8 @@
     if len(entries) % 2:
         place = place + half
     known = {}
-    for number, (ref, index, offset) in enumerate(entries):
+    for number, (_, _, _, key) in enumerate(entries):
         tail = held[number]
-        key = (id(ref),) + (index if isinstance(index, tuple) else (index,))
         if key not in known:
             present = jnp.where(tail[3:4] != 0.0, lane[0:1] + 1, 0).astype(F32)
             known[key] = jnp.max(present).astype(jnp.int32)
@@ -163,15 +163,12 @@
     return lax.fori_loop(done, jnp.maximum(lax.div(length + (wide - 1), wide), done), rest, tuple(totals))
 
 
-def plane_kernel(size_y, *refs):
-    planes, (target_ref, total_ref, near_ref, sum_ref, list_ref) = refs[:-5], refs[-5:]
-    own_ref = planes[0]
+def plane_kernel(size_y, own_ref, plane_ref, target_ref, total_ref, near_ref, sum_ref, list_ref):
     for z in range(2):
         target_ref[z] = target_rows(shifted(own_ref[z], (0, 0, z)))
     entries = []
-    for ref, shifts in zip(planes, y_shifts(size_y)):
-        for y in shifts:
-            entries += [(ref, z, (0, y, z)) for z in range(2)]
+    for plane, y, number in y_sources(size_y):
+        entries += [(plane_ref, (plane, z), (0, y, z), (number, z)) for z in range(2)]
     length = fill(near_ref, sum_ref, list_ref, entries)
     zero = jnp.zeros(total_ref.shape[1:], F32)
     targets = [target_ref[z] for z in range(2)]
@@ -182,10 +179,9 @@
 
 def slab_kernel(size_y, target_ref, before_ref, near_x_ref, far_x_ref, total_ref, near_ref, sum_ref, list_ref):
     entries = []
-    for ref, x in ((near_x_ref, ahead("gx")), (far_x_ref, -ahead("gx"))):
-        for plane, shifts in enumerate(y_shifts(size_y)):
-            for y in shifts:
-                entries += [(ref, (plane, z), (x, y, z)) for z in range(2)]
+    for side, (ref, x) in enumerate(((near_x_ref, ahead("gx")), (far_x_ref, -ahead("gx")))):
+        for plane, y, number in y_sources(size_y):
+            entries += [(ref, (plane, z), (x, y, z), (side, number, z)) for z in range(2)]
     length = fill(near_ref, sum_ref, list_ref, entries)
     targets = [target_ref[z] for z in range(2)]
     totals = sums_over(targets, (before_ref[0], before_ref[1]), near_ref, sum_ref, list_ref, length, len(entries), 3)
@@ -196,8 +192,8 @@
 def complete(size_y, first, z, speed_ref, own_ref, target_ref, before_ref, source_ref, near_ref, sum_ref, list_ref):
     entries = []
     for column, x in enumerate((0, ahead("gx"), -ahead("gx"))):
-        for plane, shifts in enumerate(y_shifts(size_y)):
-            entries += [(source_ref, (column, plane), (x, y, 3 * z - 1)) for y in shifts]
+        for plane, y, number in y_sources(size_y):
+            entries.append((source_ref, (column, plane), (x, y, 3 * z - 1), (column, number)))
     length = fill(near_ref, sum_ref, list_ref, entries)
     (total,) = sums_over([target_ref[z]], (before_ref[z],), near_ref, sum_ref, list_ref, length, len(entries), 7)
     total = total.T
@@ -291,20 +287,20 @@
     upper = lax.rem(lax.axis_index("gz"), 2)
     for subcycle in range(SUBCYCLES):
         first, last = subcycle == 0, subcycle == SUBCYCLES - 1
-        near, far = swaps("gy")
-        planes = [packed]
         if size_y > 2:
+            near, far = swaps("gy")
             other = lax.ppermute(packed, "gy", far)
-            planes += [lax.ppermute(packed, "gy", near), other]
+            plane = jnp.stack([packed, lax.ppermute(packed, "gy", near), other])
+        elif first:
+            plane = lax.all_gather(packed, "gy")
         else:
-            planes.append(lax.ppermute(packed, "gy", near))
-        plane = jnp.stack(planes)
+            plane = lax.all_to_all(jnp.broadcast_to(packed[None], (2,) + packed.shape), "gy", 0, 0)
         near, far = swaps("gx")
         far_x = lax.ppermute(plane, "gx", far)
         near_x = lax.ppermute(plane, "gx", near)
         targets, total = call(
             functools.partial(plane_kernel, size_y),
-            planes,
+            [packed, plane],
             (jax.ShapeDtypeStruct((2, slots, 48), BF16), running),
             6, 2, slots, 2,
         )

time: 35.5 us -> 39 us (1.099)
  blocking collectives: 0 us -> 12.1 us
  starting transfers between devices: 14.4 us -> 9.65 us
  waiting for transfers between devices: 4.89 us -> 0.88 us
    all_to_all x0 -> x1, blocking collectives: none -> 6.44 us  [on_device(): lax.all_to_all(jnp.broadcast_to(packed[None], (2,) + packed.shape), 'gy',...]
    all_gather x0 -> x1, blocking collectives: none -> 5.68 us  [on_device(): plane = lax.all_gather(packed, 'gy')]
    ppermute x2 -> x0, starting transfers between devices: 4.55 us -> none  [on_device(): planes.append(lax.ppermute(packed, 'gy', near))]
    ppermute x2 -> x0, waiting for transfers between devices: 3.97 us -> none  [on_device(): planes.append(lax.ppermute(packed, 'gy', near))]
  transfers between devices with their start and end apart: 10 -> 8, of which waited for: 4 -> 2; matrix products, arithmetic and copies ran while one was open for 0% -> 0% of each run, Pallas kernels for 31% -> 28%
where the time goes in v1:
time: 39 us; the launch traced here: 38.6 us
  Pallas kernels  15.1 us (39%)
  blocking collectives  12.1 us (31%)
  starting transfers between devices  9.65 us (25%)
  waiting for transfers between devices  0.88 us (2%)
  between operations  0.8 us (2%)
    pallas_call x8, Pallas kernels, call(): pl.pallas_call(kernel, out_shape=outputs, in_specs=[VMEM] * len(inputs),...  13.7 us
    all_to_all x1, blocking collectives, on_device(): lax.all_to_all(jnp.broadcast_to(packed[None], (2,) + packed.shape), 'gy',...  6.44 us
    all_gather x1, blocking collectives, on_device(): plane = lax.all_gather(packed, 'gy')  5.68 us
    ppermute x2, starting transfers between devices, on_device(): far_x = lax.ppermute(plane, 'gx', far)  3.68 us
    ppermute x2, starting transfers between devices, on_device(): lax.ppermute(lax.dynamic_index_in_dim(slab, upper, 2, False), 'gz', far)  3.39 us
    ppermute x2, starting transfers between devices, on_device(): lax.ppermute(lax.dynamic_index_in_dim(slab, 1 - upper, 2, False), 'gz', n...  2.57 us
    pallas_call x1, Pallas kernels, on_device(): pl.pallas_call(pack_kernel, out_shape=(bins, bins), in_specs=[VMEM] * 3,...  1.39 us
  transfers between devices with their start and end apart: 8, of which 2 were waited for; matrix products, arithmetic and copies ran while one was open for 0% of the time, Pallas kernels for 28%

profile of v1, /device:TPU:0, one launch (start us, length us, event | category | flops | bytes accessed | tf_op | source)
XLA Modules:
  0.0 38.6 jit_solution(1170125880639767883)
XLA Ops:
  0.6 1.4 %shard_map.59 = (f32[2,4,256]{2,1,0:T(4,128)}, f32[2,4,256]{2,1,0:T(4,128)}) custom-call(s32[1,1,2]{2,1,0:T(1,128)} %counts_ref.1, f32[3,1,1,2,256]{4,3,2,1,0:T(2,128)} %place_ref.1, f32[1,1,2,256]{3,2,1,0:T(2,128)} %mass_ref.1), custom_call_target="tpu_custom_call" | custom-call | tf_op jit(solution)/shard_map/pallas_call | solution.py:280
  2.0 0.0 copy-start
  2.0 5.7 %all-gather = f32[4,4,256]{2,1,0:T(4,128)S(1)} all-gather(f32[2,4,256]{2,1,0:T(4,128)} %get-tuple-element.11.own_ref), channel_id=2, replica_groups=mesh['gx'=4,'gy'=2,'gz'=4] {'gy'}, dimensions={0}, use_global_device_ids=true | all-gather | bytes 24576 | tf_op jit(solution)/shard_map/all_gather | solution.py:295
  7.7 0.0 collective-permute-start
  7.7 2.1 %collective-permute-start.1 = (f32[2,2,4,256]{3,2,1,0:T(4,128)S(1)}, f32[2,2,4,256]{3,2,1,0:T(4,128)S(1)}, u32[]{:S(2)}, u32[]{:S(2)}) collective-permute-start(f32[2,2,4,256]{3,2,1,0:T(4,128)S(1)} %bitcast.16), channel_id=1, source_target_pairs={{0,24},{8,16},{16,8},{24,0},{1,25},{9,17},{17,9},{25,1},{2,26},{10... | collective-permute-start | bytes 49160 | tf_op jit(solution)/shard_map/ppermute | solution.py:299
  9.8 0.0 copy-done
  9.8 1.4 %shard_map.60 = (bf16[2,256,48]{2,1,0:T(8,128)(2,1)S(1)}, f32[2,256,32]{2,1,0:T(8,128)S(1)}) custom-call(f32[2,4,256]{2,1,0:T(4,128)S(1)} %copy-done, f32[2,2,4,256]{3,2,1,0:T(4,128)S(1)} %bitcast.17), custom_call_target="tpu_custom_call" | custom-call | flops 786432000 | bytes 262144 | tf_op jit(solution)/shard_map/pallas_call | solution.py:259
  11.2 0.0 collective-permute-done.near_x_ref
  11.2 0.0 collective-permute-done.1.far_x_ref
  11.3 1.8 %collective-permute-start.2 = (f32[3,2,4,256]{3,2,1,0:T(4,128)S(1)}, f32[3,2,4,256]{3,2,1,0:T(4,128)S(1)}, u32[]{:S(2)}, u32[]{:S(2)}) collective-permute-start(f32[3,2,4,256]{3,2,1,0:T(4,128)S(1)} %get-tuple-element.21), channel_id=1, source_target_pairs={{0,1},{1,0},{2,3},{3,2},{4,5},{5,4},{6,7},{7,6},{8,9},{9,8},{10,11... | collective-permute-start | bytes 73736 | tf_op jit(solution)/shard_map/ppermute | solution.py:310
  13.1 2.5 %collective-permute-start.3 = (f32[3,2,4,256]{3,2,1,0:T(4,128)S(1)}, f32[3,2,4,256]{3,2,1,0:T(4,128)S(1)}, u32[]{:S(2)}, u32[]{:S(2)}) collective-permute-start(f32[3,2,4,256]{3,2,1,0:T(4,128)S(1)} %get-tuple-element.20), channel_id=1, source_target_pairs={{0,3},{1,2},{2,1},{3,0},{4,7},{5,6},{6,5},{7,4},{8,11},{9,10},{10,... | collective-permute-start | bytes 73736 | tf_op jit(solution)/shard_map/ppermute | solution.py:309
  15.6 0.0 copy-start.2
  15.6 2.9 %shard_map.61.before_ref = f32[2,256,32]{2,1,0:T(8,128)S(1)} custom-call(bf16[2,256,48]{2,1,0:T(8,128)(2,1)S(1)} %get-tuple-element.12.target_ref, f32[2,256,32]{2,1,0:T(8,128)S(1)} %get-tuple-element.13.before_ref, f32[2,2,4,256]{3,2,1,0:T(4,128)S(1)} %collective-permute-done.near_x_ref, f32[2,2,4,256]{3,2,1,0:T(4,128)S(1)} %collective-permute-done.1.far_x_ref), custom_call_target="tpu_custom_call" | custom-call | flops 1572864000 | bytes 262144 | tf_op jit(solution)/shard_map/pallas_call | solution.py:259
  18.4 0.0 copy-start.1
  18.5 0.0 collective-permute-done.2.source_ref
  18.5 0.0 copy-done.2
  18.5 1.2 %shard_map.62.bin_ref = f32[2,4,256]{2,1,0:T(4,128)S(1)} custom-call(f32[3,1,1,2,256]{4,3,2,1,0:T(2,128)S(1)} %copy-done.2, f32[2,4,256]{2,1,0:T(4,128)S(1)} %copy-done, bf16[2,256,48]{2,1,0:T(8,128)(2,1)S(1)} %get-tuple-element.12.target_ref, f32[2,256,32]{2,1,0:T(8,128)S(1)} %shard_map.61.before_ref, f32[3,2,4,256]{3,2,1,0:T(4,128)S(1)} %collective-permute-done.2.source_ref), custom_call_target="tpu_custom_call" | custom-call | flops 589824000 | bytes 262144 | tf_op jit(solution)/shard_map/pallas_call | solution.py:259
  19.6 0.0 collective-permute-done.3.source_ref
  19.7 0.0 copy-done.1
  19.7 1.2 %shard_map.63 = (f32[2,4,256]{2,1,0:T(4,128)S(1)}, f32[2,4,256]{2,1,0:T(4,128)S(1)}) custom-call(f32[2,4,256]{2,1,0:T(4,128)S(1)} %copy-done.1, f32[2,4,256]{2,1,0:T(4,128)S(1)} %shard_map.62.bin_ref, f32[3,1,1,2,256]{4,3,2,1,0:T(2,128)S(1)} %copy-done.2, f32[2,4,256]{2,1,0:T(4,128)S(1)} %copy-done, bf16[2,256,48]{2,1,0:T(8,128)(2,1)S(1)} %get-tuple-element.12.target_ref, ...), custom_call_target="tpu_custom_call" | custom-call | flops 589824000 | bytes 262144 | tf_op jit(solution)/shard_map/pallas_call | solution.py:259
  20.9 6.4 %all_to_all.5.plane_ref = f32[2,2,4,256]{3,2,1,0:T(4,128)S(1)} all-to-all(f32[2,2,4,256]{3,2,1,0:T(4,128)S(1)} %broadcast_in_dim.2), channel_id=1, replica_groups=mesh['gx'=4,'gy'=2,'gz'=4] {'gy'}, dimensions={0} | all-to-all | bytes 32768 | tf_op jit(solution)/shard_map/all_to_all | solution.py:297
  27.3 0.0 collective-permute-start.4
  27.3 1.6 %collective-permute-start.5 = (f32[2,2,4,256]{3,2,1,0:T(4,128)S(1)}, f32[2,2,4,256]{3,2,1,0:T(4,128)S(1)}, u32[]{:S(2)}, u32[]{:S(2)}) collective-permute-start(f32[2,2,4,256]{3,2,1,0:T(4,128)S(1)} %all_to_all.5.plane_ref), channel_id=1, source_target_pairs={{0,24},{8,16},{16,8},{24,0},{1,25},{9,17},{17,9},{25,1},{2,26},{10... | collective-permute-start | bytes 49160 | tf_op jit(solution)/shard_map/ppermute | solution.py:299
  28.9 1.4 %shard_map.64 = (bf16[2,256,48]{2,1,0:T(8,128)(2,1)S(1)}, f32[2,256,32]{2,1,0:T(8,128)S(1)}) custom-call(f32[2,4,256]{2,1,0:T(4,128)S(1)} %get-tuple-element.15.own_ref, f32[2,2,4,256]{3,2,1,0:T(4,128)S(1)} %all_to_all.5.plane_ref), custom_call_target="tpu_custom_call" | custom-call | flops 786432000 | bytes 262144 | tf_op jit(solution)/shard_map/pallas_call | solution.py:259
  30.3 0.0 collective-permute-done.4.near_x_ref
  30.3 0.2 collective-permute-done.5.far_x_ref
  30.5 0.8 %collective-permute-start.6 = (f32[3,2,4,256]{3,2,1,0:T(4,128)S(1)}, f32[3,2,4,256]{3,2,1,0:T(4,128)S(1)}, u32[]{:S(2)}, u32[]{:S(2)}) collective-permute-start(f32[3,2,4,256]{3,2,1,0:T(4,128)S(1)} %get-tuple-element.19), channel_id=1, source_target_pairs={{0,1},{1,0},{2,3},{3,2},{4,5},{5,4},{6,7},{7,6},{8,9},{9,8},{10,11... | collective-permute-start | bytes 73736 | tf_op jit(solution)/shard_map/ppermute | solution.py:310
  31.3 0.9 %collective-permute-start.7 = (f32[3,2,4,256]{3,2,1,0:T(4,128)S(1)}, f32[3,2,4,256]{3,2,1,0:T(4,128)S(1)}, u32[]{:S(2)}, u32[]{:S(2)}) collective-permute-start(f32[3,2,4,256]{3,2,1,0:T(4,128)S(1)} %get-tuple-element.18), channel_id=1, source_target_pairs={{0,3},{1,2},{2,1},{3,0},{4,7},{5,6},{6,5},{7,4},{8,11},{9,10},{10,... | collective-permute-start | bytes 73736 | tf_op jit(solution)/shard_map/ppermute | solution.py:309
  32.2 2.9 %shard_map.65.before_ref = f32[2,256,32]{2,1,0:T(8,128)S(1)} custom-call(bf16[2,256,48]{2,1,0:T(8,128)(2,1)S(1)} %get-tuple-element.16.target_ref, f32[2,256,32]{2,1,0:T(8,128)S(1)} %get-tuple-element.17.before_ref, f32[2,2,4,256]{3,2,1,0:T(4,128)S(1)} %collective-permute-done.4.near_x_ref, f32[2,2,4,256]{3,2,1,0:T(4,128)S(1)} %collective-permute-done.5.far_x_ref), custom_call_target="tpu_custom_call" | custom-call | flops 1572864000 | bytes 262144 | tf_op jit(solution)/shard_map/pallas_call | solution.py:259
  35.0 0.0 collective-permute-done.6.source_ref
  35.1 1.2 %shard_map.66.bin_ref = f32[2,4,256]{2,1,0:T(4,128)S(1)} custom-call(f32[2,4,256]{2,1,0:T(4,128)S(1)} %get-tuple-element.14.speed_ref, f32[2,4,256]{2,1,0:T(4,128)S(1)} %get-tuple-element.15.own_ref, bf16[2,256,48]{2,1,0:T(8,128)(2,1)S(1)} %get-tuple-element.16.target_ref, f32[2,256,32]{2,1,0:T(8,128)S(1)} %shard_map.65.before_ref, ...), custom_call_target="tpu_custom_call" | custom-call | flops 589824000 | bytes 262144 | tf_op jit(solution)/shard_map/pallas_call | solution.py:259
  36.2 0.7 %collective-permute-done.7.source_ref = f32[3,2,4,256]{3,2,1,0:T(4,128)S(1)} collective-permute-done((f32[3,2,4,256]{3,2,1,0:T(4,128)S(1)}, f32[3,2,4,256]{3,2,1,0:T(4,128)S(1)}, u32[]{:S(2)}, u32[]{:S(2)}) %collective-permute-start.7) | collective-permute-done | bytes 24608 | tf_op jit(solution)/shard_map/ppermute | solution.py:309
  36.9 1.7 %shard_map.67 = (f32[3,1,1,2,256]{4,3,2,1,0:T(2,128)}, f32[3,1,1,2,256]{4,3,2,1,0:T(2,128)}) custom-call(f32[2,4,256]{2,1,0:T(4,128)S(1)} %copy-done.1, f32[2,4,256]{2,1,0:T(4,128)S(1)} %shard_map.66.bin_ref, f32[2,4,256]{2,1,0:T(4,128)S(1)} %get-tuple-element.14.speed_ref, f32[2,4,256]{2,1,0:T(4,128)S(1)} %get-tuple-element.15.own_ref, ...), custom_call_target="tpu_custom_call" | custom-call | flops 589824000 | bytes 262144 | tf_op jit(solution)/shard_map/pallas_call | solution.py:259
  (5 shorter events, 0.1 us)
Async XLA Ops:
  2.0 7.8 %copy-start = (f32[2,4,256]{2,1,0:T(4,128)S(1)}, f32[2,4,256]{2,1,0:T(4,128)}, u32[]{:S(2)}) copy-start(f32[2,4,256]{2,1,0:T(4,128)} %get-tuple-element.11.own_ref) | copy-start | bytes 24580
  7.7 3.5 %collective-permute-start = (f32[2,2,4,256]{3,2,1,0:T(4,128)S(1)}, f32[2,2,4,256]{3,2,1,0:T(4,128)S(1)}, u32[]{:S(2)}, u32[]{:S(2)}) collective-permute-start(f32[2,2,4,256]{3,2,1,0:T(4,128)S(1)} %bitcast.15), channel_id=1, source_target_pairs={{0,8},{8,0},{16,24},{24,16},{1,9},{9,1},{17,25},{25,17},{2,10},{10... | collective-permute-start | bytes 49160 | tf_op jit(solution)/shard_map/ppermute | solution.py:300
  7.7 3.5 %collective-permute-start.1 = (f32[2,2,4,256]{3,2,1,0:T(4,128)S(1)}, f32[2,2,4,256]{3,2,1,0:T(4,128)S(1)}, u32[]{:S(2)}, u32[]{:S(2)}) collective-permute-start(f32[2,2,4,256]{3,2,1,0:T(4,128)S(1)} %bitcast.16), channel_id=1, source_target_pairs={{0,24},{8,16},{16,8},{24,0},{1,25},{9,17},{17,9},{25,1},{2,26},{10... | collective-permute-start | bytes 49160 | tf_op jit(solution)/shard_map/ppermute | solution.py:299
  11.3 7.2 %collective-permute-start.2 = (f32[3,2,4,256]{3,2,1,0:T(4,128)S(1)}, f32[3,2,4,256]{3,2,1,0:T(4,128)S(1)}, u32[]{:S(2)}, u32[]{:S(2)}) collective-permute-start(f32[3,2,4,256]{3,2,1,0:T(4,128)S(1)} %get-tuple-element.21), channel_id=1, source_target_pairs={{0,1},{1,0},{2,3},{3,2},{4,5},{5,4},{6,7},{7,6},{8,9},{9,8},{10,11... | collective-permute-start | bytes 73736 | tf_op jit(solution)/shard_map/ppermute | solution.py:310
  13.1 6.6 %collective-permute-start.3 = (f32[3,2,4,256]{3,2,1,0:T(4,128)S(1)}, f32[3,2,4,256]{3,2,1,0:T(4,128)S(1)}, u32[]{:S(2)}, u32[]{:S(2)}) collective-permute-start(f32[3,2,4,256]{3,2,1,0:T(4,128)S(1)} %get-tuple-element.20), channel_id=1, source_target_pairs={{0,3},{1,2},{2,1},{3,0},{4,7},{5,6},{6,5},{7,4},{8,11},{9,10},{10,... | collective-permute-start | bytes 73736 | tf_op jit(solution)/shard_map/ppermute | solution.py:309
  15.6 2.9 %copy-start.2 = (f32[3,1,1,2,256]{4,3,2,1,0:T(2,128)S(1)}, f32[3,1,1,2,256]{4,3,2,1,0:T(2,128)}, u32[]{:S(2)}) copy-start(f32[3,1,1,2,256]{4,3,2,1,0:T(2,128)} %speed_ref.3) | copy-start | bytes 18436
  18.4 1.2 %copy-start.1 = (f32[2,4,256]{2,1,0:T(4,128)S(1)}, f32[2,4,256]{2,1,0:T(4,128)}, u32[]{:S(2)}) copy-start(f32[2,4,256]{2,1,0:T(4,128)} %get-tuple-element.10.keep_ref) | copy-start | bytes 24580
  27.3 3.0 %collective-permute-start.4 = (f32[2,2,4,256]{3,2,1,0:T(4,128)S(1)}, f32[2,2,4,256]{3,2,1,0:T(4,128)S(1)}, u32[]{:S(2)}, u32[]{:S(2)}) collective-permute-start(f32[2,2,4,256]{3,2,1,0:T(4,128)S(1)} %all_to_all.5.plane_ref), channel_id=1, source_target_pairs={{0,8},{8,0},{16,24},{24,16},{1,9},{9,1},{17,25},{25,17},{2,10},{10... | collective-permute-start | bytes 49160 | tf_op jit(solution)/shard_map/ppermute | solution.py:300
  27.3 3.2 %collective-permute-start.5 = (f32[2,2,4,256]{3,2,1,0:T(4,128)S(1)}, f32[2,2,4,256]{3,2,1,0:T(4,128)S(1)}, u32[]{:S(2)}, u32[]{:S(2)}) collective-permute-start(f32[2,2,4,256]{3,2,1,0:T(4,128)S(1)} %all_to_all.5.plane_ref), channel_id=1, source_target_pairs={{0,24},{8,16},{16,8},{24,0},{1,25},{9,17},{17,9},{25,1},{2,26},{10... | collective-permute-start | bytes 49160 | tf_op jit(solution)/shard_map/ppermute | solution.py:299
  30.5 4.5 %collective-permute-start.6 = (f32[3,2,4,256]{3,2,1,0:T(4,128)S(1)}, f32[3,2,4,256]{3,2,1,0:T(4,128)S(1)}, u32[]{:S(2)}, u32[]{:S(2)}) collective-permute-start(f32[3,2,4,256]{3,2,1,0:T(4,128)S(1)} %get-tuple-element.19), channel_id=1, source_target_pairs={{0,1},{1,0},{2,3},{3,2},{4,5},{5,4},{6,7},{7,6},{8,9},{9,8},{10,11... | collective-permute-start | bytes 73736 | tf_op jit(solution)/shard_map/ppermute | solution.py:310
  31.3 5.6 %collective-permute-start.7 = (f32[3,2,4,256]{3,2,1,0:T(4,128)S(1)}, f32[3,2,4,256]{3,2,1,0:T(4,128)S(1)}, u32[]{:S(2)}, u32[]{:S(2)}) collective-permute-start(f32[3,2,4,256]{3,2,1,0:T(4,128)S(1)} %get-tuple-element.18), channel_id=1, source_target_pairs={{0,3},{1,2},{2,1},{3,0},{4,7},{5,6},{6,5},{7,4},{8,11},{9,10},{10,... | collective-permute-start | bytes 73736 | tf_op jit(solution)/shard_map/ppermute | solution.py:309

commit v2 on v0

--- a/solution.py
+++ b/solution.py
@@ -77,14 +77,8 @@
         keep_ref[z] = jnp.broadcast_to(jnp.where(keep, 1.0, 0.0), keep_ref.shape[1:])
 
 
-def ahead(axis):
-    return 1 - 2 * lax.rem(lax.axis_index(axis), 2)
-
-
 def y_shifts(size):
-    if size == 2:
-        return [[0], [-1, 1]]
-    return [[0], [ahead("gy")], [-ahead("gy")]]
+    return [[0], [-1, 1]] if size == 2 else [[0], [-1], [1]]
 
 
 def list_chunk(list_ref, chunk):
@@ -180,9 +174,9 @@
         total_ref[z] = totals[z]
 
 
-def slab_kernel(size_y, target_ref, before_ref, near_x_ref, far_x_ref, total_ref, near_ref, sum_ref, list_ref):
+def slab_kernel(size_y, target_ref, before_ref, left_ref, right_ref, total_ref, near_ref, sum_ref, list_ref):
     entries = []
-    for ref, x in ((near_x_ref, ahead("gx")), (far_x_ref, -ahead("gx"))):
+    for ref, x in ((left_ref, -1), (right_ref, 1)):
         for plane, shifts in enumerate(y_shifts(size_y)):
             for y in shifts:
                 entries += [(ref, (plane, z), (x, y, z)) for z in range(2)]
@@ -195,7 +189,7 @@
 
 def complete(size_y, first, z, speed_ref, own_ref, target_ref, before_ref, source_ref, near_ref, sum_ref, list_ref):
     entries = []
-    for column, x in enumerate((0, ahead("gx"), -ahead("gx"))):
+    for column, x in enumerate((0, -1, 1)):
         for plane, shifts in enumerate(y_shifts(size_y)):
             entries += [(source_ref, (column, plane), (x, y, 3 * z - 1)) for y in shifts]
     length = fill(near_ref, sum_ref, list_ref, entries)
@@ -205,7 +199,7 @@
     own = own_ref[z]
     accel = total - shifted(own, (0, 0, z)) * total[3:4]
     if first:
-        rows = [jnp.where(z == 1, speed_ref[c, 0, 0, 1:2, :], speed_ref[c, 0, 0, 0:1, :]) for c in range(3)]
+        rows = [speed_ref[c, 0, 0, z : z + 1, :] for c in range(3)]
         speed = jnp.concatenate(rows + [jnp.zeros_like(rows[0])], axis=0)
     else:
         speed = speed_ref[z]
@@ -214,47 +208,36 @@
     return jnp.where(row_index(*own.shape) < 3, place, own), speed
 
 
-def near_side():
-    return (1 + ahead("gz")) // 2
-
-
-def near_kernel(size_y, first, speed_ref, own_ref, target_ref, before_ref, source_ref, bin_ref, near_ref, sum_ref, list_ref):
-    place, speed = complete(
-        size_y, first, near_side(), speed_ref, own_ref, target_ref, before_ref, source_ref, near_ref, sum_ref, list_ref
-    )
+def below_kernel(size_y, first, speed_ref, own_ref, target_ref, before_ref, source_ref, bin_ref, near_ref, sum_ref, list_ref):
+    place, speed = complete(size_y, first, 0, speed_ref, own_ref, target_ref, before_ref, source_ref, near_ref, sum_ref, list_ref)
     bin_ref[0] = place
     bin_ref[1] = speed
 
 
-def far_kernel(size_y, first, last, keep_ref, bin_ref, speed_ref, own_ref, target_ref, before_ref, source_ref, place_out, speed_out, near_ref, sum_ref, list_ref):
-    other = near_side()
-    z = 1 - other
-    place, speed = complete(
-        size_y, first, z, speed_ref, own_ref, target_ref, before_ref, source_ref, near_ref, sum_ref, list_ref
-    )
-    if not last:
-        place_out[z] = place
-        speed_out[z] = speed
-        place_out[other] = bin_ref[0]
-        speed_out[other] = bin_ref[1]
-        return
-    for side in range(2):
-        keep = keep_ref[side, 0:1] > 0.0
-        moved = jnp.where(z == side, place, bin_ref[0])
-        kicked = jnp.where(z == side, speed, bin_ref[1])
+def above_kernel(size_y, first, last, keep_ref, bin_ref, speed_ref, own_ref, target_ref, before_ref, source_ref, place_out, speed_out, near_ref, sum_ref, list_ref):
+    place, speed = complete(size_y, first, 1, speed_ref, own_ref, target_ref, before_ref, source_ref, near_ref, sum_ref, list_ref)
+    for z, (moved, kicked) in enumerate(((bin_ref[0], bin_ref[1]), (place, speed))):
+        if not last:
+            place_out[z] = moved
+            speed_out[z] = kicked
+            continue
+        keep = keep_ref[z, 0:1] > 0.0
         for c in range(3):
-            place_out[c, 0, 0, side : side + 1, :] = jnp.where(keep, moved[c : c + 1], 0.0)
-            speed_out[c, 0, 0, side : side + 1, :] = jnp.where(keep, kicked[c : c + 1], 0.0)
+            place_out[c, 0, 0, z : z + 1, :] = jnp.where(keep, moved[c : c + 1], 0.0)
+            speed_out[c, 0, 0, z : z + 1, :] = jnp.where(keep, kicked[c : c + 1], 0.0)
 
 
 VMEM = pl.BlockSpec(memory_space=pltpu.VMEM)
 
 
-def swaps(axis):
+def from_before(value, axis):
     size = lax.axis_size(axis)
-    near = [(i, i ^ 1) for i in range(size)]
-    far = [(i, (((i + 1) ^ 1) - 1) % size) for i in range(size)]
-    return near, far
+    return lax.ppermute(value, axis, [(i, (i + 1) % size) for i in range(size)])
+
+
+def from_after(value, axis):
+    size = lax.axis_size(axis)
+    return lax.ppermute(value, axis, [((i + 1) % size, i) for i in range(size)])
 
 
 def call(kernel, inputs, outputs, sources, targets, slots, chunks):
@@ -288,46 +271,39 @@
         out_specs=(VMEM, VMEM),
     )(counts, positions, mass)
     speed = velocities
-    upper = lax.rem(lax.axis_index("gz"), 2)
     for subcycle in range(SUBCYCLES):
         first, last = subcycle == 0, subcycle == SUBCYCLES - 1
-        near, far = swaps("gy")
-        planes = [packed]
+        planes = [packed, from_before(packed, "gy")]
         if size_y > 2:
-            other = lax.ppermute(packed, "gy", far)
-            planes += [lax.ppermute(packed, "gy", near), other]
-        else:
-            planes.append(lax.ppermute(packed, "gy", near))
+            planes.append(from_after(packed, "gy"))
         plane = jnp.stack(planes)
-        near, far = swaps("gx")
-        far_x = lax.ppermute(plane, "gx", far)
-        near_x = lax.ppermute(plane, "gx", near)
+        right = from_after(plane, "gx")
+        left = from_before(plane, "gx")
         targets, total = call(
             functools.partial(plane_kernel, size_y),
             planes,
             (jax.ShapeDtypeStruct((2, slots, 48), BF16), running),
             6, 2, slots, 2,
         )
-        slab = jnp.stack([plane, near_x, far_x])
-        near, far = swaps("gz")
-        far_z = lax.ppermute(lax.dynamic_index_in_dim(slab, upper, 2, False), "gz", far)
-        near_z = lax.ppermute(lax.dynamic_index_in_dim(slab, 1 - upper, 2, False), "gz", near)
+        slab = jnp.stack([plane, left, right])
+        below = from_before(slab[:, :, 1], "gz")
+        above = from_after(slab[:, :, 0], "gz")
         (total,) = call(
             functools.partial(slab_kernel, size_y),
-            [targets, total, near_x, far_x],
+            [targets, total, left, right],
             (running,),
             12, 2, slots, 3,
         )
         state = [speed, packed, targets, total]
         (half_done,) = call(
-            functools.partial(near_kernel, size_y, first),
-            state + [near_z],
+            functools.partial(below_kernel, size_y, first),
+            state + [below],
             (bins,),
             9, 1, slots, 3,
         )
         packed, speed = call(
-            functools.partial(far_kernel, size_y, first, last),
-            [keep, half_done] + state + [far_z],
+            functools.partial(above_kernel, size_y, first, last),
+            [keep, half_done] + state + [above],
             (full, full) if last else (bins, bins),
             9, 1, slots, 3,
         )

time: 35.5 us -> 40.1 us (1.13)
  waiting for transfers between devices: 4.89 us -> 11.5 us
  starting transfers between devices: 14.4 us -> 11.7 us
  other arithmetic: 0.04 us -> 0.81 us
    ppermute x10, waiting for transfers between devices: 4.89 us -> 11.5 us  [the longest x6 11.5 us: from_before(): return lax.ppermute(value, axis, [(i, (i + 1) % size) for i in range(size)])]
    ppermute x10, starting transfers between devices: 14.4 us -> 11.7 us  [the longest x6 6.19 us: from_before(): return lax.ppermute(value, axis, [(i, (i + 1) % size) for i in range(size)])]
    another operation x4, other arithmetic: 0.04 us -> 0.81 us  [on_device(): slab = jnp.stack([plane, left, right])]
  transfers between devices with their start and end apart: 10 -> 10, of which waited for: 4 -> 6; matrix products, arithmetic and copies ran while one was open for 0% -> 0% of each run, Pallas kernels for 31% -> 27%
where the time goes in v2:
time: 40.1 us; the launch traced here: 39.9 us
  Pallas kernels  15 us (37%)
  starting transfers between devices  11.7 us (29%)
  waiting for transfers between devices  11.5 us (29%)
  other arithmetic  0.81 us (2%)
  between operations  0.79 us (2%)
    pallas_call x8, Pallas kernels, call(): pl.pallas_call(kernel, out_shape=outputs, in_specs=[VMEM] * len(inputs),...  13.7 us
    ppermute x6, waiting for transfers between devices, from_before(): return lax.ppermute(value, axis, [(i, (i + 1) % size) for i in range(size)])  11.5 us
    ppermute x6, starting transfers between devices, from_before(): return lax.ppermute(value, axis, [(i, (i + 1) % size) for i in range(size)])  6.19 us
    ppermute x4, starting transfers between devices, from_after(): return lax.ppermute(value, axis, [((i + 1) % size, i) for i in range(size)])  5.51 us
    pallas_call x1, Pallas kernels, on_device(): pl.pallas_call(pack_kernel, out_shape=(bins, bins), in_specs=[VMEM] * 3,...  1.39 us
    another operation x4, other arithmetic, on_device(): slab = jnp.stack([plane, left, right])  0.81 us
  transfers between devices with their start and end apart: 10, of which 6 were waited for; matrix products, arithmetic and copies ran while one was open for 0% of the time, Pallas kernels for 27%

profile of v2, /device:TPU:0, one launch (start us, length us, event | category | flops | bytes accessed | tf_op | source)
XLA Modules:
  0.0 39.9 jit_solution(4694014680341827758)
XLA Ops:
  0.6 1.4 %shard_map.59 = (f32[2,4,256]{2,1,0:T(4,128)}, f32[2,4,256]{2,1,0:T(4,128)}) custom-call(s32[1,1,2]{2,1,0:T(1,128)} %counts_ref.1, f32[3,1,1,2,256]{4,3,2,1,0:T(2,128)} %place_ref.1, f32[1,1,2,256]{3,2,1,0:T(2,128)} %mass_ref.1), custom_call_target="tpu_custom_call" | custom-call | tf_op jit(solution)/shard_map/pallas_call | solution.py:267
  2.0 3.0 %collective-permute-start = (f32[2,4,256]{2,1,0:T(4,128)}, f32[2,4,256]{2,1,0:T(4,128)S(1)}, u32[]{:S(2)}, u32[]{:S(2)}) collective-permute-start(f32[2,4,256]{2,1,0:T(4,128)} %get-tuple-element.11.refs_0_.own_ref), channel_id=1, source_target_pairs={{0,4},{4,0},{1,5},{5,1},{2,6},{6,2},{3,7},{7,3},{8,12},{12,8},{9,1... | collective-permute-start | bytes 24584 | tf_op jit(solution)/shard_map/ppermute | solution.py:235
  5.0 1.8 %collective-permute-done.refs_1_ = f32[2,4,256]{2,1,0:T(4,128)S(1)} collective-permute-done((f32[2,4,256]{2,1,0:T(4,128)}, f32[2,4,256]{2,1,0:T(4,128)S(1)}, u32[]{:S(2)}, u32[]{:S(2)}) %collective-permute-start) | collective-permute-done | bytes 8224 | tf_op jit(solution)/shard_map/ppermute | solution.py:235
  6.8 0.0 copy-start
  6.8 0.8 %fusion.1 = (f32[1,2,2,4,256]{4,3,1,0,2:T(4,128)S(1)}, f32[2,2,4,256]{3,2,0,1:T(4,128)S(1)}) fusion(f32[1,2,4,256]{3,2,0,1:T(4,128)S(1)} %bitcast.30, f32[1,2,4,256]{3,2,0,1:T(4,128)} %bitcast.29), kind=kLoop, calls=%fused_computation.9 | loop fusion | flops 4096 | bytes 49152 | tf_op jit(solution)/shard_map/stack | solution.py:288
  7.6 0.3 collective-permute-start.2
  7.9 0.2 collective-permute-start.1
  8.1 0.0 copy-done
  8.1 1.4 %shard_map.60 = (bf16[2,256,48]{2,1,0:T(8,128)(2,1)S(1)}, f32[2,256,32]{2,1,0:T(8,128)S(1)}) custom-call(f32[2,4,256]{2,1,0:T(4,128)S(1)} %copy-done, f32[2,4,256]{2,1,0:T(4,128)S(1)} %collective-permute-done.refs_1_), custom_call_target="tpu_custom_call" | custom-call | flops 786432000 | bytes 262144 | tf_op jit(solution)/shard_map/pallas_call | solution.py:246
  9.5 0.0 collective-permute-done.2
  9.5 1.6 %collective-permute-done.1 = f32[2,2,4,256]{3,2,0,1:T(4,128)S(1)} collective-permute-done((f32[2,2,4,256]{3,2,0,1:T(4,128)S(1)}, f32[2,2,4,256]{3,2,0,1:T(4,128)S(1)}, u32[]{:S(2)}, u32[]{:S(2)}) %collective-permute-start.1) | collective-permute-done | bytes 16416 | tf_op jit(solution)/shard_map/ppermute | solution.py:235
  11.2 4.0 %collective-permute-start.4 = (f32[3,2,4,256]{3,2,1,0:T(4,128)S(1)}, f32[3,2,4,256]{3,2,1,0:T(4,128)S(1)}, u32[]{:S(2)}, u32[]{:S(2)}) collective-permute-start(f32[3,2,4,256]{3,2,1,0:T(4,128)S(1)} %get-tuple-element.20), channel_id=1, source_target_pairs={{1,0},{2,1},{3,2},{0,3},{5,4},{6,5},{7,6},{4,7},{9,8},{10,9},{11,1... | collective-permute-start | bytes 73736 | tf_op jit(solution)/shard_map/ppermute | solution.py:240
  15.2 0.0 collective-permute-start.3
  15.2 0.0 copy-start.2
  15.2 2.9 %shard_map.61.before_ref = f32[2,256,32]{2,1,0:T(8,128)S(1)} custom-call(bf16[2,256,48]{2,1,0:T(8,128)(2,1)S(1)} %get-tuple-element.12.target_ref, f32[2,256,32]{2,1,0:T(8,128)S(1)} %get-tuple-element.13.before_ref, f32[2,2,4,256]{3,2,1,0:T(4,128)S(1)} %copy.6.left_ref, f32[2,2,4,256]{3,2,1,0:T(4,128)S(1)} %copy.7.right_ref), custom_call_target="tpu_custom_call" | custom-call | flops 1572864000 | bytes 262144 | tf_op jit(solution)/shard_map/pallas_call | solution.py:246
  18.1 0.0 copy-start.1
  18.1 2.7 %collective-permute-done.3.source_ref = f32[3,2,4,256]{3,2,1,0:T(4,128)S(1)} collective-permute-done((f32[3,2,4,256]{3,2,1,0:T(4,128)S(1)}, f32[3,2,4,256]{3,2,1,0:T(4,128)S(1)}, u32[]{:S(2)}, u32[]{:S(2)}) %collective-permute-start.3) | collective-permute-done | bytes 24608 | tf_op jit(solution)/shard_map/ppermute | solution.py:235
  20.8 0.0 copy-done.2
  20.8 1.1 %shard_map.62.bin_ref = f32[2,4,256]{2,1,0:T(4,128)S(1)} custom-call(f32[3,1,1,2,256]{4,3,2,1,0:T(2,128)S(1)} %copy-done.2, f32[2,4,256]{2,1,0:T(4,128)S(1)} %copy-done, bf16[2,256,48]{2,1,0:T(8,128)(2,1)S(1)} %get-tuple-element.12.target_ref, f32[2,256,32]{2,1,0:T(8,128)S(1)} %shard_map.61.before_ref, f32[3,2,4,256]{3,2,1,0:T(4,128)S(1)} %collective-permute-done.3.source_ref), custom_call_target="tpu_custom_call" | custom-call | flops 589824000 | bytes 262144 | tf_op jit(solution)/shard_map/pallas_call | solution.py:246
  22.0 0.0 collective-permute-done.4.source_ref
  22.0 0.0 copy-done.1
  22.0 1.1 %shard_map.63 = (f32[2,4,256]{2,1,0:T(4,128)S(1)}, f32[2,4,256]{2,1,0:T(4,128)S(1)}) custom-call(f32[2,4,256]{2,1,0:T(4,128)S(1)} %copy-done.1, f32[2,4,256]{2,1,0:T(4,128)S(1)} %shard_map.62.bin_ref, f32[3,1,1,2,256]{4,3,2,1,0:T(2,128)S(1)} %copy-done.2, f32[2,4,256]{2,1,0:T(4,128)S(1)} %copy-done, bf16[2,256,48]{2,1,0:T(8,128)(2,1)S(1)} %get-tuple-element.12.target_ref, ...), custom_call_target="tpu_custom_call" | custom-call | flops 589824000 | bytes 262144 | tf_op jit(solution)/shard_map/pallas_call | solution.py:246
  23.1 1.6 %collective-permute-start.5 = (f32[2,4,256]{2,1,0:T(4,128)S(1)}, f32[2,4,256]{2,1,0:T(4,128)S(1)}, u32[]{:S(2)}, u32[]{:S(2)}) collective-permute-start(f32[2,4,256]{2,1,0:T(4,128)S(1)} %get-tuple-element.15.refs_0_.own_ref), channel_id=1, source_target_pairs={{0,4},{4,0},{1,5},{5,1},{2,6},{6,2},{3,7},{7,3},{8,12},{12,8},{9,1... | collective-permute-start | bytes 24584 | tf_op jit(solution)/shard_map/ppermute | solution.py:235
  24.7 2.1 %collective-permute-done.5.refs_1_ = f32[2,4,256]{2,1,0:T(4,128)S(1)} collective-permute-done((f32[2,4,256]{2,1,0:T(4,128)S(1)}, f32[2,4,256]{2,1,0:T(4,128)S(1)}, u32[]{:S(2)}, u32[]{:S(2)}) %collective-permute-start.5) | collective-permute-done | bytes 8224 | tf_op jit(solution)/shard_map/ppermute | solution.py:235
  26.9 0.1 collective-permute-start.7
  26.9 0.5 %collective-permute-start.6 = (f32[2,2,4,256]{3,2,0,1:T(4,128)S(1)}, f32[2,2,4,256]{3,2,0,1:T(4,128)S(1)}, u32[]{:S(2)}, u32[]{:S(2)}) collective-permute-start(f32[2,2,4,256]{3,2,0,1:T(4,128)S(1)} %get-tuple-element.23), channel_id=1, source_target_pairs={{0,8},{8,16},{16,24},{24,0},{1,9},{9,17},{17,25},{25,1},{2,10},{10... | collective-permute-start | bytes 49160 | tf_op jit(solution)/shard_map/ppermute | solution.py:235
  27.4 1.4 %shard_map.64 = (bf16[2,256,48]{2,1,0:T(8,128)(2,1)S(1)}, f32[2,256,32]{2,1,0:T(8,128)S(1)}) custom-call(f32[2,4,256]{2,1,0:T(4,128)S(1)} %get-tuple-element.15.refs_0_.own_ref, f32[2,4,256]{2,1,0:T(4,128)S(1)} %collective-permute-done.5.refs_1_), custom_call_target="tpu_custom_call" | custom-call | flops 786432000 | bytes 262144 | tf_op jit(solution)/shard_map/pallas_call | solution.py:246
  28.8 0.0 collective-permute-done.7
  28.8 1.3 %collective-permute-done.6 = f32[2,2,4,256]{3,2,0,1:T(4,128)S(1)} collective-permute-done((f32[2,2,4,256]{3,2,0,1:T(4,128)S(1)}, f32[2,2,4,256]{3,2,0,1:T(4,128)S(1)}, u32[]{:S(2)}, u32[]{:S(2)}) %collective-permute-start.6) | collective-permute-done | bytes 16416 | tf_op jit(solution)/shard_map/ppermute | solution.py:235
  30.2 1.2 %collective-permute-start.9 = (f32[3,2,4,256]{3,2,1,0:T(4,128)S(1)}, f32[3,2,4,256]{3,2,1,0:T(4,128)S(1)}, u32[]{:S(2)}, u32[]{:S(2)}) collective-permute-start(f32[3,2,4,256]{3,2,1,0:T(4,128)S(1)} %get-tuple-element.18), channel_id=1, source_target_pairs={{1,0},{2,1},{3,2},{0,3},{5,4},{6,5},{7,6},{4,7},{9,8},{10,9},{11,1... | collective-permute-start | bytes 73736 | tf_op jit(solution)/shard_map/ppermute | solution.py:240
  31.3 0.9 %collective-permute-start.8 = (f32[3,2,4,256]{3,2,1,0:T(4,128)S(1)}, f32[3,2,4,256]{3,2,1,0:T(4,128)S(1)}, u32[]{:S(2)}, u32[]{:S(2)}) collective-permute-start(f32[3,2,4,256]{3,2,1,0:T(4,128)S(1)} %get-tuple-element.19), channel_id=1, source_target_pairs={{0,1},{1,2},{2,3},{3,0},{4,5},{5,6},{6,7},{7,4},{8,9},{9,10},{10,1... | collective-permute-start | bytes 73736 | tf_op jit(solution)/shard_map/ppermute | solution.py:235
  32.2 2.9 %shard_map.65.before_ref = f32[2,256,32]{2,1,0:T(8,128)S(1)} custom-call(bf16[2,256,48]{2,1,0:T(8,128)(2,1)S(1)} %get-tuple-element.16.target_ref, f32[2,256,32]{2,1,0:T(8,128)S(1)} %get-tuple-element.17.before_ref, f32[2,2,4,256]{3,2,1,0:T(4,128)S(1)} %copy.10.left_ref, f32[2,2,4,256]{3,2,1,0:T(4,128)S(1)} %copy.11.right_ref), custom_call_target="tpu_custom_call" | custom-call | flops 1572864000 | bytes 262144 | tf_op jit(solution)/shard_map/pallas_call | solution.py:246
  35.1 1.8 %collective-permute-done.8.source_ref = f32[3,2,4,256]{3,2,1,0:T(4,128)S(1)} collective-permute-done((f32[3,2,4,256]{3,2,1,0:T(4,128)S(1)}, f32[3,2,4,256]{3,2,1,0:T(4,128)S(1)}, u32[]{:S(2)}, u32[]{:S(2)}) %collective-permute-start.8) | collective-permute-done | bytes 24608 | tf_op jit(solution)/shard_map/ppermute | solution.py:235
  36.9 1.1 %shard_map.66.bin_ref = f32[2,4,256]{2,1,0:T(4,128)S(1)} custom-call(f32[2,4,256]{2,1,0:T(4,128)S(1)} %get-tuple-element.14.speed_ref, f32[2,4,256]{2,1,0:T(4,128)S(1)} %get-tuple-element.15.refs_0_.own_ref, bf16[2,256,48]{2,1,0:T(8,128)(2,1)S(1)} %get-tuple-element.16.target_ref, f32[2,256,32]{2,1,0:T(8,128)S(1)} %shard_map.65.before_ref, ...), custom_call_target="tpu_custom_call" | custom-call | flops 589824000 | bytes 262144 | tf_op jit(solution)/shard_map/pallas_call | solution.py:246
  38.1 0.0 collective-permute-done.9.source_ref
  38.1 1.8 %shard_map.67 = (f32[3,1,1,2,256]{4,3,2,1,0:T(2,128)}, f32[3,1,1,2,256]{4,3,2,1,0:T(2,128)}) custom-call(f32[2,4,256]{2,1,0:T(4,128)S(1)} %copy-done.1, f32[2,4,256]{2,1,0:T(4,128)S(1)} %shard_map.66.bin_ref, f32[2,4,256]{2,1,0:T(4,128)S(1)} %get-tuple-element.14.speed_ref, f32[2,4,256]{2,1,0:T(4,128)S(1)} %get-tuple-element.15.refs_0_.own_ref, ...), custom_call_target="tpu_custom_call" | custom-call | flops 589824000 | bytes 262144 | tf_op jit(solution)/shard_map/pallas_call | solution.py:246
  (9 shorter events, 0.1 us)
Async XLA Ops:
  2.0 4.8 %collective-permute-start = (f32[2,4,256]{2,1,0:T(4,128)}, f32[2,4,256]{2,1,0:T(4,128)S(1)}, u32[]{:S(2)}, u32[]{:S(2)}) collective-permute-start(f32[2,4,256]{2,1,0:T(4,128)} %get-tuple-element.11.refs_0_.own_ref), channel_id=1, source_target_pairs={{0,4},{4,0},{1,5},{5,1},{2,6},{6,2},{3,7},{7,3},{8,12},{12,8},{9,1... | collective-permute-start | bytes 24584 | tf_op jit(solution)/shard_map/ppermute | solution.py:235
  6.8 1.3 %copy-start = (f32[2,4,256]{2,1,0:T(4,128)S(1)}, f32[2,4,256]{2,1,0:T(4,128)}, u32[]{:S(2)}) copy-start(f32[2,4,256]{2,1,0:T(4,128)} %get-tuple-element.11.refs_0_.own_ref) | copy-start | bytes 24580
  7.6 1.9 %collective-permute-start.2 = (f32[2,2,4,256]{3,2,0,1:T(4,128)S(1)}, f32[2,2,4,256]{3,2,0,1:T(4,128)S(1)}, u32[]{:S(2)}, u32[]{:S(2)}) collective-permute-start(f32[2,2,4,256]{3,2,0,1:T(4,128)S(1)} %get-tuple-element.25), channel_id=1, source_target_pairs={{8,0},{16,8},{24,16},{0,24},{9,1},{17,9},{25,17},{1,25},{10,2},{18... | collective-permute-start | bytes 49160 | tf_op jit(solution)/shard_map/ppermute | solution.py:240
  7.9 3.2 %collective-permute-start.1 = (f32[2,2,4,256]{3,2,0,1:T(4,128)S(1)}, f32[2,2,4,256]{3,2,0,1:T(4,128)S(1)}, u32[]{:S(2)}, u32[]{:S(2)}) collective-permute-start(f32[2,2,4,256]{3,2,0,1:T(4,128)S(1)} %get-tuple-element.25), channel_id=1, source_target_pairs={{0,8},{8,16},{16,24},{24,0},{1,9},{9,17},{17,25},{25,1},{2,10},{10... | collective-permute-start | bytes 49160 | tf_op jit(solution)/shard_map/ppermute | solution.py:235
  11.2 10.8 %collective-permute-start.4 = (f32[3,2,4,256]{3,2,1,0:T(4,128)S(1)}, f32[3,2,4,256]{3,2,1,0:T(4,128)S(1)}, u32[]{:S(2)}, u32[]{:S(2)}) collective-permute-start(f32[3,2,4,256]{3,2,1,0:T(4,128)S(1)} %get-tuple-element.20), channel_id=1, source_target_pairs={{1,0},{2,1},{3,2},{0,3},{5,4},{6,5},{7,6},{4,7},{9,8},{10,9},{11,1... | collective-permute-start | bytes 73736 | tf_op jit(solution)/shard_map/ppermute | solution.py:240
  15.2 5.6 %collective-permute-start.3 = (f32[3,2,4,256]{3,2,1,0:T(4,128)S(1)}, f32[3,2,4,256]{3,2,1,0:T(4,128)S(1)}, u32[]{:S(2)}, u32[]{:S(2)}) collective-permute-start(f32[3,2,4,256]{3,2,1,0:T(4,128)S(1)} %get-tuple-element.21), channel_id=1, source_target_pairs={{0,1},{1,2},{2,3},{3,0},{4,5},{5,6},{6,7},{7,4},{8,9},{9,10},{10,1... | collective-permute-start | bytes 73736 | tf_op jit(solution)/shard_map/ppermute | solution.py:235
  15.2 5.6 %copy-start.2 = (f32[3,1,1,2,256]{4,3,2,1,0:T(2,128)S(1)}, f32[3,1,1,2,256]{4,3,2,1,0:T(2,128)}, u32[]{:S(2)}) copy-start(f32[3,1,1,2,256]{4,3,2,1,0:T(2,128)} %speed_ref.3) | copy-start | bytes 18436
  18.1 3.9 %copy-start.1 = (f32[2,4,256]{2,1,0:T(4,128)S(1)}, f32[2,4,256]{2,1,0:T(4,128)}, u32[]{:S(2)}) copy-start(f32[2,4,256]{2,1,0:T(4,128)} %get-tuple-element.10.keep_ref) | copy-start | bytes 24580
  23.1 3.7 %collective-permute-start.5 = (f32[2,4,256]{2,1,0:T(4,128)S(1)}, f32[2,4,256]{2,1,0:T(4,128)S(1)}, u32[]{:S(2)}, u32[]{:S(2)}) collective-permute-start(f32[2,4,256]{2,1,0:T(4,128)S(1)} %get-tuple-element.15.refs_0_.own_ref), channel_id=1, source_target_pairs={{0,4},{4,0},{1,5},{5,1},{2,6},{6,2},{3,7},{7,3},{8,12},{12,8},{9,1... | collective-permute-start | bytes 24584 | tf_op jit(solution)/shard_map/ppermute | solution.py:235
  26.9 1.9 %collective-permute-start.7 = (f32[2,2,4,256]{3,2,0,1:T(4,128)S(1)}, f32[2,2,4,256]{3,2,0,1:T(4,128)S(1)}, u32[]{:S(2)}, u32[]{:S(2)}) collective-permute-start(f32[2,2,4,256]{3,2,0,1:T(4,128)S(1)} %get-tuple-element.23), channel_id=1, source_target_pairs={{8,0},{16,8},{24,16},{0,24},{9,1},{17,9},{25,17},{1,25},{10,2},{18... | collective-permute-start | bytes 49160 | tf_op jit(solution)/shard_map/ppermute | solution.py:240
  26.9 3.2 %collective-permute-start.6 = (f32[2,2,4,256]{3,2,0,1:T(4,128)S(1)}, f32[2,2,4,256]{3,2,0,1:T(4,128)S(1)}, u32[]{:S(2)}, u32[]{:S(2)}) collective-permute-start(f32[2,2,4,256]{3,2,0,1:T(4,128)S(1)} %get-tuple-element.23), channel_id=1, source_target_pairs={{0,8},{8,16},{16,24},{24,0},{1,9},{9,17},{17,25},{25,1},{2,10},{10... | collective-permute-start | bytes 49160 | tf_op jit(solution)/shard_map/ppermute | solution.py:235
  30.2 7.9 %collective-permute-start.9 = (f32[3,2,4,256]{3,2,1,0:T(4,128)S(1)}, f32[3,2,4,256]{3,2,1,0:T(4,128)S(1)}, u32[]{:S(2)}, u32[]{:S(2)}) collective-permute-start(f32[3,2,4,256]{3,2,1,0:T(4,128)S(1)} %get-tuple-element.18), channel_id=1, source_target_pairs={{1,0},{2,1},{3,2},{0,3},{5,4},{6,5},{7,6},{4,7},{9,8},{10,9},{11,1... | collective-permute-start | bytes 73736 | tf_op jit(solution)/shard_map/ppermute | solution.py:240
  31.3 5.6 %collective-permute-start.8 = (f32[3,2,4,256]{3,2,1,0:T(4,128)S(1)}, f32[3,2,4,256]{3,2,1,0:T(4,128)S(1)}, u32[]{:S(2)}, u32[]{:S(2)}) collective-permute-start(f32[3,2,4,256]{3,2,1,0:T(4,128)S(1)} %get-tuple-element.19), channel_id=1, source_target_pairs={{0,1},{1,2},{2,3},{3,0},{4,5},{5,6},{6,7},{7,4},{8,9},{9,10},{10,1... | collective-permute-start | bytes 73736 | tf_op jit(solution)/shard_map/ppermute | solution.py:235

commit v3 on v0

--- a/solution.py
+++ b/solution.py
@@ -180,9 +180,9 @@
         total_ref[z] = totals[z]
 
 
-def slab_kernel(size_y, target_ref, before_ref, near_x_ref, far_x_ref, total_ref, near_ref, sum_ref, list_ref):
+def slab_kernel(size_y, target_ref, before_ref, left_ref, right_ref, total_ref, near_ref, sum_ref, list_ref):
     entries = []
-    for ref, x in ((near_x_ref, ahead("gx")), (far_x_ref, -ahead("gx"))):
+    for ref, x in ((left_ref, -1), (right_ref, 1)):
         for plane, shifts in enumerate(y_shifts(size_y)):
             for y in shifts:
                 entries += [(ref, (plane, z), (x, y, z)) for z in range(2)]
@@ -195,7 +195,7 @@
 
 def complete(size_y, first, z, speed_ref, own_ref, target_ref, before_ref, source_ref, near_ref, sum_ref, list_ref):
     entries = []
-    for column, x in enumerate((0, ahead("gx"), -ahead("gx"))):
+    for column, x in enumerate((0, -1, 1)):
         for plane, shifts in enumerate(y_shifts(size_y)):
             entries += [(source_ref, (column, plane), (x, y, 3 * z - 1)) for y in shifts]
     length = fill(near_ref, sum_ref, list_ref, entries)
@@ -255,6 +255,11 @@
     near = [(i, i ^ 1) for i in range(size)]
     far = [(i, (((i + 1) ^ 1) - 1) % size) for i in range(size)]
     return near, far
+
+
+def shift(axis, step):
+    size = lax.axis_size(axis)
+    return [(i, (i + step) % size) for i in range(size)]
 
 
 def call(kernel, inputs, outputs, sources, targets, slots, chunks):
@@ -299,22 +304,21 @@
         else:
             planes.append(lax.ppermute(packed, "gy", near))
         plane = jnp.stack(planes)
-        near, far = swaps("gx")
-        far_x = lax.ppermute(plane, "gx", far)
-        near_x = lax.ppermute(plane, "gx", near)
+        right = lax.ppermute(plane, "gx", shift("gx", -1))
+        left = lax.ppermute(plane, "gx", shift("gx", 1))
         targets, total = call(
             functools.partial(plane_kernel, size_y),
             planes,
             (jax.ShapeDtypeStruct((2, slots, 48), BF16), running),
             6, 2, slots, 2,
         )
-        slab = jnp.stack([plane, near_x, far_x])
+        slab = jnp.stack([plane, left, right])
         near, far = swaps("gz")
         far_z = lax.ppermute(lax.dynamic_index_in_dim(slab, upper, 2, False), "gz", far)
         near_z = lax.ppermute(lax.dynamic_index_in_dim(slab, 1 - upper, 2, False), "gz", near)
         (total,) = call(
             functools.partial(slab_kernel, size_y),
-            [targets, total, near_x, far_x],
+            [targets, total, left, right],
             (running,),
             12, 2, slots, 3,
         )

time: 35.5 us -> 36 us (1.014)
  the two profiles are of different devices: /device:TPU:0 before, /device:TPU:1 now
where the time goes in v3:
time: 36 us; the launch traced here: 35.9 us
  Pallas kernels  16.2 us (45%)
  starting transfers between devices  12.2 us (34%)
  waiting for transfers between devices  6.65 us (18%)
  between operations  0.8 us (2%)
    pallas_call x8, Pallas kernels, call(): pl.pallas_call(kernel, out_shape=outputs, in_specs=[VMEM] * len(inputs),...  14.9 us
    ppermute x2, starting transfers between devices, on_device(): left = lax.ppermute(plane, 'gx', shift('gx', 1))  4.4 us
    ppermute x2, waiting for transfers between devices, on_device(): right = lax.ppermute(plane, 'gx', shift('gx', -1))  3.54 us
    ppermute x2, starting transfers between devices, on_device(): lax.ppermute(lax.dynamic_index_in_dim(slab, upper, 2, False), 'gz', far)  3.13 us
    ppermute x2, waiting for transfers between devices, on_device(): planes.append(lax.ppermute(packed, 'gy', near))  3.1 us
    ppermute x2, starting transfers between devices, on_device(): planes.append(lax.ppermute(packed, 'gy', near))  2.78 us
    ppermute x2, starting transfers between devices, on_device(): lax.ppermute(lax.dynamic_index_in_dim(slab, 1 - upper, 2, False), 'gz', n...  1.83 us
    pallas_call x1, Pallas kernels, on_device(): pl.pallas_call(pack_kernel, out_shape=(bins, bins), in_specs=[VMEM] * 3,...  1.39 us
  transfers between devices with their start and end apart: 10, of which 4 were waited for; matrix products, arithmetic and copies ran while one was open for 0% of the time, Pallas kernels for 33%

profile of v3, /device:TPU:1, one launch (start us, length us, event | category | flops | bytes accessed | tf_op | source)
XLA Modules:
  0.0 35.9 jit_solution(788846116299534398)
XLA Ops:
  0.6 1.4 %shard_map.59 = (f32[2,4,256]{2,1,0:T(4,128)}, f32[2,4,256]{2,1,0:T(4,128)}) custom-call(s32[1,1,2]{2,1,0:T(1,128)} %counts_ref.1, f32[3,1,1,2,256]{4,3,2,1,0:T(2,128)} %place_ref.1, f32[1,1,2,256]{3,2,1,0:T(2,128)} %mass_ref.1), custom_call_target="tpu_custom_call" | custom-call | tf_op jit(solution)/shard_map/pallas_call | solution.py:289
  2.0 2.1 %collective-permute-start = (f32[2,4,256]{2,1,0:T(4,128)}, f32[2,4,256]{2,1,0:T(4,128)S(1)}, u32[]{:S(2)}, u32[]{:S(2)}) collective-permute-start(f32[2,4,256]{2,1,0:T(4,128)} %get-tuple-element.11.refs_0_.own_ref), channel_id=1, source_target_pairs={{0,4},{4,0},{1,5},{5,1},{2,6},{6,2},{3,7},{7,3},{8,12},{12,8},{9,1... | collective-permute-start | bytes 24584 | tf_op jit(solution)/shard_map/ppermute | solution.py:305
  4.1 0.0 copy-start
  4.1 1.2 %collective-permute-done.refs_1_ = f32[2,4,256]{2,1,0:T(4,128)S(1)} collective-permute-done((f32[2,4,256]{2,1,0:T(4,128)}, f32[2,4,256]{2,1,0:T(4,128)S(1)}, u32[]{:S(2)}, u32[]{:S(2)}) %collective-permute-start) | collective-permute-done | bytes 8224 | tf_op jit(solution)/shard_map/ppermute | solution.py:305
  5.3 0.0 copy-done
  5.4 3.2 %collective-permute-start.1 = (f32[2,2,4,256]{3,2,1,0:T(4,128)S(1)}, f32[2,2,4,256]{3,2,1,0:T(4,128)S(1)}, u32[]{:S(2)}, u32[]{:S(2)}) collective-permute-start(f32[2,2,4,256]{3,2,1,0:T(4,128)S(1)} %get-tuple-element.25), channel_id=1, source_target_pairs={{0,8},{8,16},{16,24},{24,0},{1,9},{9,17},{17,25},{25,1},{2,10},{10... | collective-permute-start | bytes 49160 | tf_op jit(solution)/shard_map/ppermute | solution.py:308
  8.6 0.0 collective-permute-start.2
  8.6 1.4 %shard_map.60 = (bf16[2,256,48]{2,1,0:T(8,128)(2,1)S(1)}, f32[2,256,32]{2,1,0:T(8,128)S(1)}) custom-call(f32[2,4,256]{2,1,0:T(4,128)S(1)} %copy-done, f32[2,4,256]{2,1,0:T(4,128)S(1)} %collective-permute-done.refs_1_), custom_call_target="tpu_custom_call" | custom-call | flops 786432000 | bytes 262144 | tf_op jit(solution)/shard_map/pallas_call | solution.py:268
  9.9 0.0 collective-permute-done.1.left_ref
  9.9 1.8 %collective-permute-done.2.right_ref = f32[2,2,4,256]{3,2,1,0:T(4,128)S(1)} collective-permute-done((f32[2,2,4,256]{3,2,1,0:T(4,128)S(1)}, f32[2,2,4,256]{3,2,1,0:T(4,128)S(1)}, u32[]{:S(2)}, u32[]{:S(2)}) %collective-permute-start.2) | collective-permute-done | bytes 16416 | tf_op jit(solution)/shard_map/ppermute | solution.py:307
  11.8 1.4 %collective-permute-start.3 = (f32[3,2,4,256]{3,2,1,0:T(4,128)S(1)}, f32[3,2,4,256]{3,2,1,0:T(4,128)S(1)}, u32[]{:S(2)}, u32[]{:S(2)}) collective-permute-start(f32[3,2,4,256]{3,2,1,0:T(4,128)S(1)} %get-tuple-element.21), channel_id=1, source_target_pairs={{0,1},{1,0},{2,3},{3,2},{4,5},{5,4},{6,7},{7,6},{8,9},{9,8},{10,11... | collective-permute-start | bytes 73736 | tf_op jit(solution)/shard_map/ppermute | solution.py:318
  13.1 2.2 %collective-permute-start.4 = (f32[3,2,4,256]{3,2,1,0:T(4,128)S(1)}, f32[3,2,4,256]{3,2,1,0:T(4,128)S(1)}, u32[]{:S(2)}, u32[]{:S(2)}) collective-permute-start(f32[3,2,4,256]{3,2,1,0:T(4,128)S(1)} %get-tuple-element.20), channel_id=1, source_target_pairs={{0,3},{1,2},{2,1},{3,0},{4,7},{5,6},{6,5},{7,4},{8,11},{9,10},{10,... | collective-permute-start | bytes 73736 | tf_op jit(solution)/shard_map/ppermute | solution.py:317
  15.3 0.0 copy-start.2
  15.3 3.4 %shard_map.61.before_ref = f32[2,256,32]{2,1,0:T(8,128)S(1)} custom-call(bf16[2,256,48]{2,1,0:T(8,128)(2,1)S(1)} %get-tuple-element.12.target_ref, f32[2,256,32]{2,1,0:T(8,128)S(1)} %get-tuple-element.13.before_ref, f32[2,2,4,256]{3,2,1,0:T(4,128)S(1)} %collective-permute-done.1.left_ref, f32[2,2,4,256]{3,2,1,0:T(4,128)S(1)} %collective-permute-done.2.right_ref), custom_call_target="tpu_custom_call" | custom-call | flops 1572864000 | bytes 262144 | tf_op jit(solution)/shard_map/pallas_call | solution.py:268
  18.8 0.0 copy-start.1
  18.8 0.0 collective-permute-done.3.source_ref
  18.8 0.0 copy-done.2
  18.8 1.2 %shard_map.62.bin_ref = f32[2,4,256]{2,1,0:T(4,128)S(1)} custom-call(f32[3,1,1,2,256]{4,3,2,1,0:T(2,128)S(1)} %copy-done.2, f32[2,4,256]{2,1,0:T(4,128)S(1)} %copy-done, bf16[2,256,48]{2,1,0:T(8,128)(2,1)S(1)} %get-tuple-element.12.target_ref, f32[2,256,32]{2,1,0:T(8,128)S(1)} %shard_map.61.before_ref, f32[3,2,4,256]{3,2,1,0:T(4,128)S(1)} %collective-permute-done.3.source_ref), custom_call_target="tpu_custom_call" | custom-call | flops 589824000 | bytes 262144 | tf_op jit(solution)/shard_map/pallas_call | solution.py:268
  20.0 0.0 collective-permute-done.4.source_ref
  20.0 0.0 copy-done.1
  20.0 1.2 %shard_map.63 = (f32[2,4,256]{2,1,0:T(4,128)S(1)}, f32[2,4,256]{2,1,0:T(4,128)S(1)}) custom-call(f32[2,4,256]{2,1,0:T(4,128)S(1)} %copy-done.1, f32[2,4,256]{2,1,0:T(4,128)S(1)} %shard_map.62.bin_ref, f32[3,1,1,2,256]{4,3,2,1,0:T(2,128)S(1)} %copy-done.2, f32[2,4,256]{2,1,0:T(4,128)S(1)} %copy-done, bf16[2,256,48]{2,1,0:T(8,128)(2,1)S(1)} %get-tuple-element.12.target_ref, ...), custom_call_target="tpu_custom_call" | custom-call | flops 589824000 | bytes 262144 | tf_op jit(solution)/shard_map/pallas_call | solution.py:268
  21.1 0.7 %collective-permute-start.5 = (f32[2,4,256]{2,1,0:T(4,128)S(1)}, f32[2,4,256]{2,1,0:T(4,128)S(1)}, u32[]{:S(2)}, u32[]{:S(2)}) collective-permute-start(f32[2,4,256]{2,1,0:T(4,128)S(1)} %get-tuple-element.15.refs_0_.own_ref), channel_id=1, source_target_pairs={{0,4},{4,0},{1,5},{5,1},{2,6},{6,2},{3,7},{7,3},{8,12},{12,8},{9,1... | collective-permute-start | bytes 24584 | tf_op jit(solution)/shard_map/ppermute | solution.py:305
  21.9 1.9 %collective-permute-done.5.refs_1_ = f32[2,4,256]{2,1,0:T(4,128)S(1)} collective-permute-done((f32[2,4,256]{2,1,0:T(4,128)S(1)}, f32[2,4,256]{2,1,0:T(4,128)S(1)}, u32[]{:S(2)}, u32[]{:S(2)}) %collective-permute-start.5) | collective-permute-done | bytes 8224 | tf_op jit(solution)/shard_map/ppermute | solution.py:305
  23.7 1.2 %collective-permute-start.6 = (f32[2,2,4,256]{3,2,1,0:T(4,128)S(1)}, f32[2,2,4,256]{3,2,1,0:T(4,128)S(1)}, u32[]{:S(2)}, u32[]{:S(2)}) collective-permute-start(f32[2,2,4,256]{3,2,1,0:T(4,128)S(1)} %get-tuple-element.23), channel_id=1, source_target_pairs={{0,8},{8,16},{16,24},{24,0},{1,9},{9,17},{17,25},{25,1},{2,10},{10... | collective-permute-start | bytes 49160 | tf_op jit(solution)/shard_map/ppermute | solution.py:308
  24.9 0.0 collective-permute-start.7
  24.9 1.4 %shard_map.64 = (bf16[2,256,48]{2,1,0:T(8,128)(2,1)S(1)}, f32[2,256,32]{2,1,0:T(8,128)S(1)}) custom-call(f32[2,4,256]{2,1,0:T(4,128)S(1)} %get-tuple-element.15.refs_0_.own_ref, f32[2,4,256]{2,1,0:T(4,128)S(1)} %collective-permute-done.5.refs_1_), custom_call_target="tpu_custom_call" | custom-call | flops 786432000 | bytes 262144 | tf_op jit(solution)/shard_map/pallas_call | solution.py:268
  26.3 0.0 collective-permute-done.6.left_ref
  26.3 1.8 %collective-permute-done.7.right_ref = f32[2,2,4,256]{3,2,1,0:T(4,128)S(1)} collective-permute-done((f32[2,2,4,256]{3,2,1,0:T(4,128)S(1)}, f32[2,2,4,256]{3,2,1,0:T(4,128)S(1)}, u32[]{:S(2)}, u32[]{:S(2)}) %collective-permute-start.7) | collective-permute-done | bytes 16416 | tf_op jit(solution)/shard_map/ppermute | solution.py:307
  28.1 0.5 %collective-permute-start.8 = (f32[3,2,4,256]{3,2,1,0:T(4,128)S(1)}, f32[3,2,4,256]{3,2,1,0:T(4,128)S(1)}, u32[]{:S(2)}, u32[]{:S(2)}) collective-permute-start(f32[3,2,4,256]{3,2,1,0:T(4,128)S(1)} %get-tuple-element.19), channel_id=1, source_target_pairs={{0,1},{1,0},{2,3},{3,2},{4,5},{5,4},{6,7},{7,6},{8,9},{9,8},{10,11... | collective-permute-start | bytes 73736 | tf_op jit(solution)/shard_map/ppermute | solution.py:318
  28.6 0.9 %collective-permute-start.9 = (f32[3,2,4,256]{3,2,1,0:T(4,128)S(1)}, f32[3,2,4,256]{3,2,1,0:T(4,128)S(1)}, u32[]{:S(2)}, u32[]{:S(2)}) collective-permute-start(f32[3,2,4,256]{3,2,1,0:T(4,128)S(1)} %get-tuple-element.18), channel_id=1, source_target_pairs={{0,3},{1,2},{2,1},{3,0},{4,7},{5,6},{6,5},{7,4},{8,11},{9,10},{10,... | collective-permute-start | bytes 73736 | tf_op jit(solution)/shard_map/ppermute | solution.py:317
  29.5 3.4 %shard_map.65.before_ref = f32[2,256,32]{2,1,0:T(8,128)S(1)} custom-call(bf16[2,256,48]{2,1,0:T(8,128)(2,1)S(1)} %get-tuple-element.16.target_ref, f32[2,256,32]{2,1,0:T(8,128)S(1)} %get-tuple-element.17.before_ref, f32[2,2,4,256]{3,2,1,0:T(4,128)S(1)} %collective-permute-done.6.left_ref, f32[2,2,4,256]{3,2,1,0:T(4,128)S(1)} %collective-permute-done.7.right_ref), custom_call_target="tpu_custom_call" | custom-call | flops 1572864000 | bytes 262144 | tf_op jit(solution)/shard_map/pallas_call | solution.py:268
  33.0 0.0 collective-permute-done.8.source_ref
  33.0 1.1 %shard_map.66.bin_ref = f32[2,4,256]{2,1,0:T(4,128)S(1)} custom-call(f32[2,4,256]{2,1,0:T(4,128)S(1)} %get-tuple-element.14.speed_ref, f32[2,4,256]{2,1,0:T(4,128)S(1)} %get-tuple-element.15.refs_0_.own_ref, bf16[2,256,48]{2,1,0:T(8,128)(2,1)S(1)} %get-tuple-element.16.target_ref, f32[2,256,32]{2,1,0:T(8,128)S(1)} %shard_map.65.before_ref, ...), custom_call_target="tpu_custom_call" | custom-call | flops 589824000 | bytes 262144 | tf_op jit(solution)/shard_map/pallas_call | solution.py:268
  34.1 0.0 collective-permute-done.9.source_ref
  34.2 1.8 %shard_map.67 = (f32[3,1,1,2,256]{4,3,2,1,0:T(2,128)}, f32[3,1,1,2,256]{4,3,2,1,0:T(2,128)}) custom-call(f32[2,4,256]{2,1,0:T(4,128)S(1)} %copy-done.1, f32[2,4,256]{2,1,0:T(4,128)S(1)} %shard_map.66.bin_ref, f32[2,4,256]{2,1,0:T(4,128)S(1)} %get-tuple-element.14.speed_ref, f32[2,4,256]{2,1,0:T(4,128)S(1)} %get-tuple-element.15.refs_0_.own_ref, ...), custom_call_target="tpu_custom_call" | custom-call | flops 589824000 | bytes 262144 | tf_op jit(solution)/shard_map/pallas_call | solution.py:268
  (6 shorter events, 0.1 us)
Async XLA Ops:
  2.0 3.3 %collective-permute-start = (f32[2,4,256]{2,1,0:T(4,128)}, f32[2,4,256]{2,1,0:T(4,128)S(1)}, u32[]{:S(2)}, u32[]{:S(2)}) collective-permute-start(f32[2,4,256]{2,1,0:T(4,128)} %get-tuple-element.11.refs_0_.own_ref), channel_id=1, source_target_pairs={{0,4},{4,0},{1,5},{5,1},{2,6},{6,2},{3,7},{7,3},{8,12},{12,8},{9,1... | collective-permute-start | bytes 24584 | tf_op jit(solution)/shard_map/ppermute | solution.py:305
  4.1 1.3 %copy-start = (f32[2,4,256]{2,1,0:T(4,128)S(1)}, f32[2,4,256]{2,1,0:T(4,128)}, u32[]{:S(2)}) copy-start(f32[2,4,256]{2,1,0:T(4,128)} %get-tuple-element.11.refs_0_.own_ref) | copy-start | bytes 24580
  5.4 4.6 %collective-permute-start.1 = (f32[2,2,4,256]{3,2,1,0:T(4,128)S(1)}, f32[2,2,4,256]{3,2,1,0:T(4,128)S(1)}, u32[]{:S(2)}, u32[]{:S(2)}) collective-permute-start(f32[2,2,4,256]{3,2,1,0:T(4,128)S(1)} %get-tuple-element.25), channel_id=1, source_target_pairs={{0,8},{8,16},{16,24},{24,0},{1,9},{9,17},{17,25},{25,1},{2,10},{10... | collective-permute-start | bytes 49160 | tf_op jit(solution)/shard_map/ppermute | solution.py:308
  8.6 3.2 %collective-permute-start.2 = (f32[2,2,4,256]{3,2,1,0:T(4,128)S(1)}, f32[2,2,4,256]{3,2,1,0:T(4,128)S(1)}, u32[]{:S(2)}, u32[]{:S(2)}) collective-permute-start(f32[2,2,4,256]{3,2,1,0:T(4,128)S(1)} %get-tuple-element.25), channel_id=1, source_target_pairs={{0,24},{8,0},{16,8},{24,16},{1,25},{9,1},{17,9},{25,17},{2,26},{10... | collective-permute-start | bytes 49160 | tf_op jit(solution)/shard_map/ppermute | solution.py:307
  11.8 7.0 %collective-permute-start.3 = (f32[3,2,4,256]{3,2,1,0:T(4,128)S(1)}, f32[3,2,4,256]{3,2,1,0:T(4,128)S(1)}, u32[]{:S(2)}, u32[]{:S(2)}) collective-permute-start(f32[3,2,4,256]{3,2,1,0:T(4,128)S(1)} %get-tuple-element.21), channel_id=1, source_target_pairs={{0,1},{1,0},{2,3},{3,2},{4,5},{5,4},{6,7},{7,6},{8,9},{9,8},{10,11... | collective-permute-start | bytes 73736 | tf_op jit(solution)/shard_map/ppermute | solution.py:318
  13.1 6.8 %collective-permute-start.4 = (f32[3,2,4,256]{3,2,1,0:T(4,128)S(1)}, f32[3,2,4,256]{3,2,1,0:T(4,128)S(1)}, u32[]{:S(2)}, u32[]{:S(2)}) collective-permute-start(f32[3,2,4,256]{3,2,1,0:T(4,128)S(1)} %get-tuple-element.20), channel_id=1, source_target_pairs={{0,3},{1,2},{2,1},{3,0},{4,7},{5,6},{6,5},{7,4},{8,11},{9,10},{10,... | collective-permute-start | bytes 73736 | tf_op jit(solution)/shard_map/ppermute | solution.py:317
  15.3 3.5 %copy-start.2 = (f32[3,1,1,2,256]{4,3,2,1,0:T(2,128)S(1)}, f32[3,1,1,2,256]{4,3,2,1,0:T(2,128)}, u32[]{:S(2)}) copy-start(f32[3,1,1,2,256]{4,3,2,1,0:T(2,128)} %speed_ref.3) | copy-start | bytes 18436
  18.8 1.2 %copy-start.1 = (f32[2,4,256]{2,1,0:T(4,128)S(1)}, f32[2,4,256]{2,1,0:T(4,128)}, u32[]{:S(2)}) copy-start(f32[2,4,256]{2,1,0:T(4,128)} %get-tuple-element.10.keep_ref) | copy-start | bytes 24580
  21.1 2.6 %collective-permute-start.5 = (f32[2,4,256]{2,1,0:T(4,128)S(1)}, f32[2,4,256]{2,1,0:T(4,128)S(1)}, u32[]{:S(2)}, u32[]{:S(2)}) collective-permute-start(f32[2,4,256]{2,1,0:T(4,128)S(1)} %get-tuple-element.15.refs_0_.own_ref), channel_id=1, source_target_pairs={{0,4},{4,0},{1,5},{5,1},{2,6},{6,2},{3,7},{7,3},{8,12},{12,8},{9,1... | collective-permute-start | bytes 24584 | tf_op jit(solution)/shard_map/ppermute | solution.py:305
  23.7 2.6 %collective-permute-start.6 = (f32[2,2,4,256]{3,2,1,0:T(4,128)S(1)}, f32[2,2,4,256]{3,2,1,0:T(4,128)S(1)}, u32[]{:S(2)}, u32[]{:S(2)}) collective-permute-start(f32[2,2,4,256]{3,2,1,0:T(4,128)S(1)} %get-tuple-element.23), channel_id=1, source_target_pairs={{0,8},{8,16},{16,24},{24,0},{1,9},{9,17},{17,25},{25,1},{2,10},{10... | collective-permute-start | bytes 49160 | tf_op jit(solution)/shard_map/ppermute | solution.py:308
  24.9 3.2 %collective-permute-start.7 = (f32[2,2,4,256]{3,2,1,0:T(4,128)S(1)}, f32[2,2,4,256]{3,2,1,0:T(4,128)S(1)}, u32[]{:S(2)}, u32[]{:S(2)}) collective-permute-start(f32[2,2,4,256]{3,2,1,0:T(4,128)S(1)} %get-tuple-element.23), channel_id=1, source_target_pairs={{0,24},{8,0},{16,8},{24,16},{1,25},{9,1},{17,9},{25,17},{2,26},{10... | collective-permute-start | bytes 49160 | tf_op jit(solution)/shard_map/ppermute | solution.py:307
  28.1 4.9 %collective-permute-start.8 = (f32[3,2,4,256]{3,2,1,0:T(4,128)S(1)}, f32[3,2,4,256]{3,2,1,0:T(4,128)S(1)}, u32[]{:S(2)}, u32[]{:S(2)}) collective-permute-start(f32[3,2,4,256]{3,2,1,0:T(4,128)S(1)} %get-tuple-element.19), channel_id=1, source_target_pairs={{0,1},{1,0},{2,3},{3,2},{4,5},{5,4},{6,7},{7,6},{8,9},{9,8},{10,11... | collective-permute-start | bytes 73736 | tf_op jit(solution)/shard_map/ppermute | solution.py:318
  28.6 5.6 %collective-permute-start.9 = (f32[3,2,4,256]{3,2,1,0:T(4,128)S(1)}, f32[3,2,4,256]{3,2,1,0:T(4,128)S(1)}, u32[]{:S(2)}, u32[]{:S(2)}) collective-permute-start(f32[3,2,4,256]{3,2,1,0:T(4,128)S(1)} %get-tuple-element.18), channel_id=1, source_target_pairs={{0,3},{1,2},{2,1},{3,0},{4,7},{5,6},{6,5},{7,4},{8,11},{9,10},{10,... | collective-permute-start | bytes 73736 | tf_op jit(solution)/shard_map/ppermute | solution.py:317

commit v4 on v0

--- a/solution.py
+++ b/solution.py
@@ -188,7 +188,7 @@
                 entries += [(ref, (plane, z), (x, y, z)) for z in range(2)]
     length = fill(near_ref, sum_ref, list_ref, entries)
     targets = [target_ref[z] for z in range(2)]
-    totals = sums_over(targets, (before_ref[0], before_ref[1]), near_ref, sum_ref, list_ref, length, len(entries), 3)
+    totals = sums_over(targets, (before_ref[0], before_ref[1]), near_ref, sum_ref, list_ref, length, len(entries), 9)
     for z in range(2):
         total_ref[z] = totals[z]
 
@@ -300,8 +300,8 @@
             planes.append(lax.ppermute(packed, "gy", near))
         plane = jnp.stack(planes)
         near, far = swaps("gx")
+        near_x = lax.ppermute(plane, "gx", near)
         far_x = lax.ppermute(plane, "gx", far)
-        near_x = lax.ppermute(plane, "gx", near)
         targets, total = call(
             functools.partial(plane_kernel, size_y),
             planes,

time: 35.5 us -> 34.8 us (0.980)
  Pallas kernels: 15.1 us -> 13.7 us
  starting transfers between devices: 14.4 us -> 15.1 us
    pallas_call x8, Pallas kernels: 13.7 us -> 12.4 us  [call(): pl.pallas_call(kernel, out_shape=outputs, in_specs=[VMEM] * len(inputs),...]
    ppermute x2, starting transfers between devices: 3.41 us -> 4.08 us  [on_device(): lax.ppermute(lax.dynamic_index_in_dim(slab, upper, 2, False), 'gz', far)]
  transfers between devices with their start and end apart: 10 -> 10, of which waited for: 4 -> 4; matrix products, arithmetic and copies ran while one was open for 0% -> 0% of each run, Pallas kernels for 31% -> 27%
where the time goes in v4:
time: 34.8 us; the launch traced here: 34.6 us
  starting transfers between devices  15.1 us (43%)
  Pallas kernels  13.7 us (39%)
  waiting for transfers between devices  4.91 us (14%)
  between operations  0.8 us (2%)
    pallas_call x8, Pallas kernels, call(): pl.pallas_call(kernel, out_shape=outputs, in_specs=[VMEM] * len(inputs),...  12.4 us
    ppermute x2, starting transfers between devices, on_device(): planes.append(lax.ppermute(packed, 'gy', near))  4.56 us
    ppermute x2, starting transfers between devices, on_device(): lax.ppermute(lax.dynamic_index_in_dim(slab, upper, 2, False), 'gz', far)  4.08 us
    ppermute x2, waiting for transfers between devices, on_device(): planes.append(lax.ppermute(packed, 'gy', near))  3.96 us
    ppermute x2, starting transfers between devices, on_device(): far_x = lax.ppermute(plane, 'gx', far)  3.72 us
    ppermute x2, starting transfers between devices, on_device(): lax.ppermute(lax.dynamic_index_in_dim(slab, 1 - upper, 2, False), 'gz', n...  2.57 us
    pallas_call x1, Pallas kernels, on_device(): pl.pallas_call(pack_kernel, out_shape=(bins, bins), in_specs=[VMEM] * 3,...  1.39 us
  transfers between devices with their start and end apart: 10, of which 4 were waited for; matrix products, arithmetic and copies ran while one was open for 0% of the time, Pallas kernels for 27%

profile of v4, /device:TPU:0, one launch (start us, length us, event | category | flops | bytes accessed | tf_op | source)
XLA Modules:
  0.0 34.6 jit_solution(14210831561622234888)
XLA Ops:
  0.6 1.4 %shard_map.59 = (f32[2,4,256]{2,1,0:T(4,128)}, f32[2,4,256]{2,1,0:T(4,128)}) custom-call(s32[1,1,2]{2,1,0:T(1,128)} %counts_ref.1, f32[3,1,1,2,256]{4,3,2,1,0:T(2,128)} %place_ref.1, f32[1,1,2,256]{3,2,1,0:T(2,128)} %mass_ref.1), custom_call_target="tpu_custom_call" | custom-call | tf_op jit(solution)/shard_map/pallas_call | solution.py:284
  2.0 3.0 %collective-permute-start = (f32[2,4,256]{2,1,0:T(4,128)}, f32[2,4,256]{2,1,0:T(4,128)S(1)}, u32[]{:S(2)}, u32[]{:S(2)}) collective-permute-start(f32[2,4,256]{2,1,0:T(4,128)} %get-tuple-element.11.refs_0_.own_ref), channel_id=1, source_target_pairs={{0,4},{4,0},{1,5},{5,1},{2,6},{6,2},{3,7},{7,3},{8,12},{12,8},{9,1... | collective-permute-start | bytes 24584 | tf_op jit(solution)/shard_map/ppermute | solution.py:300
  5.0 0.0 copy-start
  5.0 1.8 %collective-permute-done.refs_1_ = f32[2,4,256]{2,1,0:T(4,128)S(1)} collective-permute-done((f32[2,4,256]{2,1,0:T(4,128)}, f32[2,4,256]{2,1,0:T(4,128)S(1)}, u32[]{:S(2)}, u32[]{:S(2)}) %collective-permute-start) | collective-permute-done | bytes 8224 | tf_op jit(solution)/shard_map/ppermute | solution.py:300
  6.8 0.0 copy-done
  6.8 0.1 collective-permute-start.1
  6.9 2.1 %collective-permute-start.2 = (f32[2,2,4,256]{3,2,1,0:T(4,128)S(1)}, f32[2,2,4,256]{3,2,1,0:T(4,128)S(1)}, u32[]{:S(2)}, u32[]{:S(2)}) collective-permute-start(f32[2,2,4,256]{3,2,1,0:T(4,128)S(1)} %get-tuple-element.25), channel_id=1, source_target_pairs={{0,24},{8,16},{16,8},{24,0},{1,25},{9,17},{17,9},{25,1},{2,26},{10... | collective-permute-start | bytes 49160 | tf_op jit(solution)/shard_map/ppermute | solution.py:304
  9.0 1.4 %shard_map.60 = (bf16[2,256,48]{2,1,0:T(8,128)(2,1)S(1)}, f32[2,256,32]{2,1,0:T(8,128)S(1)}) custom-call(f32[2,4,256]{2,1,0:T(4,128)S(1)} %copy-done, f32[2,4,256]{2,1,0:T(4,128)S(1)} %collective-permute-done.refs_1_), custom_call_target="tpu_custom_call" | custom-call | flops 786432000 | bytes 262144 | tf_op jit(solution)/shard_map/pallas_call | solution.py:263
  10.4 0.0 collective-permute-done.1.near_x_ref
  10.4 0.1 collective-permute-done.2.far_x_ref
  10.5 1.8 %collective-permute-start.3 = (f32[3,2,4,256]{3,2,1,0:T(4,128)S(1)}, f32[3,2,4,256]{3,2,1,0:T(4,128)S(1)}, u32[]{:S(2)}, u32[]{:S(2)}) collective-permute-start(f32[3,2,4,256]{3,2,1,0:T(4,128)S(1)} %get-tuple-element.21), channel_id=1, source_target_pairs={{0,1},{1,0},{2,3},{3,2},{4,5},{5,4},{6,7},{7,6},{8,9},{9,8},{10,11... | collective-permute-start | bytes 73736 | tf_op jit(solution)/shard_map/ppermute | solution.py:314
  12.3 2.5 %collective-permute-start.4 = (f32[3,2,4,256]{3,2,1,0:T(4,128)S(1)}, f32[3,2,4,256]{3,2,1,0:T(4,128)S(1)}, u32[]{:S(2)}, u32[]{:S(2)}) collective-permute-start(f32[3,2,4,256]{3,2,1,0:T(4,128)S(1)} %get-tuple-element.20), channel_id=1, source_target_pairs={{0,3},{1,2},{2,1},{3,0},{4,7},{5,6},{6,5},{7,4},{8,11},{9,10},{10,... | collective-permute-start | bytes 73736 | tf_op jit(solution)/shard_map/ppermute | solution.py:313
  14.8 0.0 copy-start.2
  14.8 2.2 %shard_map.61.before_ref = f32[2,256,32]{2,1,0:T(8,128)S(1)} custom-call(bf16[2,256,48]{2,1,0:T(8,128)(2,1)S(1)} %get-tuple-element.12.target_ref, f32[2,256,32]{2,1,0:T(8,128)S(1)} %get-tuple-element.13.before_ref, f32[2,2,4,256]{3,2,1,0:T(4,128)S(1)} %collective-permute-done.1.near_x_ref, f32[2,2,4,256]{3,2,1,0:T(4,128)S(1)} %collective-permute-done.2.far_x_ref), custom_call_target="tpu_custom_call" | custom-call | flops 1572864000 | bytes 262144 | tf_op jit(solution)/shard_map/pallas_call | solution.py:263
  17.0 0.0 copy-start.1
  17.0 0.0 collective-permute-done.3.source_ref
  17.0 0.0 copy-done.2
  17.0 1.2 %shard_map.62.bin_ref = f32[2,4,256]{2,1,0:T(4,128)S(1)} custom-call(f32[3,1,1,2,256]{4,3,2,1,0:T(2,128)S(1)} %copy-done.2, f32[2,4,256]{2,1,0:T(4,128)S(1)} %copy-done, bf16[2,256,48]{2,1,0:T(8,128)(2,1)S(1)} %get-tuple-element.12.target_ref, f32[2,256,32]{2,1,0:T(8,128)S(1)} %shard_map.61.before_ref, f32[3,2,4,256]{3,2,1,0:T(4,128)S(1)} %collective-permute-done.3.source_ref), custom_call_target="tpu_custom_call" | custom-call | flops 589824000 | bytes 262144 | tf_op jit(solution)/shard_map/pallas_call | solution.py:263
  18.2 0.0 collective-permute-done.4.source_ref
  18.2 0.0 copy-done.1
  18.2 1.2 %shard_map.63 = (f32[2,4,256]{2,1,0:T(4,128)S(1)}, f32[2,4,256]{2,1,0:T(4,128)S(1)}) custom-call(f32[2,4,256]{2,1,0:T(4,128)S(1)} %copy-done.1, f32[2,4,256]{2,1,0:T(4,128)S(1)} %shard_map.62.bin_ref, f32[3,1,1,2,256]{4,3,2,1,0:T(2,128)S(1)} %copy-done.2, f32[2,4,256]{2,1,0:T(4,128)S(1)} %copy-done, bf16[2,256,48]{2,1,0:T(8,128)(2,1)S(1)} %get-tuple-element.12.target_ref, ...), custom_call_target="tpu_custom_call" | custom-call | flops 589824000 | bytes 262144 | tf_op jit(solution)/shard_map/pallas_call | solution.py:263
  19.4 1.6 %collective-permute-start.5 = (f32[2,4,256]{2,1,0:T(4,128)S(1)}, f32[2,4,256]{2,1,0:T(4,128)S(1)}, u32[]{:S(2)}, u32[]{:S(2)}) collective-permute-start(f32[2,4,256]{2,1,0:T(4,128)S(1)} %get-tuple-element.15.refs_0_.own_ref), channel_id=1, source_target_pairs={{0,4},{4,0},{1,5},{5,1},{2,6},{6,2},{3,7},{7,3},{8,12},{12,8},{9,1... | collective-permute-start | bytes 24584 | tf_op jit(solution)/shard_map/ppermute | solution.py:300
  21.0 2.1 %collective-permute-done.5.refs_1_ = f32[2,4,256]{2,1,0:T(4,128)S(1)} collective-permute-done((f32[2,4,256]{2,1,0:T(4,128)S(1)}, f32[2,4,256]{2,1,0:T(4,128)S(1)}, u32[]{:S(2)}, u32[]{:S(2)}) %collective-permute-start.5) | collective-permute-done | bytes 8224 | tf_op jit(solution)/shard_map/ppermute | solution.py:300
  23.1 0.1 collective-permute-start.6
  23.2 1.6 %collective-permute-start.7 = (f32[2,2,4,256]{3,2,1,0:T(4,128)S(1)}, f32[2,2,4,256]{3,2,1,0:T(4,128)S(1)}, u32[]{:S(2)}, u32[]{:S(2)}) collective-permute-start(f32[2,2,4,256]{3,2,1,0:T(4,128)S(1)} %get-tuple-element.23), channel_id=1, source_target_pairs={{0,24},{8,16},{16,8},{24,0},{1,25},{9,17},{17,9},{25,1},{2,26},{10... | collective-permute-start | bytes 49160 | tf_op jit(solution)/shard_map/ppermute | solution.py:304
  24.8 1.4 %shard_map.64 = (bf16[2,256,48]{2,1,0:T(8,128)(2,1)S(1)}, f32[2,256,32]{2,1,0:T(8,128)S(1)}) custom-call(f32[2,4,256]{2,1,0:T(4,128)S(1)} %get-tuple-element.15.refs_0_.own_ref, f32[2,4,256]{2,1,0:T(4,128)S(1)} %collective-permute-done.5.refs_1_), custom_call_target="tpu_custom_call" | custom-call | flops 786432000 | bytes 262144 | tf_op jit(solution)/shard_map/pallas_call | solution.py:263
  26.2 0.0 collective-permute-done.6.near_x_ref
  26.2 0.2 collective-permute-done.7.far_x_ref
  26.5 0.8 %collective-permute-start.8 = (f32[3,2,4,256]{3,2,1,0:T(4,128)S(1)}, f32[3,2,4,256]{3,2,1,0:T(4,128)S(1)}, u32[]{:S(2)}, u32[]{:S(2)}) collective-permute-start(f32[3,2,4,256]{3,2,1,0:T(4,128)S(1)} %get-tuple-element.19), channel_id=1, source_target_pairs={{0,1},{1,0},{2,3},{3,2},{4,5},{5,4},{6,7},{7,6},{8,9},{9,8},{10,11... | collective-permute-start | bytes 73736 | tf_op jit(solution)/shard_map/ppermute | solution.py:314
  27.2 1.6 %collective-permute-start.9 = (f32[3,2,4,256]{3,2,1,0:T(4,128)S(1)}, f32[3,2,4,256]{3,2,1,0:T(4,128)S(1)}, u32[]{:S(2)}, u32[]{:S(2)}) collective-permute-start(f32[3,2,4,256]{3,2,1,0:T(4,128)S(1)} %get-tuple-element.18), channel_id=1, source_target_pairs={{0,3},{1,2},{2,1},{3,0},{4,7},{5,6},{6,5},{7,4},{8,11},{9,10},{10,... | collective-permute-start | bytes 73736 | tf_op jit(solution)/shard_map/ppermute | solution.py:313
  28.8 2.2 %shard_map.65.before_ref = f32[2,256,32]{2,1,0:T(8,128)S(1)} custom-call(bf16[2,256,48]{2,1,0:T(8,128)(2,1)S(1)} %get-tuple-element.16.target_ref, f32[2,256,32]{2,1,0:T(8,128)S(1)} %get-tuple-element.17.before_ref, f32[2,2,4,256]{3,2,1,0:T(4,128)S(1)} %collective-permute-done.6.near_x_ref, f32[2,2,4,256]{3,2,1,0:T(4,128)S(1)} %collective-permute-done.7.far_x_ref), custom_call_target="tpu_custom_call" | custom-call | flops 1572864000 | bytes 262144 | tf_op jit(solution)/shard_map/pallas_call | solution.py:263
  31.0 0.0 collective-permute-done.8.source_ref
  31.0 1.2 %shard_map.66.bin_ref = f32[2,4,256]{2,1,0:T(4,128)S(1)} custom-call(f32[2,4,256]{2,1,0:T(4,128)S(1)} %get-tuple-element.14.speed_ref, f32[2,4,256]{2,1,0:T(4,128)S(1)} %get-tuple-element.15.refs_0_.own_ref, bf16[2,256,48]{2,1,0:T(8,128)(2,1)S(1)} %get-tuple-element.16.target_ref, f32[2,256,32]{2,1,0:T(8,128)S(1)} %shard_map.65.before_ref, ...), custom_call_target="tpu_custom_call" | custom-call | flops 589824000 | bytes 262144 | tf_op jit(solution)/shard_map/pallas_call | solution.py:263
  32.2 0.7 %collective-permute-done.9.source_ref = f32[3,2,4,256]{3,2,1,0:T(4,128)S(1)} collective-permute-done((f32[3,2,4,256]{3,2,1,0:T(4,128)S(1)}, f32[3,2,4,256]{3,2,1,0:T(4,128)S(1)}, u32[]{:S(2)}, u32[]{:S(2)}) %collective-permute-start.9) | collective-permute-done | bytes 24608 | tf_op jit(solution)/shard_map/ppermute | solution.py:313
  32.8 1.8 %shard_map.67 = (f32[3,1,1,2,256]{4,3,2,1,0:T(2,128)}, f32[3,1,1,2,256]{4,3,2,1,0:T(2,128)}) custom-call(f32[2,4,256]{2,1,0:T(4,128)S(1)} %copy-done.1, f32[2,4,256]{2,1,0:T(4,128)S(1)} %shard_map.66.bin_ref, f32[2,4,256]{2,1,0:T(4,128)S(1)} %get-tuple-element.14.speed_ref, f32[2,4,256]{2,1,0:T(4,128)S(1)} %get-tuple-element.15.refs_0_.own_ref, ...), custom_call_target="tpu_custom_call" | custom-call | flops 589824000 | bytes 262144 | tf_op jit(solution)/shard_map/pallas_call | solution.py:263
  (6 shorter events, 0.1 us)
Async XLA Ops:
  2.0 4.8 %collective-permute-start = (f32[2,4,256]{2,1,0:T(4,128)}, f32[2,4,256]{2,1,0:T(4,128)S(1)}, u32[]{:S(2)}, u32[]{:S(2)}) collective-permute-start(f32[2,4,256]{2,1,0:T(4,128)} %get-tuple-element.11.refs_0_.own_ref), channel_id=1, source_target_pairs={{0,4},{4,0},{1,5},{5,1},{2,6},{6,2},{3,7},{7,3},{8,12},{12,8},{9,1... | collective-permute-start | bytes 24584 | tf_op jit(solution)/shard_map/ppermute | solution.py:300
  5.0 1.8 %copy-start = (f32[2,4,256]{2,1,0:T(4,128)S(1)}, f32[2,4,256]{2,1,0:T(4,128)}, u32[]{:S(2)}) copy-start(f32[2,4,256]{2,1,0:T(4,128)} %get-tuple-element.11.refs_0_.own_ref) | copy-start | bytes 24580
  6.8 3.6 %collective-permute-start.1 = (f32[2,2,4,256]{3,2,1,0:T(4,128)S(1)}, f32[2,2,4,256]{3,2,1,0:T(4,128)S(1)}, u32[]{:S(2)}, u32[]{:S(2)}) collective-permute-start(f32[2,2,4,256]{3,2,1,0:T(4,128)S(1)} %get-tuple-element.25), channel_id=1, source_target_pairs={{0,8},{8,0},{16,24},{24,16},{1,9},{9,1},{17,25},{25,17},{2,10},{10... | collective-permute-start | bytes 49160 | tf_op jit(solution)/shard_map/ppermute | solution.py:303
  6.9 3.6 %collective-permute-start.2 = (f32[2,2,4,256]{3,2,1,0:T(4,128)S(1)}, f32[2,2,4,256]{3,2,1,0:T(4,128)S(1)}, u32[]{:S(2)}, u32[]{:S(2)}) collective-permute-start(f32[2,2,4,256]{3,2,1,0:T(4,128)S(1)} %get-tuple-element.25), channel_id=1, source_target_pairs={{0,24},{8,16},{16,8},{24,0},{1,25},{9,17},{17,9},{25,1},{2,26},{10... | collective-permute-start | bytes 49160 | tf_op jit(solution)/shard_map/ppermute | solution.py:304
  10.5 6.5 %collective-permute-start.3 = (f32[3,2,4,256]{3,2,1,0:T(4,128)S(1)}, f32[3,2,4,256]{3,2,1,0:T(4,128)S(1)}, u32[]{:S(2)}, u32[]{:S(2)}) collective-permute-start(f32[3,2,4,256]{3,2,1,0:T(4,128)S(1)} %get-tuple-element.21), channel_id=1, source_target_pairs={{0,1},{1,0},{2,3},{3,2},{4,5},{5,4},{6,7},{7,6},{8,9},{9,8},{10,11... | collective-permute-start | bytes 73736 | tf_op jit(solution)/shard_map/ppermute | solution.py:314
  12.3 5.9 %collective-permute-start.4 = (f32[3,2,4,256]{3,2,1,0:T(4,128)S(1)}, f32[3,2,4,256]{3,2,1,0:T(4,128)S(1)}, u32[]{:S(2)}, u32[]{:S(2)}) collective-permute-start(f32[3,2,4,256]{3,2,1,0:T(4,128)S(1)} %get-tuple-element.20), channel_id=1, source_target_pairs={{0,3},{1,2},{2,1},{3,0},{4,7},{5,6},{6,5},{7,4},{8,11},{9,10},{10,... | collective-permute-start | bytes 73736 | tf_op jit(solution)/shard_map/ppermute | solution.py:313
  14.8 2.2 %copy-start.2 = (f32[3,1,1,2,256]{4,3,2,1,0:T(2,128)S(1)}, f32[3,1,1,2,256]{4,3,2,1,0:T(2,128)}, u32[]{:S(2)}) copy-start(f32[3,1,1,2,256]{4,3,2,1,0:T(2,128)} %speed_ref.3) | copy-start | bytes 18436
  17.0 1.2 %copy-start.1 = (f32[2,4,256]{2,1,0:T(4,128)S(1)}, f32[2,4,256]{2,1,0:T(4,128)}, u32[]{:S(2)}) copy-start(f32[2,4,256]{2,1,0:T(4,128)} %get-tuple-element.10.keep_ref) | copy-start | bytes 24580
  19.4 3.7 %collective-permute-start.5 = (f32[2,4,256]{2,1,0:T(4,128)S(1)}, f32[2,4,256]{2,1,0:T(4,128)S(1)}, u32[]{:S(2)}, u32[]{:S(2)}) collective-permute-start(f32[2,4,256]{2,1,0:T(4,128)S(1)} %get-tuple-element.15.refs_0_.own_ref), channel_id=1, source_target_pairs={{0,4},{4,0},{1,5},{5,1},{2,6},{6,2},{3,7},{7,3},{8,12},{12,8},{9,1... | collective-permute-start | bytes 24584 | tf_op jit(solution)/shard_map/ppermute | solution.py:300
  23.1 3.1 %collective-permute-start.6 = (f32[2,2,4,256]{3,2,1,0:T(4,128)S(1)}, f32[2,2,4,256]{3,2,1,0:T(4,128)S(1)}, u32[]{:S(2)}, u32[]{:S(2)}) collective-permute-start(f32[2,2,4,256]{3,2,1,0:T(4,128)S(1)} %get-tuple-element.23), channel_id=1, source_target_pairs={{0,8},{8,0},{16,24},{24,16},{1,9},{9,1},{17,25},{25,17},{2,10},{10... | collective-permute-start | bytes 49160 | tf_op jit(solution)/shard_map/ppermute | solution.py:303
  23.2 3.2 %collective-permute-start.7 = (f32[2,2,4,256]{3,2,1,0:T(4,128)S(1)}, f32[2,2,4,256]{3,2,1,0:T(4,128)S(1)}, u32[]{:S(2)}, u32[]{:S(2)}) collective-permute-start(f32[2,2,4,256]{3,2,1,0:T(4,128)S(1)} %get-tuple-element.23), channel_id=1, source_target_pairs={{0,24},{8,16},{16,8},{24,0},{1,25},{9,17},{17,9},{25,1},{2,26},{10... | collective-permute-start | bytes 49160 | tf_op jit(solution)/shard_map/ppermute | solution.py:304
  26.5 4.6 %collective-permute-start.8 = (f32[3,2,4,256]{3,2,1,0:T(4,128)S(1)}, f32[3,2,4,256]{3,2,1,0:T(4,128)S(1)}, u32[]{:S(2)}, u32[]{:S(2)}) collective-permute-start(f32[3,2,4,256]{3,2,1,0:T(4,128)S(1)} %get-tuple-element.19), channel_id=1, source_target_pairs={{0,1},{1,0},{2,3},{3,2},{4,5},{5,4},{6,7},{7,6},{8,9},{9,8},{10,11... | collective-permute-start | bytes 73736 | tf_op jit(solution)/shard_map/ppermute | solution.py:314
  27.2 5.6 %collective-permute-start.9 = (f32[3,2,4,256]{3,2,1,0:T(4,128)S(1)}, f32[3,2,4,256]{3,2,1,0:T(4,128)S(1)}, u32[]{:S(2)}, u32[]{:S(2)}) collective-permute-start(f32[3,2,4,256]{3,2,1,0:T(4,128)S(1)} %get-tuple-element.18), channel_id=1, source_target_pairs={{0,3},{1,2},{2,1},{3,0},{4,7},{5,6},{6,5},{7,4},{8,11},{9,10},{10,... | collective-permute-start | bytes 73736 | tf_op jit(solution)/shard_map/ppermute | solution.py:313

commit v5 on v4

--- a/solution.py
+++ b/solution.py
@@ -180,12 +180,13 @@
         total_ref[z] = totals[z]
 
 
-def slab_kernel(size_y, target_ref, before_ref, near_x_ref, far_x_ref, total_ref, near_ref, sum_ref, list_ref):
+def slab_kernel(size_y, target_ref, before_ref, near_x_ref, *refs):
+    far_refs, (total_ref, near_ref, sum_ref, list_ref) = refs[:-4], refs[-4:]
     entries = []
-    for ref, x in ((near_x_ref, ahead("gx")), (far_x_ref, -ahead("gx"))):
-        for plane, shifts in enumerate(y_shifts(size_y)):
-            for y in shifts:
-                entries += [(ref, (plane, z), (x, y, z)) for z in range(2)]
+    for plane, shifts in enumerate(y_shifts(size_y)):
+        for y in shifts:
+            entries += [(near_x_ref, (plane, z), (ahead("gx"), y, z)) for z in range(2)]
+            entries += [(far_refs[plane], z, (-ahead("gx"), y, z)) for z in range(2)]
     length = fill(near_ref, sum_ref, list_ref, entries)
     targets = [target_ref[z] for z in range(2)]
     totals = sums_over(targets, (before_ref[0], before_ref[1]), near_ref, sum_ref, list_ref, length, len(entries), 9)
@@ -197,7 +198,8 @@
     entries = []
     for column, x in enumerate((0, ahead("gx"), -ahead("gx"))):
         for plane, shifts in enumerate(y_shifts(size_y)):
-            entries += [(source_ref, (column, plane), (x, y, 3 * z - 1)) for y in shifts]
+            index = column * len(y_shifts(size_y)) + plane
+            entries += [(source_ref, index, (x, y, 3 * z - 1)) for y in shifts]
     length = fill(near_ref, sum_ref, list_ref, entries)
     (total,) = sums_over([target_ref[z]], (before_ref[z],), near_ref, sum_ref, list_ref, length, len(entries), 7)
     total = total.T
@@ -257,6 +259,12 @@
     return near, far
 
 
+def across(value, path_x, path_y):
+    size_y = lax.axis_size("gy")
+    pairs = [(x * size_y + y, to_x * size_y + to_y) for x, to_x in path_x for y, to_y in path_y]
+    return lax.ppermute(value, ("gx", "gy"), pairs)
+
+
 def call(kernel, inputs, outputs, sources, targets, slots, chunks):
     half = slots // 2
     heads = sources // 2 * 2
@@ -291,30 +299,25 @@
     upper = lax.rem(lax.axis_index("gz"), 2)
     for subcycle in range(SUBCYCLES):
         first, last = subcycle == 0, subcycle == SUBCYCLES - 1
-        near, far = swaps("gy")
-        planes = [packed]
-        if size_y > 2:
-            other = lax.ppermute(packed, "gy", far)
-            planes += [lax.ppermute(packed, "gy", near), other]
-        else:
-            planes.append(lax.ppermute(packed, "gy", near))
+        paths = swaps("gy")[: min(size_y, 3) - 1]
+        planes = [packed] + [lax.ppermute(packed, "gy", path) for path in paths]
+        near, far = swaps("gx")
+        far_planes = [lax.ppermute(packed, "gx", far)] + [across(packed, far, path) for path in paths]
         plane = jnp.stack(planes)
-        near, far = swaps("gx")
         near_x = lax.ppermute(plane, "gx", near)
-        far_x = lax.ppermute(plane, "gx", far)
         targets, total = call(
             functools.partial(plane_kernel, size_y),
             planes,
             (jax.ShapeDtypeStruct((2, slots, 48), BF16), running),
             6, 2, slots, 2,
         )
-        slab = jnp.stack([plane, near_x, far_x])
+        slab = jnp.concatenate([plane, near_x] + [value[None] for value in far_planes], axis=0)
         near, far = swaps("gz")
-        far_z = lax.ppermute(lax.dynamic_index_in_dim(slab, upper, 2, False), "gz", far)
-        near_z = lax.ppermute(lax.dynamic_index_in_dim(slab, 1 - upper, 2, False), "gz", near)
+        far_z = lax.ppermute(lax.dynamic_index_in_dim(slab, upper, 1, False), "gz", far)
+        near_z = lax.ppermute(lax.dynamic_index_in_dim(slab, 1 - upper, 1, False), "gz", near)
         (total,) = call(
             functools.partial(slab_kernel, size_y),
-            [targets, total, near_x, far_x],
+            [targets, total, near_x] + far_planes,
             (running,),
             12, 2, slots, 3,
         )

time: 34.8 us -> 33.1 us (0.951)
  waiting for transfers between devices: 4.91 us -> 2.72 us
  local copies, waits for them, and re-layouts: 0.04 us -> 1.51 us
  starting transfers between devices: 15.1 us -> 14 us
    ppermute x8 -> x10, waiting for transfers between devices: 4.9 us -> 2.72 us  [the longest x2 1.2 us: across(): return lax.ppermute(value, ('gx', 'gy'), pairs)]
    unnamed x6 -> x14, local copies, waits for them, and re-layouts: 0.01 us -> 1.49 us
    ppermute x8 -> x10, starting transfers between devices: 14.9 us -> 13.5 us  [the longest x2 4.32 us: on_device(): planes = [packed] + [lax.ppermute(packed, 'gy', path) for path in paths]]
  transfers between devices with their start and end apart: 10 -> 12, of which waited for: 4 -> 4; matrix products, arithmetic and copies ran while one was open for 0% -> 2% of each run, Pallas kernels for 27% -> 29%
where the time goes in v5:
time: 33.1 us; the launch traced here: 32.8 us
  starting transfers between devices  14 us (42%)
  Pallas kernels  13.7 us (41%)
  waiting for transfers between devices  2.72 us (8%)
  local copies, waits for them, and re-layouts  1.51 us (5%)
  between operations  0.8 us (2%)
    pallas_call x8, Pallas kernels, call(): pl.pallas_call(kernel, out_shape=outputs, in_specs=[VMEM] * len(inputs),...  12.4 us
    ppermute x2, starting transfers between devices, on_device(): planes = [packed] + [lax.ppermute(packed, 'gy', path) for path in paths]  4.32 us
    ppermute x2, starting transfers between devices, on_device(): lax.ppermute(lax.dynamic_index_in_dim(slab, upper, 1, False), 'gz', far)  3.66 us
    ppermute x2, starting transfers between devices, on_device(): lax.ppermute(lax.dynamic_index_in_dim(slab, 1 - upper, 1, False), 'gz', n...  2.37 us
    ppermute x2, starting transfers between devices, across(): return lax.ppermute(value, ('gx', 'gy'), pairs)  1.74 us
    unnamed x14, local copies, waits for them, and re-layouts  1.49 us
    ppermute x2, starting transfers between devices, on_device(): lax.ppermute(packed, 'gx', far)  1.4 us
    pallas_call x1, Pallas kernels, on_device(): pl.pallas_call(pack_kernel, out_shape=(bins, bins), in_specs=[VMEM] * 3,...  1.39 us
  transfers between devices with their start and end apart: 12, of which 4 were waited for; matrix products, arithmetic and copies ran while one was open for 2% of the time, Pallas kernels for 29%

profile of v5, /device:TPU:0, one launch (start us, length us, event | category | flops | bytes accessed | tf_op | source)
XLA Modules:
  0.0 32.8 jit_solution(13861792580955621664)
XLA Ops:
  0.6 1.4 %shard_map.59 = (f32[2,4,256]{2,1,0:T(4,128)}, f32[2,4,256]{2,1,0:T(4,128)}) custom-call(s32[1,1,2]{2,1,0:T(1,128)} %counts_ref.1, f32[3,1,1,2,256]{4,3,2,1,0:T(2,128)} %place_ref.1, f32[1,1,2,256]{3,2,1,0:T(2,128)} %mass_ref.1), custom_call_target="tpu_custom_call" | custom-call | tf_op jit(solution)/shard_map/pallas_call | solution.py:292
  2.0 3.0 %collective-permute-start = (f32[2,4,256]{2,1,0:T(4,128)}, f32[2,4,256]{2,1,0:T(4,128)S(1)}, u32[]{:S(2)}, u32[]{:S(2)}) collective-permute-start(f32[2,4,256]{2,1,0:T(4,128)} %get-tuple-element.11.refs_0_.own_ref), channel_id=1, source_target_pairs={{0,4},{4,0},{1,5},{5,1},{2,6},{6,2},{3,7},{7,3},{8,12},{12,8},{9,1... | collective-permute-start | bytes 24584 | tf_op jit(solution)/shard_map/ppermute | solution.py:303
  5.0 0.7 %collective-permute-start.2 = (f32[2,4,256]{2,1,0:T(4,128)}, f32[2,4,256]{2,1,0:T(4,128)S(1)}, u32[]{:S(2)}, u32[]{:S(2)}) collective-permute-start(f32[2,4,256]{2,1,0:T(4,128)} %get-tuple-element.11.refs_0_.own_ref), channel_id=1, source_target_pairs={{0,24},{8,16},{16,8},{24,0},{1,25},{9,17},{17,9},{25,1},{2,26},{10... | collective-permute-start | bytes 24584 | tf_op jit(solution)/shard_map/ppermute | solution.py:305
  5.6 0.5 %collective-permute-start.3 = (f32[2,4,256]{2,1,0:T(4,128)}, f32[2,4,256]{2,1,0:T(4,128)S(1)}, u32[]{:S(2)}, u32[]{:S(2)}) collective-permute-start(f32[2,4,256]{2,1,0:T(4,128)} %get-tuple-element.11.refs_0_.own_ref), channel_id=1, source_target_pairs={{0,28},{4,24},{8,20},{12,16},{16,12},{20,8},{24,4},{28,0},{1,29},{... | collective-permute-start | bytes 24584 | tf_op jit(solution)/shard_map/ppermute | solution.py:265
  6.2 0.7 %constant_dynamic-update-slice_fusion.4 = f32[6,2,4,256]{3,2,1,0:T(4,128)S(1)} fusion(f32[2,4,256]{2,1,0:T(4,128)} %get-tuple-element.11.refs_0_.own_ref), kind=kLoop, calls=%fused_computation.8 | loop fusion | bytes 16384
  6.9 0.0 copy-start
  6.9 0.0 collective-permute-done.refs_1_
  6.9 0.7 %copy-done = f32[2,4,256]{2,1,0:T(4,128)S(1)} copy-done((f32[2,4,256]{2,1,0:T(4,128)S(1)}, f32[2,4,256]{2,1,0:T(4,128)}, u32[]{:S(2)}) %copy-start) | copy-done | bytes 8216
  7.6 0.5 %collective-permute-start.1 = (f32[2,2,4,256]{3,2,1,0:T(4,128)S(1)}, f32[2,2,4,256]{3,2,1,0:T(4,128)S(1)}, u32[]{:S(2)}, u32[]{:S(2)}) collective-permute-start(f32[2,2,4,256]{3,2,1,0:T(4,128)S(1)} %pad_maximum_fusion), channel_id=1, source_target_pairs={{0,8},{8,0},{16,24},{24,16},{1,9},{9,1},{17,25},{25,17},{2,10},{10... | collective-permute-start | bytes 49160 | tf_op jit(solution)/shard_map/ppermute | solution.py:307
  8.1 1.4 %shard_map.60 = (bf16[2,256,48]{2,1,0:T(8,128)(2,1)S(1)}, f32[2,256,32]{2,1,0:T(8,128)S(1)}) custom-call(f32[2,4,256]{2,1,0:T(4,128)S(1)} %copy-done, f32[2,4,256]{2,1,0:T(4,128)S(1)} %collective-permute-done.refs_1_), custom_call_target="tpu_custom_call" | custom-call | flops 786432000 | bytes 262144 | tf_op jit(solution)/shard_map/pallas_call | solution.py:271
  9.5 0.0 collective-permute-done.1.near_x_ref
  9.5 0.0 collective-permute-done.2.refs_0_
  9.5 0.3 collective-permute-done.3.refs_1_
  9.8 1.6 %collective-permute-start.4 = (f32[6,4,256]{2,1,0:T(4,128)S(1)}, f32[6,4,256]{2,1,0:T(4,128)S(1)}, u32[]{:S(2)}, u32[]{:S(2)}) collective-permute-start(f32[6,4,256]{2,1,0:T(4,128)S(1)} %get-tuple-element.21), channel_id=1, source_target_pairs={{0,1},{1,0},{2,3},{3,2},{4,5},{5,4},{6,7},{7,6},{8,9},{9,8},{10,11... | collective-permute-start | bytes 73736 | tf_op jit(solution)/shard_map/ppermute | solution.py:317
  11.5 2.5 %collective-permute-start.5 = (f32[6,4,256]{2,1,0:T(4,128)S(1)}, f32[6,4,256]{2,1,0:T(4,128)S(1)}, u32[]{:S(2)}, u32[]{:S(2)}) collective-permute-start(f32[6,4,256]{2,1,0:T(4,128)S(1)} %get-tuple-element.20), channel_id=1, source_target_pairs={{0,3},{1,2},{2,1},{3,0},{4,7},{5,6},{6,5},{7,4},{8,11},{9,10},{10,... | collective-permute-start | bytes 73736 | tf_op jit(solution)/shard_map/ppermute | solution.py:316
  14.0 0.0 copy-start.2
  14.0 2.2 %shard_map.61.before_ref = f32[2,256,32]{2,1,0:T(8,128)S(1)} custom-call(bf16[2,256,48]{2,1,0:T(8,128)(2,1)S(1)} %get-tuple-element.12.target_ref, f32[2,256,32]{2,1,0:T(8,128)S(1)} %get-tuple-element.13.before_ref, f32[2,2,4,256]{3,2,1,0:T(4,128)S(1)} %collective-permute-done.1.near_x_ref, f32[2,4,256]{2,1,0:T(4,128)S(1)} %collective-permute-done.2.refs_0_, ...), custom_call_target="tpu_custom_call" | custom-call | flops 1572864000 | bytes 262144 | tf_op jit(solution)/shard_map/pallas_call | solution.py:271
  16.2 0.0 copy-start.1
  16.2 0.0 collective-permute-done.4.source_ref
  16.2 0.0 copy-done.2
  16.2 1.2 %shard_map.62.bin_ref = f32[2,4,256]{2,1,0:T(4,128)S(1)} custom-call(f32[3,1,1,2,256]{4,3,2,1,0:T(2,128)S(1)} %copy-done.2, f32[2,4,256]{2,1,0:T(4,128)S(1)} %copy-done, bf16[2,256,48]{2,1,0:T(8,128)(2,1)S(1)} %get-tuple-element.12.target_ref, f32[2,256,32]{2,1,0:T(8,128)S(1)} %shard_map.61.before_ref, f32[6,4,256]{2,1,0:T(4,128)S(1)} %collective-permute-done.4.source_ref), custom_call_target="tpu_custom_call" | custom-call | flops 589824000 | bytes 262144 | tf_op jit(solution)/shard_map/pallas_call | solution.py:271
  17.3 0.0 collective-permute-done.5.source_ref
  17.4 0.0 copy-done.1
  17.4 1.2 %shard_map.63 = (f32[2,4,256]{2,1,0:T(4,128)S(1)}, f32[2,4,256]{2,1,0:T(4,128)S(1)}) custom-call(f32[2,4,256]{2,1,0:T(4,128)S(1)} %copy-done.1, f32[2,4,256]{2,1,0:T(4,128)S(1)} %shard_map.62.bin_ref, f32[3,1,1,2,256]{4,3,2,1,0:T(2,128)S(1)} %copy-done.2, f32[2,4,256]{2,1,0:T(4,128)S(1)} %copy-done, bf16[2,256,48]{2,1,0:T(8,128)(2,1)S(1)} %get-tuple-element.12.target_ref, ...), custom_call_target="tpu_custom_call" | custom-call | flops 589824000 | bytes 262144 | tf_op jit(solution)/shard_map/pallas_call | solution.py:271
  18.5 1.4 %collective-permute-start.6 = (f32[2,4,256]{2,1,0:T(4,128)S(1)}, f32[2,4,256]{2,1,0:T(4,128)S(1)}, u32[]{:S(2)}, u32[]{:S(2)}) collective-permute-start(f32[2,4,256]{2,1,0:T(4,128)S(1)} %get-tuple-element.15.refs_0_.own_ref), channel_id=1, source_target_pairs={{0,4},{4,0},{1,5},{5,1},{2,6},{6,2},{3,7},{7,3},{8,12},{12,8},{9,1... | collective-permute-start | bytes 24584 | tf_op jit(solution)/shard_map/ppermute | solution.py:303
  19.9 0.8 %collective-permute-start.8 = (f32[2,4,256]{2,1,0:T(4,128)S(1)}, f32[2,4,256]{2,1,0:T(4,128)S(1)}, u32[]{:S(2)}, u32[]{:S(2)}) collective-permute-start(f32[2,4,256]{2,1,0:T(4,128)S(1)} %get-tuple-element.15.refs_0_.own_ref), channel_id=1, source_target_pairs={{0,24},{8,16},{16,8},{24,0},{1,25},{9,17},{17,9},{25,1},{2,26},{10... | collective-permute-start | bytes 24584 | tf_op jit(solution)/shard_map/ppermute | solution.py:305
  20.7 1.2 %collective-permute-start.9 = (f32[2,4,256]{2,1,0:T(4,128)S(1)}, f32[2,4,256]{2,1,0:T(4,128)S(1)}, u32[]{:S(2)}, u32[]{:S(2)}) collective-permute-start(f32[2,4,256]{2,1,0:T(4,128)S(1)} %get-tuple-element.15.refs_0_.own_ref), channel_id=1, source_target_pairs={{0,28},{4,24},{8,20},{12,16},{16,12},{20,8},{24,4},{28,0},{1,29},{... | collective-permute-start | bytes 24584 | tf_op jit(solution)/shard_map/ppermute | solution.py:265
  21.9 0.4 %collective-permute-done.6.refs_1_ = f32[2,4,256]{2,1,0:T(4,128)S(1)} collective-permute-done((f32[2,4,256]{2,1,0:T(4,128)S(1)}, f32[2,4,256]{2,1,0:T(4,128)S(1)}, u32[]{:S(2)}, u32[]{:S(2)}) %collective-permute-start.6) | collective-permute-done | bytes 8224 | tf_op jit(solution)/shard_map/ppermute | solution.py:303
  22.3 0.0 collective-permute-start.7
  22.3 1.4 %shard_map.64 = (bf16[2,256,48]{2,1,0:T(8,128)(2,1)S(1)}, f32[2,256,32]{2,1,0:T(8,128)S(1)}) custom-call(f32[2,4,256]{2,1,0:T(4,128)S(1)} %get-tuple-element.15.refs_0_.own_ref, f32[2,4,256]{2,1,0:T(4,128)S(1)} %collective-permute-done.6.refs_1_), custom_call_target="tpu_custom_call" | custom-call | flops 786432000 | bytes 262144 | tf_op jit(solution)/shard_map/pallas_call | solution.py:271
  23.7 0.0 collective-permute-done.7.near_x_ref
  23.7 0.0 collective-permute-done.8.refs_0_
  23.7 0.9 %collective-permute-done.9.refs_1_ = f32[2,4,256]{2,1,0:T(4,128)S(1)} collective-permute-done((f32[2,4,256]{2,1,0:T(4,128)S(1)}, f32[2,4,256]{2,1,0:T(4,128)S(1)}, u32[]{:S(2)}, u32[]{:S(2)}) %collective-permute-start.9) | collective-permute-done | bytes 8224 | tf_op jit(solution)/shard_map/ppermute | solution.py:265
  24.6 0.7 %collective-permute-start.10 = (f32[6,4,256]{2,1,0:T(4,128)S(1)}, f32[6,4,256]{2,1,0:T(4,128)S(1)}, u32[]{:S(2)}, u32[]{:S(2)}) collective-permute-start(f32[6,4,256]{2,1,0:T(4,128)S(1)} %get-tuple-element.19), channel_id=1, source_target_pairs={{0,1},{1,0},{2,3},{3,2},{4,5},{5,4},{6,7},{7,6},{8,9},{9,8},{10,11... | collective-permute-start | bytes 73736 | tf_op jit(solution)/shard_map/ppermute | solution.py:317
  25.4 1.2 %collective-permute-start.11 = (f32[6,4,256]{2,1,0:T(4,128)S(1)}, f32[6,4,256]{2,1,0:T(4,128)S(1)}, u32[]{:S(2)}, u32[]{:S(2)}) collective-permute-start(f32[6,4,256]{2,1,0:T(4,128)S(1)} %get-tuple-element.18), channel_id=1, source_target_pairs={{0,3},{1,2},{2,1},{3,0},{4,7},{5,6},{6,5},{7,4},{8,11},{9,10},{10,... | collective-permute-start | bytes 73736 | tf_op jit(solution)/shard_map/ppermute | solution.py:316
  26.6 2.2 %shard_map.65.before_ref = f32[2,256,32]{2,1,0:T(8,128)S(1)} custom-call(bf16[2,256,48]{2,1,0:T(8,128)(2,1)S(1)} %get-tuple-element.16.target_ref, f32[2,256,32]{2,1,0:T(8,128)S(1)} %get-tuple-element.17.before_ref, f32[2,2,4,256]{3,2,1,0:T(4,128)S(1)} %collective-permute-done.7.near_x_ref, f32[2,4,256]{2,1,0:T(4,128)S(1)} %collective-permute-done.8.refs_0_, ...), custom_call_target="tpu_custom_call" | custom-call | flops 1572864000 | bytes 262144 | tf_op jit(solution)/shard_map/pallas_call | solution.py:271
  28.8 0.0 collective-permute-done.10.source_ref
  28.8 1.2 %shard_map.66.bin_ref = f32[2,4,256]{2,1,0:T(4,128)S(1)} custom-call(f32[2,4,256]{2,1,0:T(4,128)S(1)} %get-tuple-element.14.speed_ref, f32[2,4,256]{2,1,0:T(4,128)S(1)} %get-tuple-element.15.refs_0_.own_ref, bf16[2,256,48]{2,1,0:T(8,128)(2,1)S(1)} %get-tuple-element.16.target_ref, f32[2,256,32]{2,1,0:T(8,128)S(1)} %shard_map.65.before_ref, ...), custom_call_target="tpu_custom_call" | custom-call | flops 589824000 | bytes 262144 | tf_op jit(solution)/shard_map/pallas_call | solution.py:271
  29.9 1.1 %collective-permute-done.11.source_ref = f32[6,4,256]{2,1,0:T(4,128)S(1)} collective-permute-done((f32[6,4,256]{2,1,0:T(4,128)S(1)}, f32[6,4,256]{2,1,0:T(4,128)S(1)}, u32[]{:S(2)}, u32[]{:S(2)}) %collective-permute-start.11) | collective-permute-done | bytes 24608 | tf_op jit(solution)/shard_map/ppermute | solution.py:316
  31.0 1.8 %shard_map.67 = (f32[3,1,1,2,256]{4,3,2,1,0:T(2,128)}, f32[3,1,1,2,256]{4,3,2,1,0:T(2,128)}) custom-call(f32[2,4,256]{2,1,0:T(4,128)S(1)} %copy-done.1, f32[2,4,256]{2,1,0:T(4,128)S(1)} %shard_map.66.bin_ref, f32[2,4,256]{2,1,0:T(4,128)S(1)} %get-tuple-element.14.speed_ref, f32[2,4,256]{2,1,0:T(4,128)S(1)} %get-tuple-element.15.refs_0_.own_ref, ...), custom_call_target="tpu_custom_call" | custom-call | flops 589824000 | bytes 262144 | tf_op jit(solution)/shard_map/pallas_call | solution.py:271
  (13 shorter events, 0.1 us)
Async XLA Ops:
  2.0 4.9 %collective-permute-start = (f32[2,4,256]{2,1,0:T(4,128)}, f32[2,4,256]{2,1,0:T(4,128)S(1)}, u32[]{:S(2)}, u32[]{:S(2)}) collective-permute-start(f32[2,4,256]{2,1,0:T(4,128)} %get-tuple-element.11.refs_0_.own_ref), channel_id=1, source_target_pairs={{0,4},{4,0},{1,5},{5,1},{2,6},{6,2},{3,7},{7,3},{8,12},{12,8},{9,1... | collective-permute-start | bytes 24584 | tf_op jit(solution)/shard_map/ppermute | solution.py:303
  5.0 4.5 %collective-permute-start.2 = (f32[2,4,256]{2,1,0:T(4,128)}, f32[2,4,256]{2,1,0:T(4,128)S(1)}, u32[]{:S(2)}, u32[]{:S(2)}) collective-permute-start(f32[2,4,256]{2,1,0:T(4,128)} %get-tuple-element.11.refs_0_.own_ref), channel_id=1, source_target_pairs={{0,24},{8,16},{16,8},{24,0},{1,25},{9,17},{17,9},{25,1},{2,26},{10... | collective-permute-start | bytes 24584 | tf_op jit(solution)/shard_map/ppermute | solution.py:305
  5.6 4.2 %collective-permute-start.3 = (f32[2,4,256]{2,1,0:T(4,128)}, f32[2,4,256]{2,1,0:T(4,128)S(1)}, u32[]{:S(2)}, u32[]{:S(2)}) collective-permute-start(f32[2,4,256]{2,1,0:T(4,128)} %get-tuple-element.11.refs_0_.own_ref), channel_id=1, source_target_pairs={{0,28},{4,24},{8,20},{12,16},{16,12},{20,8},{24,4},{28,0},{1,29},{... | collective-permute-start | bytes 24584 | tf_op jit(solution)/shard_map/ppermute | solution.py:265
  6.9 0.7 %copy-start = (f32[2,4,256]{2,1,0:T(4,128)S(1)}, f32[2,4,256]{2,1,0:T(4,128)}, u32[]{:S(2)}) copy-start(f32[2,4,256]{2,1,0:T(4,128)} %get-tuple-element.11.refs_0_.own_ref) | copy-start | bytes 24580
  7.6 1.9 %collective-permute-start.1 = (f32[2,2,4,256]{3,2,1,0:T(4,128)S(1)}, f32[2,2,4,256]{3,2,1,0:T(4,128)S(1)}, u32[]{:S(2)}, u32[]{:S(2)}) collective-permute-start(f32[2,2,4,256]{3,2,1,0:T(4,128)S(1)} %pad_maximum_fusion), channel_id=1, source_target_pairs={{0,8},{8,0},{16,24},{24,16},{1,9},{9,1},{17,25},{25,17},{2,10},{10... | collective-permute-start | bytes 49160 | tf_op jit(solution)/shard_map/ppermute | solution.py:307
  9.8 6.3 %collective-permute-start.4 = (f32[6,4,256]{2,1,0:T(4,128)S(1)}, f32[6,4,256]{2,1,0:T(4,128)S(1)}, u32[]{:S(2)}, u32[]{:S(2)}) collective-permute-start(f32[6,4,256]{2,1,0:T(4,128)S(1)} %get-tuple-element.21), channel_id=1, source_target_pairs={{0,1},{1,0},{2,3},{3,2},{4,5},{5,4},{6,7},{7,6},{8,9},{9,8},{10,11... | collective-permute-start | bytes 73736 | tf_op jit(solution)/shard_map/ppermute | solution.py:317
  11.5 5.9 %collective-permute-start.5 = (f32[6,4,256]{2,1,0:T(4,128)S(1)}, f32[6,4,256]{2,1,0:T(4,128)S(1)}, u32[]{:S(2)}, u32[]{:S(2)}) collective-permute-start(f32[6,4,256]{2,1,0:T(4,128)S(1)} %get-tuple-element.20), channel_id=1, source_target_pairs={{0,3},{1,2},{2,1},{3,0},{4,7},{5,6},{6,5},{7,4},{8,11},{9,10},{10,... | collective-permute-start | bytes 73736 | tf_op jit(solution)/shard_map/ppermute | solution.py:316
  14.0 2.2 %copy-start.2 = (f32[3,1,1,2,256]{4,3,2,1,0:T(2,128)S(1)}, f32[3,1,1,2,256]{4,3,2,1,0:T(2,128)}, u32[]{:S(2)}) copy-start(f32[3,1,1,2,256]{4,3,2,1,0:T(2,128)} %speed_ref.3) | copy-start | bytes 18436
  16.2 1.2 %copy-start.1 = (f32[2,4,256]{2,1,0:T(4,128)S(1)}, f32[2,4,256]{2,1,0:T(4,128)}, u32[]{:S(2)}) copy-start(f32[2,4,256]{2,1,0:T(4,128)} %get-tuple-element.10.keep_ref) | copy-start | bytes 24580
  18.5 3.7 %collective-permute-start.6 = (f32[2,4,256]{2,1,0:T(4,128)S(1)}, f32[2,4,256]{2,1,0:T(4,128)S(1)}, u32[]{:S(2)}, u32[]{:S(2)}) collective-permute-start(f32[2,4,256]{2,1,0:T(4,128)S(1)} %get-tuple-element.15.refs_0_.own_ref), channel_id=1, source_target_pairs={{0,4},{4,0},{1,5},{5,1},{2,6},{6,2},{3,7},{7,3},{8,12},{12,8},{9,1... | collective-permute-start | bytes 24584 | tf_op jit(solution)/shard_map/ppermute | solution.py:303
  19.9 3.8 %collective-permute-start.8 = (f32[2,4,256]{2,1,0:T(4,128)S(1)}, f32[2,4,256]{2,1,0:T(4,128)S(1)}, u32[]{:S(2)}, u32[]{:S(2)}) collective-permute-start(f32[2,4,256]{2,1,0:T(4,128)S(1)} %get-tuple-element.15.refs_0_.own_ref), channel_id=1, source_target_pairs={{0,24},{8,16},{16,8},{24,0},{1,25},{9,17},{17,9},{25,1},{2,26},{10... | collective-permute-start | bytes 24584 | tf_op jit(solution)/shard_map/ppermute | solution.py:305
  20.7 4.0 %collective-permute-start.9 = (f32[2,4,256]{2,1,0:T(4,128)S(1)}, f32[2,4,256]{2,1,0:T(4,128)S(1)}, u32[]{:S(2)}, u32[]{:S(2)}) collective-permute-start(f32[2,4,256]{2,1,0:T(4,128)S(1)} %get-tuple-element.15.refs_0_.own_ref), channel_id=1, source_target_pairs={{0,28},{4,24},{8,20},{12,16},{16,12},{20,8},{24,4},{28,0},{1,29},{... | collective-permute-start | bytes 24584 | tf_op jit(solution)/shard_map/ppermute | solution.py:265
  22.3 1.4 %collective-permute-start.7 = (f32[2,2,4,256]{3,2,1,0:T(4,128)S(1)}, f32[2,2,4,256]{3,2,1,0:T(4,128)S(1)}, u32[]{:S(2)}, u32[]{:S(2)}) collective-permute-start(f32[2,2,4,256]{3,2,1,0:T(4,128)S(1)} %pad_maximum_fusion.1), channel_id=1, source_target_pairs={{0,8},{8,0},{16,24},{24,16},{1,9},{9,1},{17,25},{25,17},{2,10},{10... | collective-permute-start | bytes 49160 | tf_op jit(solution)/shard_map/ppermute | solution.py:307
  24.6 4.1 %collective-permute-start.10 = (f32[6,4,256]{2,1,0:T(4,128)S(1)}, f32[6,4,256]{2,1,0:T(4,128)S(1)}, u32[]{:S(2)}, u32[]{:S(2)}) collective-permute-start(f32[6,4,256]{2,1,0:T(4,128)S(1)} %get-tuple-element.19), channel_id=1, source_target_pairs={{0,1},{1,0},{2,3},{3,2},{4,5},{5,4},{6,7},{7,6},{8,9},{9,8},{10,11... | collective-permute-start | bytes 73736 | tf_op jit(solution)/shard_map/ppermute | solution.py:317
  25.4 5.6 %collective-permute-start.11 = (f32[6,4,256]{2,1,0:T(4,128)S(1)}, f32[6,4,256]{2,1,0:T(4,128)S(1)}, u32[]{:S(2)}, u32[]{:S(2)}) collective-permute-start(f32[6,4,256]{2,1,0:T(4,128)S(1)} %get-tuple-element.18), channel_id=1, source_target_pairs={{0,3},{1,2},{2,1},{3,0},{4,7},{5,6},{6,5},{7,4},{8,11},{9,10},{10,... | collective-permute-start | bytes 73736 | tf_op jit(solution)/shard_map/ppermute | solution.py:316

commit v6 on v5

--- a/solution.py
+++ b/solution.py
@@ -186,7 +186,7 @@
     for plane, shifts in enumerate(y_shifts(size_y)):
         for y in shifts:
             entries += [(near_x_ref, (plane, z), (ahead("gx"), y, z)) for z in range(2)]
-            entries += [(far_refs[plane], z, (-ahead("gx"), y, z)) for z in range(2)]
+            entries += [(far_refs[plane - 1], z, (-ahead("gx"), y, z)) for z in range(2)]
     length = fill(near_ref, sum_ref, list_ref, entries)
     targets = [target_ref[z] for z in range(2)]
     totals = sums_over(targets, (before_ref[0], before_ref[1]), near_ref, sum_ref, list_ref, length, len(entries), 9)
@@ -198,7 +198,8 @@
     entries = []
     for column, x in enumerate((0, ahead("gx"), -ahead("gx"))):
         for plane, shifts in enumerate(y_shifts(size_y)):
-            index = column * len(y_shifts(size_y)) + plane
+            planes = len(y_shifts(size_y))
+            index = column * planes + (plane if column < 2 else (plane - 1) % planes)
             entries += [(source_ref, index, (x, y, 3 * z - 1)) for y in shifts]
     length = fill(near_ref, sum_ref, list_ref, entries)
     (total,) = sums_over([target_ref[z]], (before_ref[z],), near_ref, sum_ref, list_ref, length, len(entries), 7)
@@ -302,7 +303,7 @@
         paths = swaps("gy")[: min(size_y, 3) - 1]
         planes = [packed] + [lax.ppermute(packed, "gy", path) for path in paths]
         near, far = swaps("gx")
-        far_planes = [lax.ppermute(packed, "gx", far)] + [across(packed, far, path) for path in paths]
+        far_planes = [across(packed, far, path) for path in paths] + [lax.ppermute(packed, "gx", far)]
         plane = jnp.stack(planes)
         near_x = lax.ppermute(plane, "gx", near)
         targets, total = call(

time: 33.1 us -> 32.3 us (0.976)
  waiting for transfers between devices: 2.72 us -> 1.52 us
  starting transfers between devices: 14 us -> 14.4 us
    ppermute x2, waiting for transfers between devices: 1.2 us -> 0.42 us  [across(): return lax.ppermute(value, ('gx', 'gy'), pairs)]
    ppermute x2, starting transfers between devices: 1.74 us -> 1.29 us  [across(): return lax.ppermute(value, ('gx', 'gy'), pairs)]
    ppermute x2, waiting for transfers between devices: 1.08 us -> 0.65 us  [on_device(): lax.ppermute(lax.dynamic_index_in_dim(slab, upper, 1, False), 'gz', far)]
    ppermute x2, starting transfers between devices: 3.66 us -> 4.08 us  [on_device(): lax.ppermute(lax.dynamic_index_in_dim(slab, upper, 1, False), 'gz', far)]
  transfers between devices with their start and end apart: 12 -> 12, of which waited for: 4 -> 3; matrix products, arithmetic and copies ran while one was open for 2% -> 2% of each run, Pallas kernels for 29% -> 29%
where the time goes in v6:
time: 32.3 us; the launch traced here: 32 us
  starting transfers between devices  14.4 us (45%)
  Pallas kernels  13.8 us (43%)
  local copies, waits for them, and re-layouts  1.52 us (5%)
  waiting for transfers between devices  1.52 us (5%)
  between operations  0.82 us (3%)
    pallas_call x8, Pallas kernels, call(): pl.pallas_call(kernel, out_shape=outputs, in_specs=[VMEM] * len(inputs),...  12.4 us
    ppermute x2, starting transfers between devices, on_device(): planes = [packed] + [lax.ppermute(packed, 'gy', path) for path in paths]  4.56 us
    ppermute x2, starting transfers between devices, on_device(): lax.ppermute(lax.dynamic_index_in_dim(slab, upper, 1, False), 'gz', far)  4.08 us
    ppermute x2, starting transfers between devices, on_device(): lax.ppermute(lax.dynamic_index_in_dim(slab, 1 - upper, 1, False), 'gz', n...  2.46 us
    ppermute x2, starting transfers between devices, on_device(): lax.ppermute(packed, 'gx', far)  1.58 us
    unnamed x14, local copies, waits for them, and re-layouts  1.49 us
    pallas_call x1, Pallas kernels, on_device(): pl.pallas_call(pack_kernel, out_shape=(bins, bins), in_specs=[VMEM] * 3,...  1.39 us
    ppermute x2, starting transfers between devices, across(): return lax.ppermute(value, ('gx', 'gy'), pairs)  1.29 us
  transfers between devices with their start and end apart: 12, of which 3 were waited for; matrix products, arithmetic and copies ran while one was open for 2% of the time, Pallas kernels for 29%

profile of v6, /device:TPU:0, one launch (start us, length us, event | category | flops | bytes accessed | tf_op | source)
XLA Modules:
  0.0 32.0 jit_solution(12604678752149675854)
XLA Ops:
  0.6 1.4 %shard_map.59 = (f32[2,4,256]{2,1,0:T(4,128)}, f32[2,4,256]{2,1,0:T(4,128)}) custom-call(s32[1,1,2]{2,1,0:T(1,128)} %counts_ref.1, f32[3,1,1,2,256]{4,3,2,1,0:T(2,128)} %place_ref.1, f32[1,1,2,256]{3,2,1,0:T(2,128)} %mass_ref.1), custom_call_target="tpu_custom_call" | custom-call | tf_op jit(solution)/shard_map/pallas_call | solution.py:293
  2.0 3.0 %collective-permute-start = (f32[2,4,256]{2,1,0:T(4,128)}, f32[2,4,256]{2,1,0:T(4,128)S(1)}, u32[]{:S(2)}, u32[]{:S(2)}) collective-permute-start(f32[2,4,256]{2,1,0:T(4,128)} %get-tuple-element.11.refs_0_.own_ref), channel_id=1, source_target_pairs={{0,4},{4,0},{1,5},{5,1},{2,6},{6,2},{3,7},{7,3},{8,12},{12,8},{9,1... | collective-permute-start | bytes 24584 | tf_op jit(solution)/shard_map/ppermute | solution.py:304
  5.0 0.6 %collective-permute-start.2 = (f32[2,4,256]{2,1,0:T(4,128)}, f32[2,4,256]{2,1,0:T(4,128)S(1)}, u32[]{:S(2)}, u32[]{:S(2)}) collective-permute-start(f32[2,4,256]{2,1,0:T(4,128)} %get-tuple-element.11.refs_0_.own_ref), channel_id=1, source_target_pairs={{0,28},{4,24},{8,20},{12,16},{16,12},{20,8},{24,4},{28,0},{1,29},{... | collective-permute-start | bytes 24584 | tf_op jit(solution)/shard_map/ppermute | solution.py:266
  5.6 0.6 %collective-permute-start.3 = (f32[2,4,256]{2,1,0:T(4,128)}, f32[2,4,256]{2,1,0:T(4,128)S(1)}, u32[]{:S(2)}, u32[]{:S(2)}) collective-permute-start(f32[2,4,256]{2,1,0:T(4,128)} %get-tuple-element.11.refs_0_.own_ref), channel_id=1, source_target_pairs={{0,24},{8,16},{16,8},{24,0},{1,25},{9,17},{17,9},{25,1},{2,26},{10... | collective-permute-start | bytes 24584 | tf_op jit(solution)/shard_map/ppermute | solution.py:306
  6.2 0.7 %constant_dynamic-update-slice_fusion.4 = f32[6,2,4,256]{3,2,1,0:T(4,128)S(1)} fusion(f32[2,4,256]{2,1,0:T(4,128)} %get-tuple-element.11.refs_0_.own_ref), kind=kLoop, calls=%fused_computation.8 | loop fusion | bytes 16384
  6.9 0.0 copy-start
  6.9 0.0 collective-permute-done.refs_1_
  6.9 0.7 %copy-done = f32[2,4,256]{2,1,0:T(4,128)S(1)} copy-done((f32[2,4,256]{2,1,0:T(4,128)S(1)}, f32[2,4,256]{2,1,0:T(4,128)}, u32[]{:S(2)}) %copy-start) | copy-done | bytes 8216
  7.6 0.4 %collective-permute-start.1 = (f32[2,2,4,256]{3,2,1,0:T(4,128)S(1)}, f32[2,2,4,256]{3,2,1,0:T(4,128)S(1)}, u32[]{:S(2)}, u32[]{:S(2)}) collective-permute-start(f32[2,2,4,256]{3,2,1,0:T(4,128)S(1)} %pad_maximum_fusion), channel_id=1, source_target_pairs={{0,8},{8,0},{16,24},{24,16},{1,9},{9,1},{17,25},{25,17},{2,10},{10... | collective-permute-start | bytes 49160 | tf_op jit(solution)/shard_map/ppermute | solution.py:308
  8.1 1.4 %shard_map.60 = (bf16[2,256,48]{2,1,0:T(8,128)(2,1)S(1)}, f32[2,256,32]{2,1,0:T(8,128)S(1)}) custom-call(f32[2,4,256]{2,1,0:T(4,128)S(1)} %copy-done, f32[2,4,256]{2,1,0:T(4,128)S(1)} %collective-permute-done.refs_1_), custom_call_target="tpu_custom_call" | custom-call | flops 786432000 | bytes 262144 | tf_op jit(solution)/shard_map/pallas_call | solution.py:272
  9.4 0.0 collective-permute-done.1.near_x_ref
  9.5 0.0 collective-permute-done.2.refs_0_
  9.5 0.0 collective-permute-done.3.refs_1_
  9.5 1.7 %collective-permute-start.4 = (f32[6,4,256]{2,1,0:T(4,128)S(1)}, f32[6,4,256]{2,1,0:T(4,128)S(1)}, u32[]{:S(2)}, u32[]{:S(2)}) collective-permute-start(f32[6,4,256]{2,1,0:T(4,128)S(1)} %get-tuple-element.21), channel_id=1, source_target_pairs={{0,1},{1,0},{2,3},{3,2},{4,5},{5,4},{6,7},{7,6},{8,9},{9,8},{10,11... | collective-permute-start | bytes 73736 | tf_op jit(solution)/shard_map/ppermute | solution.py:318
  11.3 2.5 %collective-permute-start.5 = (f32[6,4,256]{2,1,0:T(4,128)S(1)}, f32[6,4,256]{2,1,0:T(4,128)S(1)}, u32[]{:S(2)}, u32[]{:S(2)}) collective-permute-start(f32[6,4,256]{2,1,0:T(4,128)S(1)} %get-tuple-element.20), channel_id=1, source_target_pairs={{0,3},{1,2},{2,1},{3,0},{4,7},{5,6},{6,5},{7,4},{8,11},{9,10},{10,... | collective-permute-start | bytes 73736 | tf_op jit(solution)/shard_map/ppermute | solution.py:317
  13.7 0.0 copy-start.2
  13.7 2.2 %shard_map.61.before_ref = f32[2,256,32]{2,1,0:T(8,128)S(1)} custom-call(bf16[2,256,48]{2,1,0:T(8,128)(2,1)S(1)} %get-tuple-element.12.target_ref, f32[2,256,32]{2,1,0:T(8,128)S(1)} %get-tuple-element.13.before_ref, f32[2,2,4,256]{3,2,1,0:T(4,128)S(1)} %collective-permute-done.1.near_x_ref, f32[2,4,256]{2,1,0:T(4,128)S(1)} %collective-permute-done.2.refs_0_, ...), custom_call_target="tpu_custom_call" | custom-call | flops 1572864000 | bytes 262144 | tf_op jit(solution)/shard_map/pallas_call | solution.py:272
  15.9 0.0 copy-start.1
  15.9 0.0 collective-permute-done.4.source_ref
  15.9 0.0 copy-done.2
  16.0 1.2 %shard_map.62.bin_ref = f32[2,4,256]{2,1,0:T(4,128)S(1)} custom-call(f32[3,1,1,2,256]{4,3,2,1,0:T(2,128)S(1)} %copy-done.2, f32[2,4,256]{2,1,0:T(4,128)S(1)} %copy-done, bf16[2,256,48]{2,1,0:T(8,128)(2,1)S(1)} %get-tuple-element.12.target_ref, f32[2,256,32]{2,1,0:T(8,128)S(1)} %shard_map.61.before_ref, f32[6,4,256]{2,1,0:T(4,128)S(1)} %collective-permute-done.4.source_ref), custom_call_target="tpu_custom_call" | custom-call | flops 589824000 | bytes 262144 | tf_op jit(solution)/shard_map/pallas_call | solution.py:272
  17.1 0.0 collective-permute-done.5.source_ref
  17.1 0.0 copy-done.1
  17.1 1.2 %shard_map.63 = (f32[2,4,256]{2,1,0:T(4,128)S(1)}, f32[2,4,256]{2,1,0:T(4,128)S(1)}) custom-call(f32[2,4,256]{2,1,0:T(4,128)S(1)} %copy-done.1, f32[2,4,256]{2,1,0:T(4,128)S(1)} %shard_map.62.bin_ref, f32[3,1,1,2,256]{4,3,2,1,0:T(2,128)S(1)} %copy-done.2, f32[2,4,256]{2,1,0:T(4,128)S(1)} %copy-done, bf16[2,256,48]{2,1,0:T(8,128)(2,1)S(1)} %get-tuple-element.12.target_ref, ...), custom_call_target="tpu_custom_call" | custom-call | flops 589824000 | bytes 262144 | tf_op jit(solution)/shard_map/pallas_call | solution.py:272
  18.3 1.6 %collective-permute-start.6 = (f32[2,4,256]{2,1,0:T(4,128)S(1)}, f32[2,4,256]{2,1,0:T(4,128)S(1)}, u32[]{:S(2)}, u32[]{:S(2)}) collective-permute-start(f32[2,4,256]{2,1,0:T(4,128)S(1)} %get-tuple-element.15.refs_0_.own_ref), channel_id=1, source_target_pairs={{0,4},{4,0},{1,5},{5,1},{2,6},{6,2},{3,7},{7,3},{8,12},{12,8},{9,1... | collective-permute-start | bytes 24584 | tf_op jit(solution)/shard_map/ppermute | solution.py:304
  19.9 0.7 %collective-permute-start.8 = (f32[2,4,256]{2,1,0:T(4,128)S(1)}, f32[2,4,256]{2,1,0:T(4,128)S(1)}, u32[]{:S(2)}, u32[]{:S(2)}) collective-permute-start(f32[2,4,256]{2,1,0:T(4,128)S(1)} %get-tuple-element.15.refs_0_.own_ref), channel_id=1, source_target_pairs={{0,28},{4,24},{8,20},{12,16},{16,12},{20,8},{24,4},{28,0},{1,29},{... | collective-permute-start | bytes 24584 | tf_op jit(solution)/shard_map/ppermute | solution.py:266
  20.6 1.0 %collective-permute-start.9 = (f32[2,4,256]{2,1,0:T(4,128)S(1)}, f32[2,4,256]{2,1,0:T(4,128)S(1)}, u32[]{:S(2)}, u32[]{:S(2)}) collective-permute-start(f32[2,4,256]{2,1,0:T(4,128)S(1)} %get-tuple-element.15.refs_0_.own_ref), channel_id=1, source_target_pairs={{0,24},{8,16},{16,8},{24,0},{1,25},{9,17},{17,9},{25,1},{2,26},{10... | collective-permute-start | bytes 24584 | tf_op jit(solution)/shard_map/ppermute | solution.py:306
  21.6 0.4 %collective-permute-done.6.refs_1_ = f32[2,4,256]{2,1,0:T(4,128)S(1)} collective-permute-done((f32[2,4,256]{2,1,0:T(4,128)S(1)}, f32[2,4,256]{2,1,0:T(4,128)S(1)}, u32[]{:S(2)}, u32[]{:S(2)}) %collective-permute-start.6) | collective-permute-done | bytes 8224 | tf_op jit(solution)/shard_map/ppermute | solution.py:304
  22.0 0.0 collective-permute-start.7
  22.1 1.4 %shard_map.64 = (bf16[2,256,48]{2,1,0:T(8,128)(2,1)S(1)}, f32[2,256,32]{2,1,0:T(8,128)S(1)}) custom-call(f32[2,4,256]{2,1,0:T(4,128)S(1)} %get-tuple-element.15.refs_0_.own_ref, f32[2,4,256]{2,1,0:T(4,128)S(1)} %collective-permute-done.6.refs_1_), custom_call_target="tpu_custom_call" | custom-call | flops 786432000 | bytes 262144 | tf_op jit(solution)/shard_map/pallas_call | solution.py:272
  23.4 0.0 collective-permute-done.7.near_x_ref
  23.5 0.4 %collective-permute-done.8.refs_0_ = f32[2,4,256]{2,1,0:T(4,128)S(1)} collective-permute-done((f32[2,4,256]{2,1,0:T(4,128)S(1)}, f32[2,4,256]{2,1,0:T(4,128)S(1)}, u32[]{:S(2)}, u32[]{:S(2)}) %collective-permute-start.8) | collective-permute-done | bytes 8224 | tf_op jit(solution)/shard_map/ppermute | solution.py:266
  23.9 0.0 collective-permute-done.9.refs_1_
  23.9 0.7 %collective-permute-start.10 = (f32[6,4,256]{2,1,0:T(4,128)S(1)}, f32[6,4,256]{2,1,0:T(4,128)S(1)}, u32[]{:S(2)}, u32[]{:S(2)}) collective-permute-start(f32[6,4,256]{2,1,0:T(4,128)S(1)} %get-tuple-element.19), channel_id=1, source_target_pairs={{0,1},{1,0},{2,3},{3,2},{4,5},{5,4},{6,7},{7,6},{8,9},{9,8},{10,11... | collective-permute-start | bytes 73736 | tf_op jit(solution)/shard_map/ppermute | solution.py:318
  24.7 1.6 %collective-permute-start.11 = (f32[6,4,256]{2,1,0:T(4,128)S(1)}, f32[6,4,256]{2,1,0:T(4,128)S(1)}, u32[]{:S(2)}, u32[]{:S(2)}) collective-permute-start(f32[6,4,256]{2,1,0:T(4,128)S(1)} %get-tuple-element.18), channel_id=1, source_target_pairs={{0,3},{1,2},{2,1},{3,0},{4,7},{5,6},{6,5},{7,4},{8,11},{9,10},{10,... | collective-permute-start | bytes 73736 | tf_op jit(solution)/shard_map/ppermute | solution.py:317
  26.3 2.2 %shard_map.65.before_ref = f32[2,256,32]{2,1,0:T(8,128)S(1)} custom-call(bf16[2,256,48]{2,1,0:T(8,128)(2,1)S(1)} %get-tuple-element.16.target_ref, f32[2,256,32]{2,1,0:T(8,128)S(1)} %get-tuple-element.17.before_ref, f32[2,2,4,256]{3,2,1,0:T(4,128)S(1)} %collective-permute-done.7.near_x_ref, f32[2,4,256]{2,1,0:T(4,128)S(1)} %collective-permute-done.8.refs_0_, ...), custom_call_target="tpu_custom_call" | custom-call | flops 1572864000 | bytes 262144 | tf_op jit(solution)/shard_map/pallas_call | solution.py:272
  28.5 0.0 collective-permute-done.10.source_ref
  28.5 1.1 %shard_map.66.bin_ref = f32[2,4,256]{2,1,0:T(4,128)S(1)} custom-call(f32[2,4,256]{2,1,0:T(4,128)S(1)} %get-tuple-element.14.speed_ref, f32[2,4,256]{2,1,0:T(4,128)S(1)} %get-tuple-element.15.refs_0_.own_ref, bf16[2,256,48]{2,1,0:T(8,128)(2,1)S(1)} %get-tuple-element.16.target_ref, f32[2,256,32]{2,1,0:T(8,128)S(1)} %shard_map.65.before_ref, ...), custom_call_target="tpu_custom_call" | custom-call | flops 589824000 | bytes 262144 | tf_op jit(solution)/shard_map/pallas_call | solution.py:272
  29.6 0.6 %collective-permute-done.11.source_ref = f32[6,4,256]{2,1,0:T(4,128)S(1)} collective-permute-done((f32[6,4,256]{2,1,0:T(4,128)S(1)}, f32[6,4,256]{2,1,0:T(4,128)S(1)}, u32[]{:S(2)}, u32[]{:S(2)}) %collective-permute-start.11) | collective-permute-done | bytes 24608 | tf_op jit(solution)/shard_map/ppermute | solution.py:317
  30.3 1.8 %shard_map.67 = (f32[3,1,1,2,256]{4,3,2,1,0:T(2,128)}, f32[3,1,1,2,256]{4,3,2,1,0:T(2,128)}) custom-call(f32[2,4,256]{2,1,0:T(4,128)S(1)} %copy-done.1, f32[2,4,256]{2,1,0:T(4,128)S(1)} %shard_map.66.bin_ref, f32[2,4,256]{2,1,0:T(4,128)S(1)} %get-tuple-element.14.speed_ref, f32[2,4,256]{2,1,0:T(4,128)S(1)} %get-tuple-element.15.refs_0_.own_ref, ...), custom_call_target="tpu_custom_call" | custom-call | flops 589824000 | bytes 262144 | tf_op jit(solution)/shard_map/pallas_call | solution.py:272
  (13 shorter events, 0.1 us)
Async XLA Ops:
  2.0 4.9 %collective-permute-start = (f32[2,4,256]{2,1,0:T(4,128)}, f32[2,4,256]{2,1,0:T(4,128)S(1)}, u32[]{:S(2)}, u32[]{:S(2)}) collective-permute-start(f32[2,4,256]{2,1,0:T(4,128)} %get-tuple-element.11.refs_0_.own_ref), channel_id=1, source_target_pairs={{0,4},{4,0},{1,5},{5,1},{2,6},{6,2},{3,7},{7,3},{8,12},{12,8},{9,1... | collective-permute-start | bytes 24584 | tf_op jit(solution)/shard_map/ppermute | solution.py:304
  5.0 4.5 %collective-permute-start.2 = (f32[2,4,256]{2,1,0:T(4,128)}, f32[2,4,256]{2,1,0:T(4,128)S(1)}, u32[]{:S(2)}, u32[]{:S(2)}) collective-permute-start(f32[2,4,256]{2,1,0:T(4,128)} %get-tuple-element.11.refs_0_.own_ref), channel_id=1, source_target_pairs={{0,28},{4,24},{8,20},{12,16},{16,12},{20,8},{24,4},{28,0},{1,29},{... | collective-permute-start | bytes 24584 | tf_op jit(solution)/shard_map/ppermute | solution.py:266
  5.6 3.9 %collective-permute-start.3 = (f32[2,4,256]{2,1,0:T(4,128)}, f32[2,4,256]{2,1,0:T(4,128)S(1)}, u32[]{:S(2)}, u32[]{:S(2)}) collective-permute-start(f32[2,4,256]{2,1,0:T(4,128)} %get-tuple-element.11.refs_0_.own_ref), channel_id=1, source_target_pairs={{0,24},{8,16},{16,8},{24,0},{1,25},{9,17},{17,9},{25,1},{2,26},{10... | collective-permute-start | bytes 24584 | tf_op jit(solution)/shard_map/ppermute | solution.py:306
  6.9 0.7 %copy-start = (f32[2,4,256]{2,1,0:T(4,128)S(1)}, f32[2,4,256]{2,1,0:T(4,128)}, u32[]{:S(2)}) copy-start(f32[2,4,256]{2,1,0:T(4,128)} %get-tuple-element.11.refs_0_.own_ref) | copy-start | bytes 24580
  7.6 1.8 %collective-permute-start.1 = (f32[2,2,4,256]{3,2,1,0:T(4,128)S(1)}, f32[2,2,4,256]{3,2,1,0:T(4,128)S(1)}, u32[]{:S(2)}, u32[]{:S(2)}) collective-permute-start(f32[2,2,4,256]{3,2,1,0:T(4,128)S(1)} %pad_maximum_fusion), channel_id=1, source_target_pairs={{0,8},{8,0},{16,24},{24,16},{1,9},{9,1},{17,25},{25,17},{2,10},{10... | collective-permute-start | bytes 49160 | tf_op jit(solution)/shard_map/ppermute | solution.py:308
  9.5 6.4 %collective-permute-start.4 = (f32[6,4,256]{2,1,0:T(4,128)S(1)}, f32[6,4,256]{2,1,0:T(4,128)S(1)}, u32[]{:S(2)}, u32[]{:S(2)}) collective-permute-start(f32[6,4,256]{2,1,0:T(4,128)S(1)} %get-tuple-element.21), channel_id=1, source_target_pairs={{0,1},{1,0},{2,3},{3,2},{4,5},{5,4},{6,7},{7,6},{8,9},{9,8},{10,11... | collective-permute-start | bytes 73736 | tf_op jit(solution)/shard_map/ppermute | solution.py:318
  11.3 5.9 %collective-permute-start.5 = (f32[6,4,256]{2,1,0:T(4,128)S(1)}, f32[6,4,256]{2,1,0:T(4,128)S(1)}, u32[]{:S(2)}, u32[]{:S(2)}) collective-permute-start(f32[6,4,256]{2,1,0:T(4,128)S(1)} %get-tuple-element.20), channel_id=1, source_target_pairs={{0,3},{1,2},{2,1},{3,0},{4,7},{5,6},{6,5},{7,4},{8,11},{9,10},{10,... | collective-permute-start | bytes 73736 | tf_op jit(solution)/shard_map/ppermute | solution.py:317
  13.7 2.2 %copy-start.2 = (f32[3,1,1,2,256]{4,3,2,1,0:T(2,128)S(1)}, f32[3,1,1,2,256]{4,3,2,1,0:T(2,128)}, u32[]{:S(2)}) copy-start(f32[3,1,1,2,256]{4,3,2,1,0:T(2,128)} %speed_ref.3) | copy-start | bytes 18436
  15.9 1.2 %copy-start.1 = (f32[2,4,256]{2,1,0:T(4,128)S(1)}, f32[2,4,256]{2,1,0:T(4,128)}, u32[]{:S(2)}) copy-start(f32[2,4,256]{2,1,0:T(4,128)} %get-tuple-element.10.keep_ref) | copy-start | bytes 24580
  18.3 3.7 %collective-permute-start.6 = (f32[2,4,256]{2,1,0:T(4,128)S(1)}, f32[2,4,256]{2,1,0:T(4,128)S(1)}, u32[]{:S(2)}, u32[]{:S(2)}) collective-permute-start(f32[2,4,256]{2,1,0:T(4,128)S(1)} %get-tuple-element.15.refs_0_.own_ref), channel_id=1, source_target_pairs={{0,4},{4,0},{1,5},{5,1},{2,6},{6,2},{3,7},{7,3},{8,12},{12,8},{9,1... | collective-permute-start | bytes 24584 | tf_op jit(solution)/shard_map/ppermute | solution.py:304
  19.9 4.0 %collective-permute-start.8 = (f32[2,4,256]{2,1,0:T(4,128)S(1)}, f32[2,4,256]{2,1,0:T(4,128)S(1)}, u32[]{:S(2)}, u32[]{:S(2)}) collective-permute-start(f32[2,4,256]{2,1,0:T(4,128)S(1)} %get-tuple-element.15.refs_0_.own_ref), channel_id=1, source_target_pairs={{0,28},{4,24},{8,20},{12,16},{16,12},{20,8},{24,4},{28,0},{1,29},{... | collective-permute-start | bytes 24584 | tf_op jit(solution)/shard_map/ppermute | solution.py:266
  20.6 3.3 %collective-permute-start.9 = (f32[2,4,256]{2,1,0:T(4,128)S(1)}, f32[2,4,256]{2,1,0:T(4,128)S(1)}, u32[]{:S(2)}, u32[]{:S(2)}) collective-permute-start(f32[2,4,256]{2,1,0:T(4,128)S(1)} %get-tuple-element.15.refs_0_.own_ref), channel_id=1, source_target_pairs={{0,24},{8,16},{16,8},{24,0},{1,25},{9,17},{17,9},{25,1},{2,26},{10... | collective-permute-start | bytes 24584 | tf_op jit(solution)/shard_map/ppermute | solution.py:306
  22.0 1.4 %collective-permute-start.7 = (f32[2,2,4,256]{3,2,1,0:T(4,128)S(1)}, f32[2,2,4,256]{3,2,1,0:T(4,128)S(1)}, u32[]{:S(2)}, u32[]{:S(2)}) collective-permute-start(f32[2,2,4,256]{3,2,1,0:T(4,128)S(1)} %pad_maximum_fusion.1), channel_id=1, source_target_pairs={{0,8},{8,0},{16,24},{24,16},{1,9},{9,1},{17,25},{25,17},{2,10},{10... | collective-permute-start | bytes 49160 | tf_op jit(solution)/shard_map/ppermute | solution.py:308
  23.9 4.6 %collective-permute-start.10 = (f32[6,4,256]{2,1,0:T(4,128)S(1)}, f32[6,4,256]{2,1,0:T(4,128)S(1)}, u32[]{:S(2)}, u32[]{:S(2)}) collective-permute-start(f32[6,4,256]{2,1,0:T(4,128)S(1)} %get-tuple-element.19), channel_id=1, source_target_pairs={{0,1},{1,0},{2,3},{3,2},{4,5},{5,4},{6,7},{7,6},{8,9},{9,8},{10,11... | collective-permute-start | bytes 73736 | tf_op jit(solution)/shard_map/ppermute | solution.py:318
  24.7 5.6 %collective-permute-start.11 = (f32[6,4,256]{2,1,0:T(4,128)S(1)}, f32[6,4,256]{2,1,0:T(4,128)S(1)}, u32[]{:S(2)}, u32[]{:S(2)}) collective-permute-start(f32[6,4,256]{2,1,0:T(4,128)S(1)} %get-tuple-element.18), channel_id=1, source_target_pairs={{0,3},{1,2},{2,1},{3,0},{4,7},{5,6},{6,5},{7,4},{8,11},{9,10},{10,... | collective-permute-start | bytes 73736 | tf_op jit(solution)/shard_map/ppermute | solution.py:317

commit v7 on v6

--- a/solution.py
+++ b/solution.py
@@ -295,6 +295,7 @@
         out_shape=(bins, bins),
         in_specs=[VMEM] * 3,
         out_specs=(VMEM, VMEM),
+        compiler_params=pltpu.CompilerParams(vmem_limit_bytes=8 * 1024 * 1024),
     )(counts, positions, mass)
     speed = velocities
     upper = lax.rem(lax.axis_index("gz"), 2)

time: 32.3 us -> 32 us (level)
  Pallas kernels: 13.8 us -> 12.4 us
  waiting for transfers between devices: 1.52 us -> 2.41 us
  local copies, waits for them, and re-layouts: 1.52 us -> 2.11 us
  starting transfers between devices: 14.4 us -> 14 us
    pallas_call x1, Pallas kernels: 1.39 us -> 0.08 us  [on_device(): pl.pallas_call(pack_kernel, out_shape=(bins, bins), in_specs=[VMEM] * 3,...]
    unnamed x14 -> x16, local copies, waits for them, and re-layouts: 1.49 us -> 2.08 us
    ppermute x2, waiting for transfers between devices: 0.42 us -> 0.94 us  [across(): return lax.ppermute(value, ('gx', 'gy'), pairs)]
    ppermute x2, starting transfers between devices: 1.58 us -> 2.03 us  [on_device(): lax.ppermute(packed, 'gx', far)]
    ppermute x2, starting transfers between devices: 0.44 us -> 0.05 us  [on_device(): near_x = lax.ppermute(plane, 'gx', near)]
    ppermute x2, waiting for transfers between devices: 0.44 us -> 0.81 us  [on_device(): planes = [packed] + [lax.ppermute(packed, 'gy', path) for path in paths]]
    ppermute x2, starting transfers between devices: 4.56 us -> 4.22 us  [on_device(): planes = [packed] + [lax.ppermute(packed, 'gy', path) for path in paths]]
  transfers between devices with their start and end apart: 12 -> 12, of which waited for: 3 -> 5; matrix products, arithmetic and copies ran while one was open for 2% -> 0% of each run, Pallas kernels for 29% -> 30%
where the time goes in v7:
time: 32 us; the launch traced here: 31.8 us
  starting transfers between devices  14 us (44%)
  Pallas kernels  12.4 us (39%)
  waiting for transfers between devices  2.41 us (8%)
  local copies, waits for them, and re-layouts  2.11 us (7%)
  between operations  0.79 us (2%)
    pallas_call x8, Pallas kernels, call(): pl.pallas_call(kernel, out_shape=outputs, in_specs=[VMEM] * len(inputs),...  12.4 us
    ppermute x2, starting transfers between devices, on_device(): planes = [packed] + [lax.ppermute(packed, 'gy', path) for path in paths]  4.22 us
    ppermute x2, starting transfers between devices, on_device(): lax.ppermute(lax.dynamic_index_in_dim(slab, upper, 1, False), 'gz', far)  4.09 us
    ppermute x2, starting transfers between devices, on_device(): lax.ppermute(lax.dynamic_index_in_dim(slab, 1 - upper, 1, False), 'gz', n...  2.38 us
    unnamed x16, local copies, waits for them, and re-layouts  2.08 us
    ppermute x2, starting transfers between devices, on_device(): lax.ppermute(packed, 'gx', far)  2.03 us
    ppermute x2, starting transfers between devices, across(): return lax.ppermute(value, ('gx', 'gy'), pairs)  1.25 us
    ppermute x2, waiting for transfers between devices, across(): return lax.ppermute(value, ('gx', 'gy'), pairs)  0.94 us
  transfers between devices with their start and end apart: 12, of which 5 were waited for; matrix products, arithmetic and copies ran while one was open for 0% of the time, Pallas kernels for 30%

profile of v7, /device:TPU:0, one launch (start us, length us, event | category | flops | bytes accessed | tf_op | source)
XLA Modules:
  0.0 31.8 jit_solution(2618770749349221959)
XLA Ops:
  0.6 0.0 copy-start
  0.6 0.7 %copy-done = f32[3,1,1,2,256]{4,3,2,1,0:T(2,128)S(1)} copy-done((f32[3,1,1,2,256]{4,3,2,1,0:T(2,128)S(1)}, f32[3,1,1,2,256]{4,3,2,1,0:T(2,128)}, u32[]{:S(2)}) %copy-start) | copy-done | bytes 6168
  1.3 0.0 copy-start.1
  1.3 0.7 %copy-done.1 = f32[1,1,2,256]{3,2,1,0:T(2,128)S(1)} copy-done((f32[1,1,2,256]{3,2,1,0:T(2,128)S(1)}, f32[1,1,2,256]{3,2,1,0:T(2,128)}, u32[]{:S(2)}) %copy-start.1) | copy-done | bytes 2072
  2.0 0.0 copy-start.2
  2.0 0.7 %copy-done.2 = s32[1,1,2]{2,1,0:T(1,128)S(1)} copy-done((s32[1,1,2]{2,1,0:T(1,128)S(1)}, s32[1,1,2]{2,1,0:T(1,128)}, u32[]{:S(2)}) %copy-start.2) | copy-done | bytes 32
  2.7 0.1 shard_map.59
  2.7 3.0 %collective-permute-start = (f32[2,4,256]{2,1,0:T(4,128)S(1)}, f32[2,4,256]{2,1,0:T(4,128)S(1)}, u32[]{:S(2)}, u32[]{:S(2)}) collective-permute-start(f32[2,4,256]{2,1,0:T(4,128)S(1)} %get-tuple-element.11.refs_0_.own_ref), channel_id=1, source_target_pairs={{0,4},{4,0},{1,5},{5,1},{2,6},{6,2},{3,7},{7,3},{8,12},{12,8},{9,1... | collective-permute-start | bytes 24584 | tf_op jit(solution)/shard_map/ppermute | solution.py:305
  5.7 0.6 %collective-permute-start.2 = (f32[2,4,256]{2,1,0:T(4,128)S(1)}, f32[2,4,256]{2,1,0:T(4,128)S(1)}, u32[]{:S(2)}, u32[]{:S(2)}) collective-permute-start(f32[2,4,256]{2,1,0:T(4,128)S(1)} %get-tuple-element.11.refs_0_.own_ref), channel_id=1, source_target_pairs={{0,28},{4,24},{8,20},{12,16},{16,12},{20,8},{24,4},{28,0},{1,29},{... | collective-permute-start | bytes 24584 | tf_op jit(solution)/shard_map/ppermute | solution.py:266
  6.3 0.7 %collective-permute-start.3 = (f32[2,4,256]{2,1,0:T(4,128)S(1)}, f32[2,4,256]{2,1,0:T(4,128)S(1)}, u32[]{:S(2)}, u32[]{:S(2)}) collective-permute-start(f32[2,4,256]{2,1,0:T(4,128)S(1)} %get-tuple-element.11.refs_0_.own_ref), channel_id=1, source_target_pairs={{0,24},{8,16},{16,8},{24,0},{1,25},{9,17},{17,9},{25,1},{2,26},{10... | collective-permute-start | bytes 24584 | tf_op jit(solution)/shard_map/ppermute | solution.py:307
  7.0 0.4 %collective-permute-done.refs_1_ = f32[2,4,256]{2,1,0:T(4,128)S(1)} collective-permute-done((f32[2,4,256]{2,1,0:T(4,128)S(1)}, f32[2,4,256]{2,1,0:T(4,128)S(1)}, u32[]{:S(2)}, u32[]{:S(2)}) %collective-permute-start) | collective-permute-done | bytes 8224 | tf_op jit(solution)/shard_map/ppermute | solution.py:305
  7.3 0.1 collective-permute-start.1
  7.4 1.4 %shard_map.60 = (bf16[2,256,48]{2,1,0:T(8,128)(2,1)S(1)}, f32[2,256,32]{2,1,0:T(8,128)S(1)}) custom-call(f32[2,4,256]{2,1,0:T(4,128)S(1)} %get-tuple-element.11.refs_0_.own_ref, f32[2,4,256]{2,1,0:T(4,128)S(1)} %collective-permute-done.refs_1_), custom_call_target="tpu_custom_call" | custom-call | flops 786432000 | bytes 262144 | tf_op jit(solution)/shard_map/pallas_call | solution.py:272
  8.8 0.0 collective-permute-done.1.near_x_ref
  8.8 0.9 %collective-permute-done.2.refs_0_ = f32[2,4,256]{2,1,0:T(4,128)S(1)} collective-permute-done((f32[2,4,256]{2,1,0:T(4,128)S(1)}, f32[2,4,256]{2,1,0:T(4,128)S(1)}, u32[]{:S(2)}, u32[]{:S(2)}) %collective-permute-start.2) | collective-permute-done | bytes 8224 | tf_op jit(solution)/shard_map/ppermute | solution.py:266
  9.7 0.0 collective-permute-done.3.refs_1_
  9.7 1.6 %collective-permute-start.4 = (f32[6,4,256]{2,1,0:T(4,128)S(1)}, f32[6,4,256]{2,1,0:T(4,128)S(1)}, u32[]{:S(2)}, u32[]{:S(2)}) collective-permute-start(f32[6,4,256]{2,1,0:T(4,128)S(1)} %get-tuple-element.21), channel_id=1, source_target_pairs={{0,1},{1,0},{2,3},{3,2},{4,5},{5,4},{6,7},{7,6},{8,9},{9,8},{10,11... | collective-permute-start | bytes 73736 | tf_op jit(solution)/shard_map/ppermute | solution.py:319
  11.4 2.5 %collective-permute-start.5 = (f32[6,4,256]{2,1,0:T(4,128)S(1)}, f32[6,4,256]{2,1,0:T(4,128)S(1)}, u32[]{:S(2)}, u32[]{:S(2)}) collective-permute-start(f32[6,4,256]{2,1,0:T(4,128)S(1)} %get-tuple-element.20), channel_id=1, source_target_pairs={{0,3},{1,2},{2,1},{3,0},{4,7},{5,6},{6,5},{7,4},{8,11},{9,10},{10,... | collective-permute-start | bytes 73736 | tf_op jit(solution)/shard_map/ppermute | solution.py:318
  13.8 0.0 copy-start.3
  13.8 2.2 %shard_map.61.before_ref = f32[2,256,32]{2,1,0:T(8,128)S(1)} custom-call(bf16[2,256,48]{2,1,0:T(8,128)(2,1)S(1)} %get-tuple-element.12.target_ref, f32[2,256,32]{2,1,0:T(8,128)S(1)} %get-tuple-element.13.before_ref, f32[2,2,4,256]{3,2,1,0:T(4,128)S(1)} %collective-permute-done.1.near_x_ref, f32[2,4,256]{2,1,0:T(4,128)S(1)} %collective-permute-done.2.refs_0_, ...), custom_call_target="tpu_custom_call" | custom-call | flops 1572864000 | bytes 262144 | tf_op jit(solution)/shard_map/pallas_call | solution.py:272
  16.0 0.0 collective-permute-done.4.source_ref
  16.0 0.0 copy-done.3
  16.1 1.2 %shard_map.62.bin_ref = f32[2,4,256]{2,1,0:T(4,128)S(1)} custom-call(f32[3,1,1,2,256]{4,3,2,1,0:T(2,128)S(1)} %copy-done.3, f32[2,4,256]{2,1,0:T(4,128)S(1)} %get-tuple-element.11.refs_0_.own_ref, bf16[2,256,48]{2,1,0:T(8,128)(2,1)S(1)} %get-tuple-element.12.target_ref, f32[2,256,32]{2,1,0:T(8,128)S(1)} %shard_map.61.before_ref, ...), custom_call_target="tpu_custom_call" | custom-call | flops 589824000 | bytes 262144 | tf_op jit(solution)/shard_map/pallas_call | solution.py:272
  17.2 0.0 collective-permute-done.5.source_ref
  17.2 1.2 %shard_map.63 = (f32[2,4,256]{2,1,0:T(4,128)S(1)}, f32[2,4,256]{2,1,0:T(4,128)S(1)}) custom-call(f32[2,4,256]{2,1,0:T(4,128)S(1)} %get-tuple-element.10.keep_ref, f32[2,4,256]{2,1,0:T(4,128)S(1)} %shard_map.62.bin_ref, f32[3,1,1,2,256]{4,3,2,1,0:T(2,128)S(1)} %copy-done.3, f32[2,4,256]{2,1,0:T(4,128)S(1)} %get-tuple-element.11.refs_0_.own_ref, ...), custom_call_target="tpu_custom_call" | custom-call | flops 589824000 | bytes 262144 | tf_op jit(solution)/shard_map/pallas_call | solution.py:272
  18.4 1.3 %collective-permute-start.6 = (f32[2,4,256]{2,1,0:T(4,128)S(1)}, f32[2,4,256]{2,1,0:T(4,128)S(1)}, u32[]{:S(2)}, u32[]{:S(2)}) collective-permute-start(f32[2,4,256]{2,1,0:T(4,128)S(1)} %get-tuple-element.15.refs_0_.own_ref), channel_id=1, source_target_pairs={{0,4},{4,0},{1,5},{5,1},{2,6},{6,2},{3,7},{7,3},{8,12},{12,8},{9,1... | collective-permute-start | bytes 24584 | tf_op jit(solution)/shard_map/ppermute | solution.py:305
  19.7 0.7 %collective-permute-start.8 = (f32[2,4,256]{2,1,0:T(4,128)S(1)}, f32[2,4,256]{2,1,0:T(4,128)S(1)}, u32[]{:S(2)}, u32[]{:S(2)}) collective-permute-start(f32[2,4,256]{2,1,0:T(4,128)S(1)} %get-tuple-element.15.refs_0_.own_ref), channel_id=1, source_target_pairs={{0,28},{4,24},{8,20},{12,16},{16,12},{20,8},{24,4},{28,0},{1,29},{... | collective-permute-start | bytes 24584 | tf_op jit(solution)/shard_map/ppermute | solution.py:266
  20.3 1.4 %collective-permute-start.9 = (f32[2,4,256]{2,1,0:T(4,128)S(1)}, f32[2,4,256]{2,1,0:T(4,128)S(1)}, u32[]{:S(2)}, u32[]{:S(2)}) collective-permute-start(f32[2,4,256]{2,1,0:T(4,128)S(1)} %get-tuple-element.15.refs_0_.own_ref), channel_id=1, source_target_pairs={{0,24},{8,16},{16,8},{24,0},{1,25},{9,17},{17,9},{25,1},{2,26},{10... | collective-permute-start | bytes 24584 | tf_op jit(solution)/shard_map/ppermute | solution.py:307
  21.7 0.4 %collective-permute-done.6.refs_1_ = f32[2,4,256]{2,1,0:T(4,128)S(1)} collective-permute-done((f32[2,4,256]{2,1,0:T(4,128)S(1)}, f32[2,4,256]{2,1,0:T(4,128)S(1)}, u32[]{:S(2)}, u32[]{:S(2)}) %collective-permute-start.6) | collective-permute-done | bytes 8224 | tf_op jit(solution)/shard_map/ppermute | solution.py:305
  22.1 0.0 collective-permute-start.7
  22.1 1.4 %shard_map.64 = (bf16[2,256,48]{2,1,0:T(8,128)(2,1)S(1)}, f32[2,256,32]{2,1,0:T(8,128)S(1)}) custom-call(f32[2,4,256]{2,1,0:T(4,128)S(1)} %get-tuple-element.15.refs_0_.own_ref, f32[2,4,256]{2,1,0:T(4,128)S(1)} %collective-permute-done.6.refs_1_), custom_call_target="tpu_custom_call" | custom-call | flops 786432000 | bytes 262144 | tf_op jit(solution)/shard_map/pallas_call | solution.py:272
  23.5 0.0 collective-permute-done.7.near_x_ref
  23.6 0.1 collective-permute-done.8.refs_0_
  23.6 0.0 collective-permute-done.9.refs_1_
  23.7 0.7 %collective-permute-start.10 = (f32[6,4,256]{2,1,0:T(4,128)S(1)}, f32[6,4,256]{2,1,0:T(4,128)S(1)}, u32[]{:S(2)}, u32[]{:S(2)}) collective-permute-start(f32[6,4,256]{2,1,0:T(4,128)S(1)} %get-tuple-element.19), channel_id=1, source_target_pairs={{0,1},{1,0},{2,3},{3,2},{4,5},{5,4},{6,7},{7,6},{8,9},{9,8},{10,11... | collective-permute-start | bytes 73736 | tf_op jit(solution)/shard_map/ppermute | solution.py:319
  24.4 1.6 %collective-permute-start.11 = (f32[6,4,256]{2,1,0:T(4,128)S(1)}, f32[6,4,256]{2,1,0:T(4,128)S(1)}, u32[]{:S(2)}, u32[]{:S(2)}) collective-permute-start(f32[6,4,256]{2,1,0:T(4,128)S(1)} %get-tuple-element.18), channel_id=1, source_target_pairs={{0,3},{1,2},{2,1},{3,0},{4,7},{5,6},{6,5},{7,4},{8,11},{9,10},{10,... | collective-permute-start | bytes 73736 | tf_op jit(solution)/shard_map/ppermute | solution.py:318
  26.0 2.2 %shard_map.65.before_ref = f32[2,256,32]{2,1,0:T(8,128)S(1)} custom-call(bf16[2,256,48]{2,1,0:T(8,128)(2,1)S(1)} %get-tuple-element.16.target_ref, f32[2,256,32]{2,1,0:T(8,128)S(1)} %get-tuple-element.17.before_ref, f32[2,2,4,256]{3,2,1,0:T(4,128)S(1)} %collective-permute-done.7.near_x_ref, f32[2,4,256]{2,1,0:T(4,128)S(1)} %collective-permute-done.8.refs_0_, ...), custom_call_target="tpu_custom_call" | custom-call | flops 1572864000 | bytes 262144 | tf_op jit(solution)/shard_map/pallas_call | solution.py:272
  28.2 0.0 collective-permute-done.10.source_ref
  28.2 1.1 %shard_map.66.bin_ref = f32[2,4,256]{2,1,0:T(4,128)S(1)} custom-call(f32[2,4,256]{2,1,0:T(4,128)S(1)} %get-tuple-element.14.speed_ref, f32[2,4,256]{2,1,0:T(4,128)S(1)} %get-tuple-element.15.refs_0_.own_ref, bf16[2,256,48]{2,1,0:T(8,128)(2,1)S(1)} %get-tuple-element.16.target_ref, f32[2,256,32]{2,1,0:T(8,128)S(1)} %shard_map.65.before_ref, ...), custom_call_target="tpu_custom_call" | custom-call | flops 589824000 | bytes 262144 | tf_op jit(solution)/shard_map/pallas_call | solution.py:272
  29.4 0.6 %collective-permute-done.11.source_ref = f32[6,4,256]{2,1,0:T(4,128)S(1)} collective-permute-done((f32[6,4,256]{2,1,0:T(4,128)S(1)}, f32[6,4,256]{2,1,0:T(4,128)S(1)}, u32[]{:S(2)}, u32[]{:S(2)}) %collective-permute-start.11) | collective-permute-done | bytes 24608 | tf_op jit(solution)/shard_map/ppermute | solution.py:318
  30.0 1.8 %shard_map.67 = (f32[3,1,1,2,256]{4,3,2,1,0:T(2,128)}, f32[3,1,1,2,256]{4,3,2,1,0:T(2,128)}) custom-call(f32[2,4,256]{2,1,0:T(4,128)S(1)} %get-tuple-element.10.keep_ref, f32[2,4,256]{2,1,0:T(4,128)S(1)} %shard_map.66.bin_ref, f32[2,4,256]{2,1,0:T(4,128)S(1)} %get-tuple-element.14.speed_ref, f32[2,4,256]{2,1,0:T(4,128)S(1)} %get-tuple-element.15.refs_0_.own_ref, ...), custom_call_target="tpu_custom_call" | custom-call | flops 589824000 | bytes 262144 | tf_op jit(solution)/shard_map/pallas_call | solution.py:272
  (14 shorter events, 0.1 us)
Async XLA Ops:
  0.6 0.7 %copy-start = (f32[3,1,1,2,256]{4,3,2,1,0:T(2,128)S(1)}, f32[3,1,1,2,256]{4,3,2,1,0:T(2,128)}, u32[]{:S(2)}) copy-start(f32[3,1,1,2,256]{4,3,2,1,0:T(2,128)} %place_ref.1) | copy-start | bytes 18436
  1.3 0.7 %copy-start.1 = (f32[1,1,2,256]{3,2,1,0:T(2,128)S(1)}, f32[1,1,2,256]{3,2,1,0:T(2,128)}, u32[]{:S(2)}) copy-start(f32[1,1,2,256]{3,2,1,0:T(2,128)} %mass_ref.1) | copy-start | bytes 6148
  2.0 0.7 %copy-start.2 = (s32[1,1,2]{2,1,0:T(1,128)S(1)}, s32[1,1,2]{2,1,0:T(1,128)}, u32[]{:S(2)}) copy-start(s32[1,1,2]{2,1,0:T(1,128)} %counts_ref.1) | copy-start | bytes 28
  2.7 4.6 %collective-permute-start = (f32[2,4,256]{2,1,0:T(4,128)S(1)}, f32[2,4,256]{2,1,0:T(4,128)S(1)}, u32[]{:S(2)}, u32[]{:S(2)}) collective-permute-start(f32[2,4,256]{2,1,0:T(4,128)S(1)} %get-tuple-element.11.refs_0_.own_ref), channel_id=1, source_target_pairs={{0,4},{4,0},{1,5},{5,1},{2,6},{6,2},{3,7},{7,3},{8,12},{12,8},{9,1... | collective-permute-start | bytes 24584 | tf_op jit(solution)/shard_map/ppermute | solution.py:305
  5.7 4.0 %collective-permute-start.2 = (f32[2,4,256]{2,1,0:T(4,128)S(1)}, f32[2,4,256]{2,1,0:T(4,128)S(1)}, u32[]{:S(2)}, u32[]{:S(2)}) collective-permute-start(f32[2,4,256]{2,1,0:T(4,128)S(1)} %get-tuple-element.11.refs_0_.own_ref), channel_id=1, source_target_pairs={{0,28},{4,24},{8,20},{12,16},{16,12},{20,8},{24,4},{28,0},{1,29},{... | collective-permute-start | bytes 24584 | tf_op jit(solution)/shard_map/ppermute | solution.py:266
  6.3 3.4 %collective-permute-start.3 = (f32[2,4,256]{2,1,0:T(4,128)S(1)}, f32[2,4,256]{2,1,0:T(4,128)S(1)}, u32[]{:S(2)}, u32[]{:S(2)}) collective-permute-start(f32[2,4,256]{2,1,0:T(4,128)S(1)} %get-tuple-element.11.refs_0_.own_ref), channel_id=1, source_target_pairs={{0,24},{8,16},{16,8},{24,0},{1,25},{9,17},{17,9},{25,1},{2,26},{10... | collective-permute-start | bytes 24584 | tf_op jit(solution)/shard_map/ppermute | solution.py:307
  7.3 1.5 %collective-permute-start.1 = (f32[2,2,4,256]{3,2,1,0:T(4,128)S(1)}, f32[2,2,4,256]{3,2,1,0:T(4,128)S(1)}, u32[]{:S(2)}, u32[]{:S(2)}) collective-permute-start(f32[2,2,4,256]{3,2,1,0:T(4,128)S(1)} %pad_maximum_fusion), channel_id=1, source_target_pairs={{0,8},{8,0},{16,24},{24,16},{1,9},{9,1},{17,25},{25,17},{2,10},{10... | collective-permute-start | bytes 49160 | tf_op jit(solution)/shard_map/ppermute | solution.py:309
  9.7 6.3 %collective-permute-start.4 = (f32[6,4,256]{2,1,0:T(4,128)S(1)}, f32[6,4,256]{2,1,0:T(4,128)S(1)}, u32[]{:S(2)}, u32[]{:S(2)}) collective-permute-start(f32[6,4,256]{2,1,0:T(4,128)S(1)} %get-tuple-element.21), channel_id=1, source_target_pairs={{0,1},{1,0},{2,3},{3,2},{4,5},{5,4},{6,7},{7,6},{8,9},{9,8},{10,11... | collective-permute-start | bytes 73736 | tf_op jit(solution)/shard_map/ppermute | solution.py:319
  11.4 5.9 %collective-permute-start.5 = (f32[6,4,256]{2,1,0:T(4,128)S(1)}, f32[6,4,256]{2,1,0:T(4,128)S(1)}, u32[]{:S(2)}, u32[]{:S(2)}) collective-permute-start(f32[6,4,256]{2,1,0:T(4,128)S(1)} %get-tuple-element.20), channel_id=1, source_target_pairs={{0,3},{1,2},{2,1},{3,0},{4,7},{5,6},{6,5},{7,4},{8,11},{9,10},{10,... | collective-permute-start | bytes 73736 | tf_op jit(solution)/shard_map/ppermute | solution.py:318
  13.8 2.2 %copy-start.3 = (f32[3,1,1,2,256]{4,3,2,1,0:T(2,128)S(1)}, f32[3,1,1,2,256]{4,3,2,1,0:T(2,128)}, u32[]{:S(2)}) copy-start(f32[3,1,1,2,256]{4,3,2,1,0:T(2,128)} %speed_ref.3) | copy-start | bytes 18436
  18.4 3.7 %collective-permute-start.6 = (f32[2,4,256]{2,1,0:T(4,128)S(1)}, f32[2,4,256]{2,1,0:T(4,128)S(1)}, u32[]{:S(2)}, u32[]{:S(2)}) collective-permute-start(f32[2,4,256]{2,1,0:T(4,128)S(1)} %get-tuple-element.15.refs_0_.own_ref), channel_id=1, source_target_pairs={{0,4},{4,0},{1,5},{5,1},{2,6},{6,2},{3,7},{7,3},{8,12},{12,8},{9,1... | collective-permute-start | bytes 24584 | tf_op jit(solution)/shard_map/ppermute | solution.py:305
  19.7 4.0 %collective-permute-start.8 = (f32[2,4,256]{2,1,0:T(4,128)S(1)}, f32[2,4,256]{2,1,0:T(4,128)S(1)}, u32[]{:S(2)}, u32[]{:S(2)}) collective-permute-start(f32[2,4,256]{2,1,0:T(4,128)S(1)} %get-tuple-element.15.refs_0_.own_ref), channel_id=1, source_target_pairs={{0,28},{4,24},{8,20},{12,16},{16,12},{20,8},{24,4},{28,0},{1,29},{... | collective-permute-start | bytes 24584 | tf_op jit(solution)/shard_map/ppermute | solution.py:266
  20.3 3.3 %collective-permute-start.9 = (f32[2,4,256]{2,1,0:T(4,128)S(1)}, f32[2,4,256]{2,1,0:T(4,128)S(1)}, u32[]{:S(2)}, u32[]{:S(2)}) collective-permute-start(f32[2,4,256]{2,1,0:T(4,128)S(1)} %get-tuple-element.15.refs_0_.own_ref), channel_id=1, source_target_pairs={{0,24},{8,16},{16,8},{24,0},{1,25},{9,17},{17,9},{25,1},{2,26},{10... | collective-permute-start | bytes 24584 | tf_op jit(solution)/shard_map/ppermute | solution.py:307
  22.1 1.4 %collective-permute-start.7 = (f32[2,2,4,256]{3,2,1,0:T(4,128)S(1)}, f32[2,2,4,256]{3,2,1,0:T(4,128)S(1)}, u32[]{:S(2)}, u32[]{:S(2)}) collective-permute-start(f32[2,2,4,256]{3,2,1,0:T(4,128)S(1)} %pad_maximum_fusion.1), channel_id=1, source_target_pairs={{0,8},{8,0},{16,24},{24,16},{1,9},{9,1},{17,25},{25,17},{2,10},{10... | collective-permute-start | bytes 49160 | tf_op jit(solution)/shard_map/ppermute | solution.py:309
  23.7 4.6 %collective-permute-start.10 = (f32[6,4,256]{2,1,0:T(4,128)S(1)}, f32[6,4,256]{2,1,0:T(4,128)S(1)}, u32[]{:S(2)}, u32[]{:S(2)}) collective-permute-start(f32[6,4,256]{2,1,0:T(4,128)S(1)} %get-tuple-element.19), channel_id=1, source_target_pairs={{0,1},{1,0},{2,3},{3,2},{4,5},{5,4},{6,7},{7,6},{8,9},{9,8},{10,11... | collective-permute-start | bytes 73736 | tf_op jit(solution)/shard_map/ppermute | solution.py:319
  24.4 5.6 %collective-permute-start.11 = (f32[6,4,256]{2,1,0:T(4,128)S(1)}, f32[6,4,256]{2,1,0:T(4,128)S(1)}, u32[]{:S(2)}, u32[]{:S(2)}) collective-permute-start(f32[6,4,256]{2,1,0:T(4,128)S(1)} %get-tuple-element.18), channel_id=1, source_target_pairs={{0,3},{1,2},{2,1},{3,0},{4,7},{5,6},{6,5},{7,4},{8,11},{9,10},{10,... | collective-permute-start | bytes 73736 | tf_op jit(solution)/shard_map/ppermute | solution.py:318

commit v8 on v7

--- a/solution.py
+++ b/solution.py
@@ -68,13 +68,10 @@
     return lax.dot_general(weights, rows, (((1,), (1,)), ((), ())), preferred_element_type=F32)
 
 
-def pack_kernel(counts_ref, place_ref, mass_ref, packed_ref, keep_ref):
+def pack_kernel(rows_ref, packed_ref, keep_ref):
     for z in range(2):
-        mass = mass_ref[0, 0, z : z + 1, :]
-        keep = lax.broadcasted_iota(jnp.int32, mass.shape, 1) < counts_ref[0, :, z : z + 1]
-        rows = [place_ref[c, 0, 0, z : z + 1, :] for c in range(3)]
-        packed_ref[z] = jnp.concatenate(rows + [jnp.where(keep, mass, 0.0)], axis=0)
-        keep_ref[z] = jnp.broadcast_to(jnp.where(keep, 1.0, 0.0), keep_ref.shape[1:])
+        packed_ref[z] = jnp.concatenate([rows_ref[c, z : z + 1, :] for c in range(4)], axis=0)
+        keep_ref[z] = jnp.broadcast_to(rows_ref[4, z : z + 1, :], keep_ref.shape[1:])
 
 
 def ahead(axis):
@@ -290,13 +287,15 @@
     bins = jax.ShapeDtypeStruct((2, 4, slots), F32)
     full = jax.ShapeDtypeStruct(positions.shape, F32)
     running = jax.ShapeDtypeStruct((2, slots, 32), F32)
+    present = lax.broadcasted_iota(jnp.int32, mass.shape, 3) < counts[..., None]
+    rows = [positions, jnp.where(present, mass, 0.0)[None], jnp.where(present, 1.0, 0.0).astype(F32)[None]]
     packed, keep = pl.pallas_call(
         pack_kernel,
         out_shape=(bins, bins),
-        in_specs=[VMEM] * 3,
+        in_specs=[VMEM],
         out_specs=(VMEM, VMEM),
         compiler_params=pltpu.CompilerParams(vmem_limit_bytes=8 * 1024 * 1024),
-    )(counts, positions, mass)
+    )(jnp.concatenate(rows, axis=0).reshape(5, 2, slots))
     speed = velocities
     upper = lax.rem(lax.axis_index("gz"), 2)
     for subcycle in range(SUBCYCLES):

time: 32 us -> 30.8 us (0.963)
  local copies, waits for them, and re-layouts: 2.11 us -> 0.72 us
    unnamed x16, local copies, waits for them, and re-layouts: 2.08 us -> 0.69 us
  transfers between devices with their start and end apart: 12 -> 12, of which waited for: 5 -> 5; matrix products, arithmetic and copies ran while one was open for 0% -> 0% of each run, Pallas kernels for 30% -> 31%
where the time goes in v8:
time: 30.8 us; the launch traced here: 30.6 us
  starting transfers between devices  14.1 us (46%)
  Pallas kernels  12.4 us (40%)
  waiting for transfers between devices  2.47 us (8%)
  between operations  0.82 us (3%)
  local copies, waits for them, and re-layouts  0.72 us (2%)
    pallas_call x8, Pallas kernels, call(): pl.pallas_call(kernel, out_shape=outputs, in_specs=[VMEM] * len(inputs),...  12.4 us
    ppermute x2, starting transfers between devices, on_device(): planes = [packed] + [lax.ppermute(packed, 'gy', path) for path in paths]  4.32 us
    ppermute x2, starting transfers between devices, on_device(): lax.ppermute(lax.dynamic_index_in_dim(slab, upper, 1, False), 'gz', far)  4.06 us
    ppermute x2, starting transfers between devices, on_device(): lax.ppermute(lax.dynamic_index_in_dim(slab, 1 - upper, 1, False), 'gz', n...  2.38 us
    ppermute x2, starting transfers between devices, on_device(): lax.ppermute(packed, 'gx', far)  2.04 us
    ppermute x2, starting transfers between devices, across(): return lax.ppermute(value, ('gx', 'gy'), pairs)  1.21 us
    ppermute x2, waiting for transfers between devices, across(): return lax.ppermute(value, ('gx', 'gy'), pairs)  0.98 us
    ppermute x2, waiting for transfers between devices, on_device(): planes = [packed] + [lax.ppermute(packed, 'gy', path) for path in paths]  0.81 us
  transfers between devices with their start and end apart: 12, of which 5 were waited for; matrix products, arithmetic and copies ran while one was open for 0% of the time, Pallas kernels for 31%

profile of v8, /device:TPU:0, one launch (start us, length us, event | category | flops | bytes accessed | tf_op | source)
XLA Modules:
  0.0 30.6 jit_solution(10638548942255724104)
XLA Ops:
  0.6 0.0 copy-start.2
  0.6 0.0 copy-start.3
  0.6 0.0 copy-start.1
  0.7 0.6 %copy-done.2 = s32[1,1,2]{2,1,0:T(1,128)S(1)} copy-done((s32[1,1,2]{2,1,0:T(1,128)S(1)}, s32[1,1,2]{2,1,0:T(1,128)}, u32[]{:S(2)}) %copy-start.2) | copy-done | bytes 32
  1.3 0.1 compare_select_fusion
  1.4 0.0 copy-done.3
  1.4 0.1 fusion
  1.4 0.0 copy-done.1
  1.5 3.0 %collective-permute-start = (f32[2,4,256]{2,1,0:T(4,128)S(1)}, f32[2,4,256]{2,1,0:T(4,128)S(1)}, u32[]{:S(2)}, u32[]{:S(2)}) collective-permute-start(f32[2,4,256]{2,1,0:T(4,128)S(1)} %get-tuple-element.11.refs_0_.own_ref), channel_id=1, source_target_pairs={{0,4},{4,0},{1,5},{5,1},{2,6},{6,2},{3,7},{7,3},{8,12},{12,8},{9,1... | collective-permute-start | bytes 24584 | tf_op jit(solution)/shard_map/ppermute | solution.py:304
  4.5 0.6 %collective-permute-start.2 = (f32[2,4,256]{2,1,0:T(4,128)S(1)}, f32[2,4,256]{2,1,0:T(4,128)S(1)}, u32[]{:S(2)}, u32[]{:S(2)}) collective-permute-start(f32[2,4,256]{2,1,0:T(4,128)S(1)} %get-tuple-element.11.refs_0_.own_ref), channel_id=1, source_target_pairs={{0,28},{4,24},{8,20},{12,16},{16,12},{20,8},{24,4},{28,0},{1,29},{... | collective-permute-start | bytes 24584 | tf_op jit(solution)/shard_map/ppermute | solution.py:263
  5.1 0.7 %collective-permute-start.3 = (f32[2,4,256]{2,1,0:T(4,128)S(1)}, f32[2,4,256]{2,1,0:T(4,128)S(1)}, u32[]{:S(2)}, u32[]{:S(2)}) collective-permute-start(f32[2,4,256]{2,1,0:T(4,128)S(1)} %get-tuple-element.11.refs_0_.own_ref), channel_id=1, source_target_pairs={{0,24},{8,16},{16,8},{24,0},{1,25},{9,17},{17,9},{25,1},{2,26},{10... | collective-permute-start | bytes 24584 | tf_op jit(solution)/shard_map/ppermute | solution.py:306
  5.8 0.4 %collective-permute-done.refs_1_ = f32[2,4,256]{2,1,0:T(4,128)S(1)} collective-permute-done((f32[2,4,256]{2,1,0:T(4,128)S(1)}, f32[2,4,256]{2,1,0:T(4,128)S(1)}, u32[]{:S(2)}, u32[]{:S(2)}) %collective-permute-start) | collective-permute-done | bytes 8224 | tf_op jit(solution)/shard_map/ppermute | solution.py:304
  6.1 0.1 collective-permute-start.1
  6.2 1.4 %shard_map.63 = (bf16[2,256,48]{2,1,0:T(8,128)(2,1)S(1)}, f32[2,256,32]{2,1,0:T(8,128)S(1)}) custom-call(f32[2,4,256]{2,1,0:T(4,128)S(1)} %get-tuple-element.11.refs_0_.own_ref, f32[2,4,256]{2,1,0:T(4,128)S(1)} %collective-permute-done.refs_1_), custom_call_target="tpu_custom_call" | custom-call | flops 786432000 | bytes 262144 | tf_op jit(solution)/shard_map/pallas_call | solution.py:269
  7.6 0.0 collective-permute-done.1.near_x_ref
  7.6 0.9 %collective-permute-done.2.refs_0_ = f32[2,4,256]{2,1,0:T(4,128)S(1)} collective-permute-done((f32[2,4,256]{2,1,0:T(4,128)S(1)}, f32[2,4,256]{2,1,0:T(4,128)S(1)}, u32[]{:S(2)}, u32[]{:S(2)}) %collective-permute-start.2) | collective-permute-done | bytes 8224 | tf_op jit(solution)/shard_map/ppermute | solution.py:263
  8.5 0.0 collective-permute-done.3.refs_1_
  8.5 1.6 %collective-permute-start.4 = (f32[6,4,256]{2,1,0:T(4,128)S(1)}, f32[6,4,256]{2,1,0:T(4,128)S(1)}, u32[]{:S(2)}, u32[]{:S(2)}) collective-permute-start(f32[6,4,256]{2,1,0:T(4,128)S(1)} %get-tuple-element.21), channel_id=1, source_target_pairs={{0,1},{1,0},{2,3},{3,2},{4,5},{5,4},{6,7},{7,6},{8,9},{9,8},{10,11... | collective-permute-start | bytes 73736 | tf_op jit(solution)/shard_map/ppermute | solution.py:318
  10.1 2.5 %collective-permute-start.5 = (f32[6,4,256]{2,1,0:T(4,128)S(1)}, f32[6,4,256]{2,1,0:T(4,128)S(1)}, u32[]{:S(2)}, u32[]{:S(2)}) collective-permute-start(f32[6,4,256]{2,1,0:T(4,128)S(1)} %get-tuple-element.20), channel_id=1, source_target_pairs={{0,3},{1,2},{2,1},{3,0},{4,7},{5,6},{6,5},{7,4},{8,11},{9,10},{10,... | collective-permute-start | bytes 73736 | tf_op jit(solution)/shard_map/ppermute | solution.py:317
  12.6 0.0 copy-start
  12.6 2.2 %shard_map.64.before_ref = f32[2,256,32]{2,1,0:T(8,128)S(1)} custom-call(bf16[2,256,48]{2,1,0:T(8,128)(2,1)S(1)} %get-tuple-element.12.target_ref, f32[2,256,32]{2,1,0:T(8,128)S(1)} %get-tuple-element.13.before_ref, f32[2,2,4,256]{3,2,1,0:T(4,128)S(1)} %collective-permute-done.1.near_x_ref, f32[2,4,256]{2,1,0:T(4,128)S(1)} %collective-permute-done.2.refs_0_, ...), custom_call_target="tpu_custom_call" | custom-call | flops 1572864000 | bytes 262144 | tf_op jit(solution)/shard_map/pallas_call | solution.py:269
  14.8 0.0 collective-permute-done.4.source_ref
  14.8 0.0 copy-done
  14.8 1.2 %shard_map.65.bin_ref = f32[2,4,256]{2,1,0:T(4,128)S(1)} custom-call(f32[3,1,1,2,256]{4,3,2,1,0:T(2,128)S(1)} %copy-done, f32[2,4,256]{2,1,0:T(4,128)S(1)} %get-tuple-element.11.refs_0_.own_ref, bf16[2,256,48]{2,1,0:T(8,128)(2,1)S(1)} %get-tuple-element.12.target_ref, f32[2,256,32]{2,1,0:T(8,128)S(1)} %shard_map.64.before_ref, ...), custom_call_target="tpu_custom_call" | custom-call | flops 589824000 | bytes 262144 | tf_op jit(solution)/shard_map/pallas_call | solution.py:269
  16.0 0.0 collective-permute-done.5.source_ref
  16.0 1.2 %shard_map.66 = (f32[2,4,256]{2,1,0:T(4,128)S(1)}, f32[2,4,256]{2,1,0:T(4,128)S(1)}) custom-call(f32[2,4,256]{2,1,0:T(4,128)S(1)} %get-tuple-element.10.keep_ref, f32[2,4,256]{2,1,0:T(4,128)S(1)} %shard_map.65.bin_ref, f32[3,1,1,2,256]{4,3,2,1,0:T(2,128)S(1)} %copy-done, f32[2,4,256]{2,1,0:T(4,128)S(1)} %get-tuple-element.11.refs_0_.own_ref, ...), custom_call_target="tpu_custom_call" | custom-call | flops 589824000 | bytes 262144 | tf_op jit(solution)/shard_map/pallas_call | solution.py:269
  17.2 1.3 %collective-permute-start.6 = (f32[2,4,256]{2,1,0:T(4,128)S(1)}, f32[2,4,256]{2,1,0:T(4,128)S(1)}, u32[]{:S(2)}, u32[]{:S(2)}) collective-permute-start(f32[2,4,256]{2,1,0:T(4,128)S(1)} %get-tuple-element.15.refs_0_.own_ref), channel_id=1, source_target_pairs={{0,4},{4,0},{1,5},{5,1},{2,6},{6,2},{3,7},{7,3},{8,12},{12,8},{9,1... | collective-permute-start | bytes 24584 | tf_op jit(solution)/shard_map/ppermute | solution.py:304
  18.5 0.6 %collective-permute-start.8 = (f32[2,4,256]{2,1,0:T(4,128)S(1)}, f32[2,4,256]{2,1,0:T(4,128)S(1)}, u32[]{:S(2)}, u32[]{:S(2)}) collective-permute-start(f32[2,4,256]{2,1,0:T(4,128)S(1)} %get-tuple-element.15.refs_0_.own_ref), channel_id=1, source_target_pairs={{0,28},{4,24},{8,20},{12,16},{16,12},{20,8},{24,4},{28,0},{1,29},{... | collective-permute-start | bytes 24584 | tf_op jit(solution)/shard_map/ppermute | solution.py:263
  19.1 1.4 %collective-permute-start.9 = (f32[2,4,256]{2,1,0:T(4,128)S(1)}, f32[2,4,256]{2,1,0:T(4,128)S(1)}, u32[]{:S(2)}, u32[]{:S(2)}) collective-permute-start(f32[2,4,256]{2,1,0:T(4,128)S(1)} %get-tuple-element.15.refs_0_.own_ref), channel_id=1, source_target_pairs={{0,24},{8,16},{16,8},{24,0},{1,25},{9,17},{17,9},{25,1},{2,26},{10... | collective-permute-start | bytes 24584 | tf_op jit(solution)/shard_map/ppermute | solution.py:306
  20.5 0.4 %collective-permute-done.6.refs_1_ = f32[2,4,256]{2,1,0:T(4,128)S(1)} collective-permute-done((f32[2,4,256]{2,1,0:T(4,128)S(1)}, f32[2,4,256]{2,1,0:T(4,128)S(1)}, u32[]{:S(2)}, u32[]{:S(2)}) %collective-permute-start.6) | collective-permute-done | bytes 8224 | tf_op jit(solution)/shard_map/ppermute | solution.py:304
  20.9 0.0 collective-permute-start.7
  20.9 1.4 %shard_map.67 = (bf16[2,256,48]{2,1,0:T(8,128)(2,1)S(1)}, f32[2,256,32]{2,1,0:T(8,128)S(1)}) custom-call(f32[2,4,256]{2,1,0:T(4,128)S(1)} %get-tuple-element.15.refs_0_.own_ref, f32[2,4,256]{2,1,0:T(4,128)S(1)} %collective-permute-done.6.refs_1_), custom_call_target="tpu_custom_call" | custom-call | flops 786432000 | bytes 262144 | tf_op jit(solution)/shard_map/pallas_call | solution.py:269
  22.3 0.0 collective-permute-done.7.near_x_ref
  22.3 0.1 collective-permute-done.8.refs_0_
  22.5 0.0 collective-permute-done.9.refs_1_
  22.5 0.7 %collective-permute-start.10 = (f32[6,4,256]{2,1,0:T(4,128)S(1)}, f32[6,4,256]{2,1,0:T(4,128)S(1)}, u32[]{:S(2)}, u32[]{:S(2)}) collective-permute-start(f32[6,4,256]{2,1,0:T(4,128)S(1)} %get-tuple-element.19), channel_id=1, source_target_pairs={{0,1},{1,0},{2,3},{3,2},{4,5},{5,4},{6,7},{7,6},{8,9},{9,8},{10,11... | collective-permute-start | bytes 73736 | tf_op jit(solution)/shard_map/ppermute | solution.py:318
  23.2 1.6 %collective-permute-start.11 = (f32[6,4,256]{2,1,0:T(4,128)S(1)}, f32[6,4,256]{2,1,0:T(4,128)S(1)}, u32[]{:S(2)}, u32[]{:S(2)}) collective-permute-start(f32[6,4,256]{2,1,0:T(4,128)S(1)} %get-tuple-element.18), channel_id=1, source_target_pairs={{0,3},{1,2},{2,1},{3,0},{4,7},{5,6},{6,5},{7,4},{8,11},{9,10},{10,... | collective-permute-start | bytes 73736 | tf_op jit(solution)/shard_map/ppermute | solution.py:317
  24.8 2.2 %shard_map.68.before_ref = f32[2,256,32]{2,1,0:T(8,128)S(1)} custom-call(bf16[2,256,48]{2,1,0:T(8,128)(2,1)S(1)} %get-tuple-element.16.target_ref, f32[2,256,32]{2,1,0:T(8,128)S(1)} %get-tuple-element.17.before_ref, f32[2,2,4,256]{3,2,1,0:T(4,128)S(1)} %collective-permute-done.7.near_x_ref, f32[2,4,256]{2,1,0:T(4,128)S(1)} %collective-permute-done.8.refs_0_, ...), custom_call_target="tpu_custom_call" | custom-call | flops 1572864000 | bytes 262144 | tf_op jit(solution)/shard_map/pallas_call | solution.py:269
  27.0 0.0 collective-permute-done.10.source_ref
  27.0 1.1 %shard_map.69.bin_ref = f32[2,4,256]{2,1,0:T(4,128)S(1)} custom-call(f32[2,4,256]{2,1,0:T(4,128)S(1)} %get-tuple-element.14.speed_ref, f32[2,4,256]{2,1,0:T(4,128)S(1)} %get-tuple-element.15.refs_0_.own_ref, bf16[2,256,48]{2,1,0:T(8,128)(2,1)S(1)} %get-tuple-element.16.target_ref, f32[2,256,32]{2,1,0:T(8,128)S(1)} %shard_map.68.before_ref, ...), custom_call_target="tpu_custom_call" | custom-call | flops 589824000 | bytes 262144 | tf_op jit(solution)/shard_map/pallas_call | solution.py:269
  28.2 0.7 %collective-permute-done.11.source_ref = f32[6,4,256]{2,1,0:T(4,128)S(1)} collective-permute-done((f32[6,4,256]{2,1,0:T(4,128)S(1)}, f32[6,4,256]{2,1,0:T(4,128)S(1)}, u32[]{:S(2)}, u32[]{:S(2)}) %collective-permute-start.11) | collective-permute-done | bytes 24608 | tf_op jit(solution)/shard_map/ppermute | solution.py:317
  28.9 1.8 %shard_map.70 = (f32[3,1,1,2,256]{4,3,2,1,0:T(2,128)}, f32[3,1,1,2,256]{4,3,2,1,0:T(2,128)}) custom-call(f32[2,4,256]{2,1,0:T(4,128)S(1)} %get-tuple-element.10.keep_ref, f32[2,4,256]{2,1,0:T(4,128)S(1)} %shard_map.69.bin_ref, f32[2,4,256]{2,1,0:T(4,128)S(1)} %get-tuple-element.14.speed_ref, f32[2,4,256]{2,1,0:T(4,128)S(1)} %get-tuple-element.15.refs_0_.own_ref, ...), custom_call_target="tpu_custom_call" | custom-call | flops 589824000 | bytes 262144 | tf_op jit(solution)/shard_map/pallas_call | solution.py:269
  (16 shorter events, 0.1 us)
Async XLA Ops:
  0.6 0.7 %copy-start.2 = (s32[1,1,2]{2,1,0:T(1,128)S(1)}, s32[1,1,2]{2,1,0:T(1,128)}, u32[]{:S(2)}) copy-start(s32[1,1,2]{2,1,0:T(1,128)} %param.7) | copy-start | bytes 28
  0.6 0.7 %copy-start.3 = (f32[1,1,2,256]{3,2,1,0:T(2,128)S(1)}, f32[1,1,2,256]{3,2,1,0:T(2,128)}, u32[]{:S(2)}) copy-start(f32[1,1,2,256]{3,2,1,0:T(2,128)} %param.6) | copy-start | bytes 6148
  0.6 0.8 %copy-start.1 = (f32[3,1,1,2,256]{4,3,2,1,0:T(2,128)S(1)}, f32[3,1,1,2,256]{4,3,2,1,0:T(2,128)}, u32[]{:S(2)}) copy-start(f32[3,1,1,2,256]{4,3,2,1,0:T(2,128)} %param.4) | copy-start | bytes 18436
  1.5 4.7 %collective-permute-start = (f32[2,4,256]{2,1,0:T(4,128)S(1)}, f32[2,4,256]{2,1,0:T(4,128)S(1)}, u32[]{:S(2)}, u32[]{:S(2)}) collective-permute-start(f32[2,4,256]{2,1,0:T(4,128)S(1)} %get-tuple-element.11.refs_0_.own_ref), channel_id=1, source_target_pairs={{0,4},{4,0},{1,5},{5,1},{2,6},{6,2},{3,7},{7,3},{8,12},{12,8},{9,1... | collective-permute-start | bytes 24584 | tf_op jit(solution)/shard_map/ppermute | solution.py:304
  4.5 4.0 %collective-permute-start.2 = (f32[2,4,256]{2,1,0:T(4,128)S(1)}, f32[2,4,256]{2,1,0:T(4,128)S(1)}, u32[]{:S(2)}, u32[]{:S(2)}) collective-permute-start(f32[2,4,256]{2,1,0:T(4,128)S(1)} %get-tuple-element.11.refs_0_.own_ref), channel_id=1, source_target_pairs={{0,28},{4,24},{8,20},{12,16},{16,12},{20,8},{24,4},{28,0},{1,29},{... | collective-permute-start | bytes 24584 | tf_op jit(solution)/shard_map/ppermute | solution.py:263
  5.1 3.4 %collective-permute-start.3 = (f32[2,4,256]{2,1,0:T(4,128)S(1)}, f32[2,4,256]{2,1,0:T(4,128)S(1)}, u32[]{:S(2)}, u32[]{:S(2)}) collective-permute-start(f32[2,4,256]{2,1,0:T(4,128)S(1)} %get-tuple-element.11.refs_0_.own_ref), channel_id=1, source_target_pairs={{0,24},{8,16},{16,8},{24,0},{1,25},{9,17},{17,9},{25,1},{2,26},{10... | collective-permute-start | bytes 24584 | tf_op jit(solution)/shard_map/ppermute | solution.py:306
  6.1 1.4 %collective-permute-start.1 = (f32[2,2,4,256]{3,2,1,0:T(4,128)S(1)}, f32[2,2,4,256]{3,2,1,0:T(4,128)S(1)}, u32[]{:S(2)}, u32[]{:S(2)}) collective-permute-start(f32[2,2,4,256]{3,2,1,0:T(4,128)S(1)} %pad_maximum_fusion), channel_id=1, source_target_pairs={{0,8},{8,0},{16,24},{24,16},{1,9},{9,1},{17,25},{25,17},{2,10},{10... | collective-permute-start | bytes 49160 | tf_op jit(solution)/shard_map/ppermute | solution.py:308
  8.5 6.3 %collective-permute-start.4 = (f32[6,4,256]{2,1,0:T(4,128)S(1)}, f32[6,4,256]{2,1,0:T(4,128)S(1)}, u32[]{:S(2)}, u32[]{:S(2)}) collective-permute-start(f32[6,4,256]{2,1,0:T(4,128)S(1)} %get-tuple-element.21), channel_id=1, source_target_pairs={{0,1},{1,0},{2,3},{3,2},{4,5},{5,4},{6,7},{7,6},{8,9},{9,8},{10,11... | collective-permute-start | bytes 73736 | tf_op jit(solution)/shard_map/ppermute | solution.py:318
  10.1 5.9 %collective-permute-start.5 = (f32[6,4,256]{2,1,0:T(4,128)S(1)}, f32[6,4,256]{2,1,0:T(4,128)S(1)}, u32[]{:S(2)}, u32[]{:S(2)}) collective-permute-start(f32[6,4,256]{2,1,0:T(4,128)S(1)} %get-tuple-element.20), channel_id=1, source_target_pairs={{0,3},{1,2},{2,1},{3,0},{4,7},{5,6},{6,5},{7,4},{8,11},{9,10},{10,... | collective-permute-start | bytes 73736 | tf_op jit(solution)/shard_map/ppermute | solution.py:317
  12.6 2.2 %copy-start = (f32[3,1,1,2,256]{4,3,2,1,0:T(2,128)S(1)}, f32[3,1,1,2,256]{4,3,2,1,0:T(2,128)}, u32[]{:S(2)}) copy-start(f32[3,1,1,2,256]{4,3,2,1,0:T(2,128)} %speed_ref.3) | copy-start | bytes 18436
  17.2 3.7 %collective-permute-start.6 = (f32[2,4,256]{2,1,0:T(4,128)S(1)}, f32[2,4,256]{2,1,0:T(4,128)S(1)}, u32[]{:S(2)}, u32[]{:S(2)}) collective-permute-start(f32[2,4,256]{2,1,0:T(4,128)S(1)} %get-tuple-element.15.refs_0_.own_ref), channel_id=1, source_target_pairs={{0,4},{4,0},{1,5},{5,1},{2,6},{6,2},{3,7},{7,3},{8,12},{12,8},{9,1... | collective-permute-start | bytes 24584 | tf_op jit(solution)/shard_map/ppermute | solution.py:304
  18.5 4.0 %collective-permute-start.8 = (f32[2,4,256]{2,1,0:T(4,128)S(1)}, f32[2,4,256]{2,1,0:T(4,128)S(1)}, u32[]{:S(2)}, u32[]{:S(2)}) collective-permute-start(f32[2,4,256]{2,1,0:T(4,128)S(1)} %get-tuple-element.15.refs_0_.own_ref), channel_id=1, source_target_pairs={{0,28},{4,24},{8,20},{12,16},{16,12},{20,8},{24,4},{28,0},{1,29},{... | collective-permute-start | bytes 24584 | tf_op jit(solution)/shard_map/ppermute | solution.py:263
  19.1 3.4 %collective-permute-start.9 = (f32[2,4,256]{2,1,0:T(4,128)S(1)}, f32[2,4,256]{2,1,0:T(4,128)S(1)}, u32[]{:S(2)}, u32[]{:S(2)}) collective-permute-start(f32[2,4,256]{2,1,0:T(4,128)S(1)} %get-tuple-element.15.refs_0_.own_ref), channel_id=1, source_target_pairs={{0,24},{8,16},{16,8},{24,0},{1,25},{9,17},{17,9},{25,1},{2,26},{10... | collective-permute-start | bytes 24584 | tf_op jit(solution)/shard_map/ppermute | solution.py:306
  20.9 1.4 %collective-permute-start.7 = (f32[2,2,4,256]{3,2,1,0:T(4,128)S(1)}, f32[2,2,4,256]{3,2,1,0:T(4,128)S(1)}, u32[]{:S(2)}, u32[]{:S(2)}) collective-permute-start(f32[2,2,4,256]{3,2,1,0:T(4,128)S(1)} %pad_maximum_fusion.1), channel_id=1, source_target_pairs={{0,8},{8,0},{16,24},{24,16},{1,9},{9,1},{17,25},{25,17},{2,10},{10... | collective-permute-start | bytes 49160 | tf_op jit(solution)/shard_map/ppermute | solution.py:308
  22.5 4.5 %collective-permute-start.10 = (f32[6,4,256]{2,1,0:T(4,128)S(1)}, f32[6,4,256]{2,1,0:T(4,128)S(1)}, u32[]{:S(2)}, u32[]{:S(2)}) collective-permute-start(f32[6,4,256]{2,1,0:T(4,128)S(1)} %get-tuple-element.19), channel_id=1, source_target_pairs={{0,1},{1,0},{2,3},{3,2},{4,5},{5,4},{6,7},{7,6},{8,9},{9,8},{10,11... | collective-permute-start | bytes 73736 | tf_op jit(solution)/shard_map/ppermute | solution.py:318
  23.2 5.6 %collective-permute-start.11 = (f32[6,4,256]{2,1,0:T(4,128)S(1)}, f32[6,4,256]{2,1,0:T(4,128)S(1)}, u32[]{:S(2)}, u32[]{:S(2)}) collective-permute-start(f32[6,4,256]{2,1,0:T(4,128)S(1)} %get-tuple-element.18), channel_id=1, source_target_pairs={{0,3},{1,2},{2,1},{3,0},{4,7},{5,6},{6,5},{7,4},{8,11},{9,10},{10,... | collective-permute-start | bytes 73736 | tf_op jit(solution)/shard_map/ppermute | solution.py:317

commit v9 on v8

--- a/solution.py
+++ b/solution.py
@@ -107,6 +107,7 @@
     if len(entries) % 2:
         place = place + half
     known = {}
+    tile_rows = jnp.zeros((8, half), F32)
     for number, (ref, index, offset) in enumerate(entries):
         tail = held[number]
         key = (id(ref),) + (index if isinstance(index, tuple) else (index,))
@@ -117,9 +118,11 @@
         tile, turn = lax.div(place, half), lax.rem(place, half)
         tail = jnp.where(lane < length, jnp.concatenate([tail, jnp.zeros_like(tail)], axis=0), 0.0)
         tail = pltpu.roll(tail, turn, 1)
-        list_ref[tile] += jnp.where(lane >= turn, tail, 0.0)
-        list_ref[tile + 1] += jnp.where(lane < turn, tail, 0.0)
+        upto = tile_rows + jnp.where(lane >= turn, tail, 0.0)
+        list_ref[tile] = upto
         place = place + length
+        tile_rows = jnp.where(turn + length >= half, jnp.where(lane < turn, tail, 0.0), upto)
+    list_ref[lax.div(place, half)] = tile_rows
     done = (len(entries) // 2) * 2 * half
     for chunk in range((near_ref.shape[1] - done) // (2 * half)):
         distance, summed = source_rows(list_chunk(list_ref, chunk))

time: 30.8 us -> 30.7 us (level)
  no operation moved by 1% of the time
where the time goes in v9:
time: 30.7 us; the launch traced here: 30.5 us
  starting transfers between devices  14.1 us (46%)
  Pallas kernels  12.2 us (40%)
  waiting for transfers between devices  2.48 us (8%)
  between operations  0.82 us (3%)
  local copies, waits for them, and re-layouts  0.72 us (2%)
    pallas_call x8, Pallas kernels, call(): pl.pallas_call(kernel, out_shape=outputs, in_specs=[VMEM] * len(inputs),...  12.2 us
    ppermute x2, starting transfers between devices, on_device(): planes = [packed] + [lax.ppermute(packed, 'gy', path) for path in paths]  4.29 us
    ppermute x2, starting transfers between devices, on_device(): lax.ppermute(lax.dynamic_index_in_dim(slab, upper, 1, False), 'gz', far)  4.12 us
    ppermute x2, starting transfers between devices, on_device(): lax.ppermute(lax.dynamic_index_in_dim(slab, 1 - upper, 1, False), 'gz', n...  2.39 us
    ppermute x2, starting transfers between devices, on_device(): lax.ppermute(packed, 'gx', far)  2.05 us
    ppermute x2, starting transfers between devices, across(): return lax.ppermute(value, ('gx', 'gy'), pairs)  1.22 us
    ppermute x2, waiting for transfers between devices, across(): return lax.ppermute(value, ('gx', 'gy'), pairs)  1.02 us
    ppermute x2, waiting for transfers between devices, on_device(): planes = [packed] + [lax.ppermute(packed, 'gy', path) for path in paths]  0.81 us
  transfers between devices with their start and end apart: 12, of which 5 were waited for; matrix products, arithmetic and copies ran while one was open for 0% of the time, Pallas kernels for 31%

profile of v9, /device:TPU:0, one launch (start us, length us, event | category | flops | bytes accessed | tf_op | source)
XLA Modules:
  0.0 30.5 jit_solution(15776449420566876748)
XLA Ops:
  0.6 0.0 copy-start.2
  0.6 0.0 copy-start.3
  0.6 0.0 copy-start.1
  0.7 0.6 %copy-done.2 = s32[1,1,2]{2,1,0:T(1,128)S(1)} copy-done((s32[1,1,2]{2,1,0:T(1,128)S(1)}, s32[1,1,2]{2,1,0:T(1,128)}, u32[]{:S(2)}) %copy-start.2) | copy-done | bytes 32
  1.3 0.1 compare_select_fusion
  1.4 0.0 copy-done.3
  1.4 0.1 fusion
  1.4 0.0 copy-done.1
  1.5 3.0 %collective-permute-start = (f32[2,4,256]{2,1,0:T(4,128)S(1)}, f32[2,4,256]{2,1,0:T(4,128)S(1)}, u32[]{:S(2)}, u32[]{:S(2)}) collective-permute-start(f32[2,4,256]{2,1,0:T(4,128)S(1)} %get-tuple-element.11.refs_0_.own_ref), channel_id=1, source_target_pairs={{0,4},{4,0},{1,5},{5,1},{2,6},{6,2},{3,7},{7,3},{8,12},{12,8},{9,1... | collective-permute-start | bytes 24584 | tf_op jit(solution)/shard_map/ppermute | solution.py:307
  4.5 0.6 %collective-permute-start.2 = (f32[2,4,256]{2,1,0:T(4,128)S(1)}, f32[2,4,256]{2,1,0:T(4,128)S(1)}, u32[]{:S(2)}, u32[]{:S(2)}) collective-permute-start(f32[2,4,256]{2,1,0:T(4,128)S(1)} %get-tuple-element.11.refs_0_.own_ref), channel_id=1, source_target_pairs={{0,28},{4,24},{8,20},{12,16},{16,12},{20,8},{24,4},{28,0},{1,29},{... | collective-permute-start | bytes 24584 | tf_op jit(solution)/shard_map/ppermute | solution.py:266
  5.1 0.7 %collective-permute-start.3 = (f32[2,4,256]{2,1,0:T(4,128)S(1)}, f32[2,4,256]{2,1,0:T(4,128)S(1)}, u32[]{:S(2)}, u32[]{:S(2)}) collective-permute-start(f32[2,4,256]{2,1,0:T(4,128)S(1)} %get-tuple-element.11.refs_0_.own_ref), channel_id=1, source_target_pairs={{0,24},{8,16},{16,8},{24,0},{1,25},{9,17},{17,9},{25,1},{2,26},{10... | collective-permute-start | bytes 24584 | tf_op jit(solution)/shard_map/ppermute | solution.py:309
  5.8 0.4 %collective-permute-done.refs_1_ = f32[2,4,256]{2,1,0:T(4,128)S(1)} collective-permute-done((f32[2,4,256]{2,1,0:T(4,128)S(1)}, f32[2,4,256]{2,1,0:T(4,128)S(1)}, u32[]{:S(2)}, u32[]{:S(2)}) %collective-permute-start) | collective-permute-done | bytes 8224 | tf_op jit(solution)/shard_map/ppermute | solution.py:307
  6.1 0.1 collective-permute-start.1
  6.2 1.3 %shard_map.63 = (bf16[2,256,48]{2,1,0:T(8,128)(2,1)S(1)}, f32[2,256,32]{2,1,0:T(8,128)S(1)}) custom-call(f32[2,4,256]{2,1,0:T(4,128)S(1)} %get-tuple-element.11.refs_0_.own_ref, f32[2,4,256]{2,1,0:T(4,128)S(1)} %collective-permute-done.refs_1_), custom_call_target="tpu_custom_call" | custom-call | flops 786432000 | bytes 262144 | tf_op jit(solution)/shard_map/pallas_call | solution.py:272
  7.5 0.0 collective-permute-done.1.near_x_ref
  7.6 0.9 %collective-permute-done.2.refs_0_ = f32[2,4,256]{2,1,0:T(4,128)S(1)} collective-permute-done((f32[2,4,256]{2,1,0:T(4,128)S(1)}, f32[2,4,256]{2,1,0:T(4,128)S(1)}, u32[]{:S(2)}, u32[]{:S(2)}) %collective-permute-start.2) | collective-permute-done | bytes 8224 | tf_op jit(solution)/shard_map/ppermute | solution.py:266
  8.5 0.0 collective-permute-done.3.refs_1_
  8.5 1.6 %collective-permute-start.4 = (f32[6,4,256]{2,1,0:T(4,128)S(1)}, f32[6,4,256]{2,1,0:T(4,128)S(1)}, u32[]{:S(2)}, u32[]{:S(2)}) collective-permute-start(f32[6,4,256]{2,1,0:T(4,128)S(1)} %get-tuple-element.21), channel_id=1, source_target_pairs={{0,1},{1,0},{2,3},{3,2},{4,5},{5,4},{6,7},{7,6},{8,9},{9,8},{10,11... | collective-permute-start | bytes 73736 | tf_op jit(solution)/shard_map/ppermute | solution.py:321
  10.1 2.5 %collective-permute-start.5 = (f32[6,4,256]{2,1,0:T(4,128)S(1)}, f32[6,4,256]{2,1,0:T(4,128)S(1)}, u32[]{:S(2)}, u32[]{:S(2)}) collective-permute-start(f32[6,4,256]{2,1,0:T(4,128)S(1)} %get-tuple-element.20), channel_id=1, source_target_pairs={{0,3},{1,2},{2,1},{3,0},{4,7},{5,6},{6,5},{7,4},{8,11},{9,10},{10,... | collective-permute-start | bytes 73736 | tf_op jit(solution)/shard_map/ppermute | solution.py:320
  12.6 0.0 copy-start
  12.6 2.2 %shard_map.64.before_ref = f32[2,256,32]{2,1,0:T(8,128)S(1)} custom-call(bf16[2,256,48]{2,1,0:T(8,128)(2,1)S(1)} %get-tuple-element.12.target_ref, f32[2,256,32]{2,1,0:T(8,128)S(1)} %get-tuple-element.13.before_ref, f32[2,2,4,256]{3,2,1,0:T(4,128)S(1)} %collective-permute-done.1.near_x_ref, f32[2,4,256]{2,1,0:T(4,128)S(1)} %collective-permute-done.2.refs_0_, ...), custom_call_target="tpu_custom_call" | custom-call | flops 1572864000 | bytes 262144 | tf_op jit(solution)/shard_map/pallas_call | solution.py:272
  14.8 0.0 collective-permute-done.4.source_ref
  14.8 0.0 copy-done
  14.8 1.1 %shard_map.65.bin_ref = f32[2,4,256]{2,1,0:T(4,128)S(1)} custom-call(f32[3,1,1,2,256]{4,3,2,1,0:T(2,128)S(1)} %copy-done, f32[2,4,256]{2,1,0:T(4,128)S(1)} %get-tuple-element.11.refs_0_.own_ref, bf16[2,256,48]{2,1,0:T(8,128)(2,1)S(1)} %get-tuple-element.12.target_ref, f32[2,256,32]{2,1,0:T(8,128)S(1)} %shard_map.64.before_ref, ...), custom_call_target="tpu_custom_call" | custom-call | flops 589824000 | bytes 262144 | tf_op jit(solution)/shard_map/pallas_call | solution.py:272
  16.0 0.0 collective-permute-done.5.source_ref
  16.0 1.1 %shard_map.66 = (f32[2,4,256]{2,1,0:T(4,128)S(1)}, f32[2,4,256]{2,1,0:T(4,128)S(1)}) custom-call(f32[2,4,256]{2,1,0:T(4,128)S(1)} %get-tuple-element.10.keep_ref, f32[2,4,256]{2,1,0:T(4,128)S(1)} %shard_map.65.bin_ref, f32[3,1,1,2,256]{4,3,2,1,0:T(2,128)S(1)} %copy-done, f32[2,4,256]{2,1,0:T(4,128)S(1)} %get-tuple-element.11.refs_0_.own_ref, ...), custom_call_target="tpu_custom_call" | custom-call | flops 589824000 | bytes 262144 | tf_op jit(solution)/shard_map/pallas_call | solution.py:272
  17.1 1.3 %collective-permute-start.6 = (f32[2,4,256]{2,1,0:T(4,128)S(1)}, f32[2,4,256]{2,1,0:T(4,128)S(1)}, u32[]{:S(2)}, u32[]{:S(2)}) collective-permute-start(f32[2,4,256]{2,1,0:T(4,128)S(1)} %get-tuple-element.15.refs_0_.own_ref), channel_id=1, source_target_pairs={{0,4},{4,0},{1,5},{5,1},{2,6},{6,2},{3,7},{7,3},{8,12},{12,8},{9,1... | collective-permute-start | bytes 24584 | tf_op jit(solution)/shard_map/ppermute | solution.py:307
  18.4 0.6 %collective-permute-start.8 = (f32[2,4,256]{2,1,0:T(4,128)S(1)}, f32[2,4,256]{2,1,0:T(4,128)S(1)}, u32[]{:S(2)}, u32[]{:S(2)}) collective-permute-start(f32[2,4,256]{2,1,0:T(4,128)S(1)} %get-tuple-element.15.refs_0_.own_ref), channel_id=1, source_target_pairs={{0,28},{4,24},{8,20},{12,16},{16,12},{20,8},{24,4},{28,0},{1,29},{... | collective-permute-start | bytes 24584 | tf_op jit(solution)/shard_map/ppermute | solution.py:266
  19.0 1.4 %collective-permute-start.9 = (f32[2,4,256]{2,1,0:T(4,128)S(1)}, f32[2,4,256]{2,1,0:T(4,128)S(1)}, u32[]{:S(2)}, u32[]{:S(2)}) collective-permute-start(f32[2,4,256]{2,1,0:T(4,128)S(1)} %get-tuple-element.15.refs_0_.own_ref), channel_id=1, source_target_pairs={{0,24},{8,16},{16,8},{24,0},{1,25},{9,17},{17,9},{25,1},{2,26},{10... | collective-permute-start | bytes 24584 | tf_op jit(solution)/shard_map/ppermute | solution.py:309
  20.4 0.4 %collective-permute-done.6.refs_1_ = f32[2,4,256]{2,1,0:T(4,128)S(1)} collective-permute-done((f32[2,4,256]{2,1,0:T(4,128)S(1)}, f32[2,4,256]{2,1,0:T(4,128)S(1)}, u32[]{:S(2)}, u32[]{:S(2)}) %collective-permute-start.6) | collective-permute-done | bytes 8224 | tf_op jit(solution)/shard_map/ppermute | solution.py:307
  20.9 0.0 collective-permute-start.7
  20.9 1.3 %shard_map.67 = (bf16[2,256,48]{2,1,0:T(8,128)(2,1)S(1)}, f32[2,256,32]{2,1,0:T(8,128)S(1)}) custom-call(f32[2,4,256]{2,1,0:T(4,128)S(1)} %get-tuple-element.15.refs_0_.own_ref, f32[2,4,256]{2,1,0:T(4,128)S(1)} %collective-permute-done.6.refs_1_), custom_call_target="tpu_custom_call" | custom-call | flops 786432000 | bytes 262144 | tf_op jit(solution)/shard_map/pallas_call | solution.py:272
  22.2 0.0 collective-permute-done.7.near_x_ref
  22.3 0.1 collective-permute-done.8.refs_0_
  22.4 0.0 collective-permute-done.9.refs_1_
  22.4 0.7 %collective-permute-start.10 = (f32[6,4,256]{2,1,0:T(4,128)S(1)}, f32[6,4,256]{2,1,0:T(4,128)S(1)}, u32[]{:S(2)}, u32[]{:S(2)}) collective-permute-start(f32[6,4,256]{2,1,0:T(4,128)S(1)} %get-tuple-element.19), channel_id=1, source_target_pairs={{0,1},{1,0},{2,3},{3,2},{4,5},{5,4},{6,7},{7,6},{8,9},{9,8},{10,11... | collective-permute-start | bytes 73736 | tf_op jit(solution)/shard_map/ppermute | solution.py:321
  23.1 1.6 %collective-permute-start.11 = (f32[6,4,256]{2,1,0:T(4,128)S(1)}, f32[6,4,256]{2,1,0:T(4,128)S(1)}, u32[]{:S(2)}, u32[]{:S(2)}) collective-permute-start(f32[6,4,256]{2,1,0:T(4,128)S(1)} %get-tuple-element.18), channel_id=1, source_target_pairs={{0,3},{1,2},{2,1},{3,0},{4,7},{5,6},{6,5},{7,4},{8,11},{9,10},{10,... | collective-permute-start | bytes 73736 | tf_op jit(solution)/shard_map/ppermute | solution.py:320
  24.8 2.2 %shard_map.68.before_ref = f32[2,256,32]{2,1,0:T(8,128)S(1)} custom-call(bf16[2,256,48]{2,1,0:T(8,128)(2,1)S(1)} %get-tuple-element.16.target_ref, f32[2,256,32]{2,1,0:T(8,128)S(1)} %get-tuple-element.17.before_ref, f32[2,2,4,256]{3,2,1,0:T(4,128)S(1)} %collective-permute-done.7.near_x_ref, f32[2,4,256]{2,1,0:T(4,128)S(1)} %collective-permute-done.8.refs_0_, ...), custom_call_target="tpu_custom_call" | custom-call | flops 1572864000 | bytes 262144 | tf_op jit(solution)/shard_map/pallas_call | solution.py:272
  27.0 0.0 collective-permute-done.10.source_ref
  27.0 1.1 %shard_map.69.bin_ref = f32[2,4,256]{2,1,0:T(4,128)S(1)} custom-call(f32[2,4,256]{2,1,0:T(4,128)S(1)} %get-tuple-element.14.speed_ref, f32[2,4,256]{2,1,0:T(4,128)S(1)} %get-tuple-element.15.refs_0_.own_ref, bf16[2,256,48]{2,1,0:T(8,128)(2,1)S(1)} %get-tuple-element.16.target_ref, f32[2,256,32]{2,1,0:T(8,128)S(1)} %shard_map.68.before_ref, ...), custom_call_target="tpu_custom_call" | custom-call | flops 589824000 | bytes 262144 | tf_op jit(solution)/shard_map/pallas_call | solution.py:272
  28.1 0.6 %collective-permute-done.11.source_ref = f32[6,4,256]{2,1,0:T(4,128)S(1)} collective-permute-done((f32[6,4,256]{2,1,0:T(4,128)S(1)}, f32[6,4,256]{2,1,0:T(4,128)S(1)}, u32[]{:S(2)}, u32[]{:S(2)}) %collective-permute-start.11) | collective-permute-done | bytes 24608 | tf_op jit(solution)/shard_map/ppermute | solution.py:320
  28.8 1.7 %shard_map.70 = (f32[3,1,1,2,256]{4,3,2,1,0:T(2,128)}, f32[3,1,1,2,256]{4,3,2,1,0:T(2,128)}) custom-call(f32[2,4,256]{2,1,0:T(4,128)S(1)} %get-tuple-element.10.keep_ref, f32[2,4,256]{2,1,0:T(4,128)S(1)} %shard_map.69.bin_ref, f32[2,4,256]{2,1,0:T(4,128)S(1)} %get-tuple-element.14.speed_ref, f32[2,4,256]{2,1,0:T(4,128)S(1)} %get-tuple-element.15.refs_0_.own_ref, ...), custom_call_target="tpu_custom_call" | custom-call | flops 589824000 | bytes 262144 | tf_op jit(solution)/shard_map/pallas_call | solution.py:272
  (16 shorter events, 0.1 us)
Async XLA Ops:
  0.6 0.7 %copy-start.2 = (s32[1,1,2]{2,1,0:T(1,128)S(1)}, s32[1,1,2]{2,1,0:T(1,128)}, u32[]{:S(2)}) copy-start(s32[1,1,2]{2,1,0:T(1,128)} %param.7) | copy-start | bytes 28
  0.6 0.7 %copy-start.3 = (f32[1,1,2,256]{3,2,1,0:T(2,128)S(1)}, f32[1,1,2,256]{3,2,1,0:T(2,128)}, u32[]{:S(2)}) copy-start(f32[1,1,2,256]{3,2,1,0:T(2,128)} %param.6) | copy-start | bytes 6148
  0.6 0.8 %copy-start.1 = (f32[3,1,1,2,256]{4,3,2,1,0:T(2,128)S(1)}, f32[3,1,1,2,256]{4,3,2,1,0:T(2,128)}, u32[]{:S(2)}) copy-start(f32[3,1,1,2,256]{4,3,2,1,0:T(2,128)} %param.4) | copy-start | bytes 18436
  1.5 4.7 %collective-permute-start = (f32[2,4,256]{2,1,0:T(4,128)S(1)}, f32[2,4,256]{2,1,0:T(4,128)S(1)}, u32[]{:S(2)}, u32[]{:S(2)}) collective-permute-start(f32[2,4,256]{2,1,0:T(4,128)S(1)} %get-tuple-element.11.refs_0_.own_ref), channel_id=1, source_target_pairs={{0,4},{4,0},{1,5},{5,1},{2,6},{6,2},{3,7},{7,3},{8,12},{12,8},{9,1... | collective-permute-start | bytes 24584 | tf_op jit(solution)/shard_map/ppermute | solution.py:307
  4.5 4.0 %collective-permute-start.2 = (f32[2,4,256]{2,1,0:T(4,128)S(1)}, f32[2,4,256]{2,1,0:T(4,128)S(1)}, u32[]{:S(2)}, u32[]{:S(2)}) collective-permute-start(f32[2,4,256]{2,1,0:T(4,128)S(1)} %get-tuple-element.11.refs_0_.own_ref), channel_id=1, source_target_pairs={{0,28},{4,24},{8,20},{12,16},{16,12},{20,8},{24,4},{28,0},{1,29},{... | collective-permute-start | bytes 24584 | tf_op jit(solution)/shard_map/ppermute | solution.py:266
  5.1 3.4 %collective-permute-start.3 = (f32[2,4,256]{2,1,0:T(4,128)S(1)}, f32[2,4,256]{2,1,0:T(4,128)S(1)}, u32[]{:S(2)}, u32[]{:S(2)}) collective-permute-start(f32[2,4,256]{2,1,0:T(4,128)S(1)} %get-tuple-element.11.refs_0_.own_ref), channel_id=1, source_target_pairs={{0,24},{8,16},{16,8},{24,0},{1,25},{9,17},{17,9},{25,1},{2,26},{10... | collective-permute-start | bytes 24584 | tf_op jit(solution)/shard_map/ppermute | solution.py:309
  6.1 1.4 %collective-permute-start.1 = (f32[2,2,4,256]{3,2,1,0:T(4,128)S(1)}, f32[2,2,4,256]{3,2,1,0:T(4,128)S(1)}, u32[]{:S(2)}, u32[]{:S(2)}) collective-permute-start(f32[2,2,4,256]{3,2,1,0:T(4,128)S(1)} %pad_maximum_fusion), channel_id=1, source_target_pairs={{0,8},{8,0},{16,24},{24,16},{1,9},{9,1},{17,25},{25,17},{2,10},{10... | collective-permute-start | bytes 49160 | tf_op jit(solution)/shard_map/ppermute | solution.py:311
  8.5 6.3 %collective-permute-start.4 = (f32[6,4,256]{2,1,0:T(4,128)S(1)}, f32[6,4,256]{2,1,0:T(4,128)S(1)}, u32[]{:S(2)}, u32[]{:S(2)}) collective-permute-start(f32[6,4,256]{2,1,0:T(4,128)S(1)} %get-tuple-element.21), channel_id=1, source_target_pairs={{0,1},{1,0},{2,3},{3,2},{4,5},{5,4},{6,7},{7,6},{8,9},{9,8},{10,11... | collective-permute-start | bytes 73736 | tf_op jit(solution)/shard_map/ppermute | solution.py:321
  10.1 5.8 %collective-permute-start.5 = (f32[6,4,256]{2,1,0:T(4,128)S(1)}, f32[6,4,256]{2,1,0:T(4,128)S(1)}, u32[]{:S(2)}, u32[]{:S(2)}) collective-permute-start(f32[6,4,256]{2,1,0:T(4,128)S(1)} %get-tuple-element.20), channel_id=1, source_target_pairs={{0,3},{1,2},{2,1},{3,0},{4,7},{5,6},{6,5},{7,4},{8,11},{9,10},{10,... | collective-permute-start | bytes 73736 | tf_op jit(solution)/shard_map/ppermute | solution.py:320
  12.6 2.2 %copy-start = (f32[3,1,1,2,256]{4,3,2,1,0:T(2,128)S(1)}, f32[3,1,1,2,256]{4,3,2,1,0:T(2,128)}, u32[]{:S(2)}) copy-start(f32[3,1,1,2,256]{4,3,2,1,0:T(2,128)} %speed_ref.3) | copy-start | bytes 18436
  17.1 3.7 %collective-permute-start.6 = (f32[2,4,256]{2,1,0:T(4,128)S(1)}, f32[2,4,256]{2,1,0:T(4,128)S(1)}, u32[]{:S(2)}, u32[]{:S(2)}) collective-permute-start(f32[2,4,256]{2,1,0:T(4,128)S(1)} %get-tuple-element.15.refs_0_.own_ref), channel_id=1, source_target_pairs={{0,4},{4,0},{1,5},{5,1},{2,6},{6,2},{3,7},{7,3},{8,12},{12,8},{9,1... | collective-permute-start | bytes 24584 | tf_op jit(solution)/shard_map/ppermute | solution.py:307
  18.4 4.0 %collective-permute-start.8 = (f32[2,4,256]{2,1,0:T(4,128)S(1)}, f32[2,4,256]{2,1,0:T(4,128)S(1)}, u32[]{:S(2)}, u32[]{:S(2)}) collective-permute-start(f32[2,4,256]{2,1,0:T(4,128)S(1)} %get-tuple-element.15.refs_0_.own_ref), channel_id=1, source_target_pairs={{0,28},{4,24},{8,20},{12,16},{16,12},{20,8},{24,4},{28,0},{1,29},{... | collective-permute-start | bytes 24584 | tf_op jit(solution)/shard_map/ppermute | solution.py:266
  19.0 3.4 %collective-permute-start.9 = (f32[2,4,256]{2,1,0:T(4,128)S(1)}, f32[2,4,256]{2,1,0:T(4,128)S(1)}, u32[]{:S(2)}, u32[]{:S(2)}) collective-permute-start(f32[2,4,256]{2,1,0:T(4,128)S(1)} %get-tuple-element.15.refs_0_.own_ref), channel_id=1, source_target_pairs={{0,24},{8,16},{16,8},{24,0},{1,25},{9,17},{17,9},{25,1},{2,26},{10... | collective-permute-start | bytes 24584 | tf_op jit(solution)/shard_map/ppermute | solution.py:309
  20.9 1.4 %collective-permute-start.7 = (f32[2,2,4,256]{3,2,1,0:T(4,128)S(1)}, f32[2,2,4,256]{3,2,1,0:T(4,128)S(1)}, u32[]{:S(2)}, u32[]{:S(2)}) collective-permute-start(f32[2,2,4,256]{3,2,1,0:T(4,128)S(1)} %pad_maximum_fusion.1), channel_id=1, source_target_pairs={{0,8},{8,0},{16,24},{24,16},{1,9},{9,1},{17,25},{25,17},{2,10},{10... | collective-permute-start | bytes 49160 | tf_op jit(solution)/shard_map/ppermute | solution.py:311
  22.4 4.6 %collective-permute-start.10 = (f32[6,4,256]{2,1,0:T(4,128)S(1)}, f32[6,4,256]{2,1,0:T(4,128)S(1)}, u32[]{:S(2)}, u32[]{:S(2)}) collective-permute-start(f32[6,4,256]{2,1,0:T(4,128)S(1)} %get-tuple-element.19), channel_id=1, source_target_pairs={{0,1},{1,0},{2,3},{3,2},{4,5},{5,4},{6,7},{7,6},{8,9},{9,8},{10,11... | collective-permute-start | bytes 73736 | tf_op jit(solution)/shard_map/ppermute | solution.py:321
  23.1 5.6 %collective-permute-start.11 = (f32[6,4,256]{2,1,0:T(4,128)S(1)}, f32[6,4,256]{2,1,0:T(4,128)S(1)}, u32[]{:S(2)}, u32[]{:S(2)}) collective-permute-start(f32[6,4,256]{2,1,0:T(4,128)S(1)} %get-tuple-element.18), channel_id=1, source_target_pairs={{0,3},{1,2},{2,1},{3,0},{4,7},{5,6},{6,5},{7,4},{8,11},{9,10},{10,... | collective-permute-start | bytes 73736 | tf_op jit(solution)/shard_map/ppermute | solution.py:320

commit v10 on v9

--- a/solution.py
+++ b/solution.py
@@ -163,33 +163,32 @@
     return lax.fori_loop(done, jnp.maximum(lax.div(length + (wide - 1), wide), done), rest, tuple(totals))
 
 
-def plane_kernel(size_y, *refs):
-    planes, (target_ref, total_ref, near_ref, sum_ref, list_ref) = refs[:-5], refs[-5:]
-    own_ref = planes[0]
+def pair_kernel(own_ref, near_x_ref, target_ref, total_ref, near_ref, sum_ref, list_ref):
     for z in range(2):
         target_ref[z] = target_rows(shifted(own_ref[z], (0, 0, z)))
-    entries = []
-    for ref, shifts in zip(planes, y_shifts(size_y)):
-        for y in shifts:
-            entries += [(ref, z, (0, y, z)) for z in range(2)]
+    entries = [(own_ref, z, (0, 0, z)) for z in range(2)] + [(near_x_ref, z, (ahead("gx"), 0, z)) for z in range(2)]
     length = fill(near_ref, sum_ref, list_ref, entries)
     zero = jnp.zeros(total_ref.shape[1:], F32)
     targets = [target_ref[z] for z in range(2)]
-    totals = sums_over(targets, (zero, zero), near_ref, sum_ref, list_ref, length, len(entries), 5)
+    totals = sums_over(targets, (zero, zero), near_ref, sum_ref, list_ref, length, len(entries), 3)
     for z in range(2):
         total_ref[z] = totals[z]
 
 
-def slab_kernel(size_y, target_ref, before_ref, near_x_ref, *refs):
-    far_refs, (total_ref, near_ref, sum_ref, list_ref) = refs[:-4], refs[-4:]
-    entries = []
-    for plane, shifts in enumerate(y_shifts(size_y)):
+def slab_kernel(size_y, target_ref, before_ref, *refs):
+    others, (total_ref, near_ref, sum_ref, list_ref) = refs[:-4], refs[-4:]
+    planes = len(others) // 2
+    far_ref = others[planes]
+    entries = [(far_ref, (0, z), (-ahead("gx"), 0, z)) for z in range(2)]
+    for plane, shifts in enumerate(y_shifts(size_y)[1:]):
         for y in shifts:
-            entries += [(near_x_ref, (plane, z), (ahead("gx"), y, z)) for z in range(2)]
-            entries += [(far_refs[plane - 1], z, (-ahead("gx"), y, z)) for z in range(2)]
+            for z in range(2):
+                entries.append((others[plane], (0, z), (0, y, z)))
+                entries.append((others[plane], (1, z), (ahead("gx"), y, z)))
+                entries.append((others[planes + 1 + plane], z, (-ahead("gx"), y, z)))
     length = fill(near_ref, sum_ref, list_ref, entries)
     targets = [target_ref[z] for z in range(2)]
-    totals = sums_over(targets, (before_ref[0], before_ref[1]), near_ref, sum_ref, list_ref, length, len(entries), 9)
+    totals = sums_over(targets, (before_ref[0], before_ref[1]), near_ref, sum_ref, list_ref, length, len(entries), 10)
     for z in range(2):
         total_ref[z] = totals[z]
 
@@ -199,7 +198,7 @@
     for column, x in enumerate((0, ahead("gx"), -ahead("gx"))):
         for plane, shifts in enumerate(y_shifts(size_y)):
             planes = len(y_shifts(size_y))
-            index = column * planes + (plane if column < 2 else (plane - 1) % planes)
+            index = 2 * plane + column if column < 2 else 2 * planes + plane
             entries += [(source_ref, index, (x, y, 3 * z - 1)) for y in shifts]
     length = fill(near_ref, sum_ref, list_ref, entries)
     (total,) = sums_over([target_ref[z]], (before_ref[z],), near_ref, sum_ref, list_ref, length, len(entries), 7)
@@ -304,26 +303,27 @@
     for subcycle in range(SUBCYCLES):
         first, last = subcycle == 0, subcycle == SUBCYCLES - 1
         paths = swaps("gy")[: min(size_y, 3) - 1]
-        planes = [packed] + [lax.ppermute(packed, "gy", path) for path in paths]
         near, far = swaps("gx")
-        far_planes = [across(packed, far, path) for path in paths] + [lax.ppermute(packed, "gx", far)]
-        plane = jnp.stack(planes)
-        near_x = lax.ppermute(plane, "gx", near)
+        near_x = lax.ppermute(packed, "gx", near)
+        corners = [across(packed, far, path) for path in paths]
+        pair = jnp.stack([packed, near_x])
+        along_y = [lax.ppermute(pair, "gy", path) for path in paths]
+        far_x = lax.ppermute(pair, "gx", far)
         targets, total = call(
-            functools.partial(plane_kernel, size_y),
-            planes,
+            pair_kernel,
+            [packed, near_x],
             (jax.ShapeDtypeStruct((2, slots, 48), BF16), running),
-            6, 2, slots, 2,
+            4, 2, slots, 1,
         )
-        slab = jnp.concatenate([plane, near_x] + [value[None] for value in far_planes], axis=0)
+        slab = jnp.concatenate([pair] + along_y + [far_x[:1]] + [value[None] for value in corners], axis=0)
         near, far = swaps("gz")
         far_z = lax.ppermute(lax.dynamic_index_in_dim(slab, upper, 1, False), "gz", far)
         near_z = lax.ppermute(lax.dynamic_index_in_dim(slab, 1 - upper, 1, False), "gz", near)
         (total,) = call(
             functools.partial(slab_kernel, size_y),
-            [targets, total, near_x] + far_planes,
+            [targets, total] + along_y + [far_x] + corners,
             (running,),
-            12, 2, slots, 3,
+            14, 2, slots, 3,
         )
         state = [speed, packed, targets, total]
         (half_done,) = call(

time: 30.7 us -> 32.7 us (1.065)
  waiting for transfers between devices: 2.48 us -> 4.49 us
  starting transfers between devices: 14.1 us -> 14.6 us
  Pallas kernels: 12.2 us -> 11.8 us
    ppermute x2, starting transfers between devices: 1.22 us -> 5.17 us  [across(): return lax.ppermute(value, ('gx', 'gy'), pairs)]
    ppermute x6, starting transfers between devices: 6.4 us -> 3.14 us  [the longest x2 1.66 us: on_device(): along_y = [lax.ppermute(pair, 'gy', path) for path in paths]]
    ppermute x6, waiting for transfers between devices: 0.82 us -> 3.85 us  [the longest x2 3.22 us: on_device(): along_y = [lax.ppermute(pair, 'gy', path) for path in paths]]
    ppermute x2, waiting for transfers between devices: 1.02 us -> 0.01 us  [across(): return lax.ppermute(value, ('gx', 'gy'), pairs)]
    pallas_call x8, Pallas kernels: 12.2 us -> 11.8 us  [call(): pl.pallas_call(kernel, out_shape=outputs, in_specs=[VMEM] * len(inputs),...]
  transfers between devices with their start and end apart: 12 -> 12, of which waited for: 5 -> 5; matrix products, arithmetic and copies ran while one was open for 0% -> 0% of each run, Pallas kernels for 31% -> 27%
where the time goes in v10:
time: 32.7 us; the launch traced here: 32.5 us
  starting transfers between devices  14.6 us (45%)
  Pallas kernels  11.8 us (36%)
  waiting for transfers between devices  4.49 us (14%)
  between operations  0.8 us (2%)
  local copies, waits for them, and re-layouts  0.72 us (2%)
    pallas_call x8, Pallas kernels, call(): pl.pallas_call(kernel, out_shape=outputs, in_specs=[VMEM] * len(inputs),...  11.8 us
    ppermute x2, starting transfers between devices, across(): return lax.ppermute(value, ('gx', 'gy'), pairs)  5.17 us
    ppermute x2, starting transfers between devices, on_device(): lax.ppermute(lax.dynamic_index_in_dim(slab, upper, 1, False), 'gz', far)  3.89 us
    ppermute x2, waiting for transfers between devices, on_device(): along_y = [lax.ppermute(pair, 'gy', path) for path in paths]  3.22 us
    ppermute x2, starting transfers between devices, on_device(): lax.ppermute(lax.dynamic_index_in_dim(slab, 1 - upper, 1, False), 'gz', n...  2.38 us
    ppermute x2, starting transfers between devices, on_device(): along_y = [lax.ppermute(pair, 'gy', path) for path in paths]  1.66 us
    ppermute x2, starting transfers between devices, on_device(): far_x = lax.ppermute(pair, 'gx', far)  0.89 us
    unnamed x16, local copies, waits for them, and re-layouts  0.69 us
  transfers between devices with their start and end apart: 12, of which 5 were waited for; matrix products, arithmetic and copies ran while one was open for 0% of the time, Pallas kernels for 27%

profile of v10, /device:TPU:0, one launch (start us, length us, event | category | flops | bytes accessed | tf_op | source)
XLA Modules:
  0.0 32.5 jit_solution(1091479154902223786)
XLA Ops:
  0.6 0.0 copy-start.2
  0.6 0.0 copy-start.3
  0.6 0.0 copy-start.1
  0.7 0.6 %copy-done.2 = s32[1,1,2]{2,1,0:T(1,128)S(1)} copy-done((s32[1,1,2]{2,1,0:T(1,128)S(1)}, s32[1,1,2]{2,1,0:T(1,128)}, u32[]{:S(2)}) %copy-start.2) | copy-done | bytes 32
  1.3 0.1 compare_select_fusion
  1.4 0.0 copy-done.3
  1.4 0.1 fusion
  1.4 0.0 copy-done.1
  1.5 0.5 %collective-permute-start = (f32[2,4,256]{2,1,0:T(4,128)S(1)}, f32[2,4,256]{2,1,0:T(4,128)S(1)}, u32[]{:S(2)}, u32[]{:S(2)}) collective-permute-start(f32[2,4,256]{2,1,0:T(4,128)S(1)} %get-tuple-element.11.own_ref), channel_id=1, source_target_pairs={{0,8},{8,0},{16,24},{24,16},{1,9},{9,1},{17,25},{25,17},{2,10},{10... | collective-permute-start | bytes 24584 | tf_op jit(solution)/shard_map/ppermute | solution.py:307
  2.0 3.6 %collective-permute-start.3 = (f32[2,4,256]{2,1,0:T(4,128)S(1)}, f32[2,4,256]{2,1,0:T(4,128)S(1)}, u32[]{:S(2)}, u32[]{:S(2)}) collective-permute-start(f32[2,4,256]{2,1,0:T(4,128)S(1)} %get-tuple-element.11.own_ref), channel_id=1, source_target_pairs={{0,28},{4,24},{8,20},{12,16},{16,12},{20,8},{24,4},{28,0},{1,29},{... | collective-permute-start | bytes 24584 | tf_op jit(solution)/shard_map/ppermute | solution.py:265
  5.6 0.0 collective-permute-done.near_x_ref
  5.6 0.6 %collective-permute-start.1 = (f32[2,2,4,256]{3,2,1,0:T(4,128)S(1)}, f32[2,2,4,256]{3,2,1,0:T(4,128)S(1)}, u32[]{:S(2)}, u32[]{:S(2)}) collective-permute-start(f32[2,2,4,256]{3,2,1,0:T(4,128)S(1)} %pad_maximum_fusion), channel_id=1, source_target_pairs={{0,4},{4,0},{1,5},{5,1},{2,6},{6,2},{3,7},{7,3},{8,12},{12,8},{9,1... | collective-permute-start | bytes 49160 | tf_op jit(solution)/shard_map/ppermute | solution.py:310
  6.1 0.5 %collective-permute-start.2 = (f32[2,2,4,256]{3,2,1,0:T(4,128)S(1)}, f32[2,2,4,256]{3,2,1,0:T(4,128)S(1)}, u32[]{:S(2)}, u32[]{:S(2)}) collective-permute-start(f32[2,2,4,256]{3,2,1,0:T(4,128)S(1)} %pad_maximum_fusion), channel_id=1, source_target_pairs={{0,24},{8,16},{16,8},{24,0},{1,25},{9,17},{17,9},{25,1},{2,26},{10... | collective-permute-start | bytes 49160 | tf_op jit(solution)/shard_map/ppermute | solution.py:311
  6.7 0.9 %shard_map.63 = (bf16[2,256,48]{2,1,0:T(8,128)(2,1)S(1)}, f32[2,256,32]{2,1,0:T(8,128)S(1)}) custom-call(f32[2,4,256]{2,1,0:T(4,128)S(1)} %get-tuple-element.11.own_ref, f32[2,4,256]{2,1,0:T(4,128)S(1)} %collective-permute-done.near_x_ref), custom_call_target="tpu_custom_call" | custom-call | flops 524288000 | bytes 262144 | tf_op jit(solution)/shard_map/pallas_call | solution.py:271
  7.6 1.8 %collective-permute-done.1.refs_0_ = f32[2,2,4,256]{3,2,1,0:T(4,128)S(1)} collective-permute-done((f32[2,2,4,256]{3,2,1,0:T(4,128)S(1)}, f32[2,2,4,256]{3,2,1,0:T(4,128)S(1)}, u32[]{:S(2)}, u32[]{:S(2)}) %collective-permute-start.1) | collective-permute-done | bytes 16416 | tf_op jit(solution)/shard_map/ppermute | solution.py:310
  9.4 0.1 collective-permute-done.2.refs_1_
  9.4 0.0 collective-permute-done.3.refs_2_
  9.5 1.6 %collective-permute-start.4 = (f32[6,4,256]{2,1,0:T(4,128)S(1)}, f32[6,4,256]{2,1,0:T(4,128)S(1)}, u32[]{:S(2)}, u32[]{:S(2)}) collective-permute-start(f32[6,4,256]{2,1,0:T(4,128)S(1)} %get-tuple-element.21), channel_id=1, source_target_pairs={{0,1},{1,0},{2,3},{3,2},{4,5},{5,4},{6,7},{7,6},{8,9},{9,8},{10,11... | collective-permute-start | bytes 73736 | tf_op jit(solution)/shard_map/ppermute | solution.py:321
  11.1 2.5 %collective-permute-start.5 = (f32[6,4,256]{2,1,0:T(4,128)S(1)}, f32[6,4,256]{2,1,0:T(4,128)S(1)}, u32[]{:S(2)}, u32[]{:S(2)}) collective-permute-start(f32[6,4,256]{2,1,0:T(4,128)S(1)} %get-tuple-element.20), channel_id=1, source_target_pairs={{0,3},{1,2},{2,1},{3,0},{4,7},{5,6},{6,5},{7,4},{8,11},{9,10},{10,... | collective-permute-start | bytes 73736 | tf_op jit(solution)/shard_map/ppermute | solution.py:320
  13.6 0.0 copy-start
  13.6 2.4 %shard_map.64.before_ref = f32[2,256,32]{2,1,0:T(8,128)S(1)} custom-call(bf16[2,256,48]{2,1,0:T(8,128)(2,1)S(1)} %get-tuple-element.12.target_ref, f32[2,256,32]{2,1,0:T(8,128)S(1)} %get-tuple-element.13.before_ref, f32[2,2,4,256]{3,2,1,0:T(4,128)S(1)} %collective-permute-done.1.refs_0_, f32[2,2,4,256]{3,2,1,0:T(4,128)S(1)} %collective-permute-done.2.refs_1_, ...), custom_call_target="tpu_custom_call" | custom-call | flops 1835008000 | bytes 262144 | tf_op jit(solution)/shard_map/pallas_call | solution.py:271
  16.0 0.0 collective-permute-done.4.source_ref
  16.0 0.0 copy-done
  16.0 1.1 %shard_map.65.bin_ref = f32[2,4,256]{2,1,0:T(4,128)S(1)} custom-call(f32[3,1,1,2,256]{4,3,2,1,0:T(2,128)S(1)} %copy-done, f32[2,4,256]{2,1,0:T(4,128)S(1)} %get-tuple-element.11.own_ref, bf16[2,256,48]{2,1,0:T(8,128)(2,1)S(1)} %get-tuple-element.12.target_ref, f32[2,256,32]{2,1,0:T(8,128)S(1)} %shard_map.64.before_ref, ...), custom_call_target="tpu_custom_call" | custom-call | flops 589824000 | bytes 262144 | tf_op jit(solution)/shard_map/pallas_call | solution.py:271
  17.2 0.0 collective-permute-done.5.source_ref
  17.2 1.1 %shard_map.66 = (f32[2,4,256]{2,1,0:T(4,128)S(1)}, f32[2,4,256]{2,1,0:T(4,128)S(1)}) custom-call(f32[2,4,256]{2,1,0:T(4,128)S(1)} %get-tuple-element.10.keep_ref, f32[2,4,256]{2,1,0:T(4,128)S(1)} %shard_map.65.bin_ref, f32[3,1,1,2,256]{4,3,2,1,0:T(2,128)S(1)} %copy-done, f32[2,4,256]{2,1,0:T(4,128)S(1)} %get-tuple-element.11.own_ref, ...), custom_call_target="tpu_custom_call" | custom-call | flops 589824000 | bytes 262144 | tf_op jit(solution)/shard_map/pallas_call | solution.py:271
  18.3 0.1 collective-permute-start.6
  18.4 1.6 %collective-permute-start.9 = (f32[2,4,256]{2,1,0:T(4,128)S(1)}, f32[2,4,256]{2,1,0:T(4,128)S(1)}, u32[]{:S(2)}, u32[]{:S(2)}) collective-permute-start(f32[2,4,256]{2,1,0:T(4,128)S(1)} %get-tuple-element.15.own_ref), channel_id=1, source_target_pairs={{0,28},{4,24},{8,20},{12,16},{16,12},{20,8},{24,4},{28,0},{1,29},{... | collective-permute-start | bytes 24584 | tf_op jit(solution)/shard_map/ppermute | solution.py:265
  20.0 0.0 collective-permute-done.6.near_x_ref
  20.0 1.1 %collective-permute-start.7 = (f32[2,2,4,256]{3,2,1,0:T(4,128)S(1)}, f32[2,2,4,256]{3,2,1,0:T(4,128)S(1)}, u32[]{:S(2)}, u32[]{:S(2)}) collective-permute-start(f32[2,2,4,256]{3,2,1,0:T(4,128)S(1)} %pad_maximum_fusion.1), channel_id=1, source_target_pairs={{0,4},{4,0},{1,5},{5,1},{2,6},{6,2},{3,7},{7,3},{8,12},{12,8},{9,1... | collective-permute-start | bytes 49160 | tf_op jit(solution)/shard_map/ppermute | solution.py:310
  21.1 0.4 %collective-permute-start.8 = (f32[2,2,4,256]{3,2,1,0:T(4,128)S(1)}, f32[2,2,4,256]{3,2,1,0:T(4,128)S(1)}, u32[]{:S(2)}, u32[]{:S(2)}) collective-permute-start(f32[2,2,4,256]{3,2,1,0:T(4,128)S(1)} %pad_maximum_fusion.1), channel_id=1, source_target_pairs={{0,24},{8,16},{16,8},{24,0},{1,25},{9,17},{17,9},{25,1},{2,26},{10... | collective-permute-start | bytes 49160 | tf_op jit(solution)/shard_map/ppermute | solution.py:311
  21.5 0.9 %shard_map.67 = (bf16[2,256,48]{2,1,0:T(8,128)(2,1)S(1)}, f32[2,256,32]{2,1,0:T(8,128)S(1)}) custom-call(f32[2,4,256]{2,1,0:T(4,128)S(1)} %get-tuple-element.15.own_ref, f32[2,4,256]{2,1,0:T(4,128)S(1)} %collective-permute-done.6.near_x_ref), custom_call_target="tpu_custom_call" | custom-call | flops 524288000 | bytes 262144 | tf_op jit(solution)/shard_map/pallas_call | solution.py:271
  22.4 1.4 %collective-permute-done.7.refs_0_ = f32[2,2,4,256]{3,2,1,0:T(4,128)S(1)} collective-permute-done((f32[2,2,4,256]{3,2,1,0:T(4,128)S(1)}, f32[2,2,4,256]{3,2,1,0:T(4,128)S(1)}, u32[]{:S(2)}, u32[]{:S(2)}) %collective-permute-start.7) | collective-permute-done | bytes 16416 | tf_op jit(solution)/shard_map/ppermute | solution.py:310
  23.8 0.6 %collective-permute-done.8.refs_1_ = f32[2,2,4,256]{3,2,1,0:T(4,128)S(1)} collective-permute-done((f32[2,2,4,256]{3,2,1,0:T(4,128)S(1)}, f32[2,2,4,256]{3,2,1,0:T(4,128)S(1)}, u32[]{:S(2)}, u32[]{:S(2)}) %collective-permute-start.8) | collective-permute-done | bytes 16416 | tf_op jit(solution)/shard_map/ppermute | solution.py:311
  24.4 0.0 collective-permute-done.9.refs_2_
  24.4 0.7 %collective-permute-start.10 = (f32[6,4,256]{2,1,0:T(4,128)S(1)}, f32[6,4,256]{2,1,0:T(4,128)S(1)}, u32[]{:S(2)}, u32[]{:S(2)}) collective-permute-start(f32[6,4,256]{2,1,0:T(4,128)S(1)} %get-tuple-element.19), channel_id=1, source_target_pairs={{0,1},{1,0},{2,3},{3,2},{4,5},{5,4},{6,7},{7,6},{8,9},{9,8},{10,11... | collective-permute-start | bytes 73736 | tf_op jit(solution)/shard_map/ppermute | solution.py:321
  25.2 1.4 %collective-permute-start.11 = (f32[6,4,256]{2,1,0:T(4,128)S(1)}, f32[6,4,256]{2,1,0:T(4,128)S(1)}, u32[]{:S(2)}, u32[]{:S(2)}) collective-permute-start(f32[6,4,256]{2,1,0:T(4,128)S(1)} %get-tuple-element.18), channel_id=1, source_target_pairs={{0,3},{1,2},{2,1},{3,0},{4,7},{5,6},{6,5},{7,4},{8,11},{9,10},{10,... | collective-permute-start | bytes 73736 | tf_op jit(solution)/shard_map/ppermute | solution.py:320
  26.6 2.4 %shard_map.68.before_ref = f32[2,256,32]{2,1,0:T(8,128)S(1)} custom-call(bf16[2,256,48]{2,1,0:T(8,128)(2,1)S(1)} %get-tuple-element.16.target_ref, f32[2,256,32]{2,1,0:T(8,128)S(1)} %get-tuple-element.17.before_ref, f32[2,2,4,256]{3,2,1,0:T(4,128)S(1)} %collective-permute-done.7.refs_0_, f32[2,2,4,256]{3,2,1,0:T(4,128)S(1)} %collective-permute-done.8.refs_1_, ...), custom_call_target="tpu_custom_call" | custom-call | flops 1835008000 | bytes 262144 | tf_op jit(solution)/shard_map/pallas_call | solution.py:271
  29.0 0.0 collective-permute-done.10.source_ref
  29.0 1.1 %shard_map.69.bin_ref = f32[2,4,256]{2,1,0:T(4,128)S(1)} custom-call(f32[2,4,256]{2,1,0:T(4,128)S(1)} %get-tuple-element.14.speed_ref, f32[2,4,256]{2,1,0:T(4,128)S(1)} %get-tuple-element.15.own_ref, bf16[2,256,48]{2,1,0:T(8,128)(2,1)S(1)} %get-tuple-element.16.target_ref, f32[2,256,32]{2,1,0:T(8,128)S(1)} %shard_map.68.before_ref, ...), custom_call_target="tpu_custom_call" | custom-call | flops 589824000 | bytes 262144 | tf_op jit(solution)/shard_map/pallas_call | solution.py:271
  30.2 0.6 %collective-permute-done.11.source_ref = f32[6,4,256]{2,1,0:T(4,128)S(1)} collective-permute-done((f32[6,4,256]{2,1,0:T(4,128)S(1)}, f32[6,4,256]{2,1,0:T(4,128)S(1)}, u32[]{:S(2)}, u32[]{:S(2)}) %collective-permute-start.11) | collective-permute-done | bytes 24608 | tf_op jit(solution)/shard_map/ppermute | solution.py:320
  30.8 1.7 %shard_map.70 = (f32[3,1,1,2,256]{4,3,2,1,0:T(2,128)}, f32[3,1,1,2,256]{4,3,2,1,0:T(2,128)}) custom-call(f32[2,4,256]{2,1,0:T(4,128)S(1)} %get-tuple-element.10.keep_ref, f32[2,4,256]{2,1,0:T(4,128)S(1)} %shard_map.69.bin_ref, f32[2,4,256]{2,1,0:T(4,128)S(1)} %get-tuple-element.14.speed_ref, f32[2,4,256]{2,1,0:T(4,128)S(1)} %get-tuple-element.15.own_ref, ...), custom_call_target="tpu_custom_call" | custom-call | flops 589824000 | bytes 262144 | tf_op jit(solution)/shard_map/pallas_call | solution.py:271
  (16 shorter events, 0.1 us)
Async XLA Ops:
  0.6 0.7 %copy-start.2 = (s32[1,1,2]{2,1,0:T(1,128)S(1)}, s32[1,1,2]{2,1,0:T(1,128)}, u32[]{:S(2)}) copy-start(s32[1,1,2]{2,1,0:T(1,128)} %param.7) | copy-start | bytes 28
  0.6 0.7 %copy-start.3 = (f32[1,1,2,256]{3,2,1,0:T(2,128)S(1)}, f32[1,1,2,256]{3,2,1,0:T(2,128)}, u32[]{:S(2)}) copy-start(f32[1,1,2,256]{3,2,1,0:T(2,128)} %param.6) | copy-start | bytes 6148
  0.6 0.8 %copy-start.1 = (f32[3,1,1,2,256]{4,3,2,1,0:T(2,128)S(1)}, f32[3,1,1,2,256]{4,3,2,1,0:T(2,128)}, u32[]{:S(2)}) copy-start(f32[3,1,1,2,256]{4,3,2,1,0:T(2,128)} %param.4) | copy-start | bytes 18436
  1.5 4.1 %collective-permute-start = (f32[2,4,256]{2,1,0:T(4,128)S(1)}, f32[2,4,256]{2,1,0:T(4,128)S(1)}, u32[]{:S(2)}, u32[]{:S(2)}) collective-permute-start(f32[2,4,256]{2,1,0:T(4,128)S(1)} %get-tuple-element.11.own_ref), channel_id=1, source_target_pairs={{0,8},{8,0},{16,24},{24,16},{1,9},{9,1},{17,25},{25,17},{2,10},{10... | collective-permute-start | bytes 24584 | tf_op jit(solution)/shard_map/ppermute | solution.py:307
  2.0 7.5 %collective-permute-start.3 = (f32[2,4,256]{2,1,0:T(4,128)S(1)}, f32[2,4,256]{2,1,0:T(4,128)S(1)}, u32[]{:S(2)}, u32[]{:S(2)}) collective-permute-start(f32[2,4,256]{2,1,0:T(4,128)S(1)} %get-tuple-element.11.own_ref), channel_id=1, source_target_pairs={{0,28},{4,24},{8,20},{12,16},{16,12},{20,8},{24,4},{28,0},{1,29},{... | collective-permute-start | bytes 24584 | tf_op jit(solution)/shard_map/ppermute | solution.py:265
  5.6 3.8 %collective-permute-start.1 = (f32[2,2,4,256]{3,2,1,0:T(4,128)S(1)}, f32[2,2,4,256]{3,2,1,0:T(4,128)S(1)}, u32[]{:S(2)}, u32[]{:S(2)}) collective-permute-start(f32[2,2,4,256]{3,2,1,0:T(4,128)S(1)} %pad_maximum_fusion), channel_id=1, source_target_pairs={{0,4},{4,0},{1,5},{5,1},{2,6},{6,2},{3,7},{7,3},{8,12},{12,8},{9,1... | collective-permute-start | bytes 49160 | tf_op jit(solution)/shard_map/ppermute | solution.py:310
  6.1 3.3 %collective-permute-start.2 = (f32[2,2,4,256]{3,2,1,0:T(4,128)S(1)}, f32[2,2,4,256]{3,2,1,0:T(4,128)S(1)}, u32[]{:S(2)}, u32[]{:S(2)}) collective-permute-start(f32[2,2,4,256]{3,2,1,0:T(4,128)S(1)} %pad_maximum_fusion), channel_id=1, source_target_pairs={{0,24},{8,16},{16,8},{24,0},{1,25},{9,17},{17,9},{25,1},{2,26},{10... | collective-permute-start | bytes 49160 | tf_op jit(solution)/shard_map/ppermute | solution.py:311
  9.5 6.5 %collective-permute-start.4 = (f32[6,4,256]{2,1,0:T(4,128)S(1)}, f32[6,4,256]{2,1,0:T(4,128)S(1)}, u32[]{:S(2)}, u32[]{:S(2)}) collective-permute-start(f32[6,4,256]{2,1,0:T(4,128)S(1)} %get-tuple-element.21), channel_id=1, source_target_pairs={{0,1},{1,0},{2,3},{3,2},{4,5},{5,4},{6,7},{7,6},{8,9},{9,8},{10,11... | collective-permute-start | bytes 73736 | tf_op jit(solution)/shard_map/ppermute | solution.py:321
  11.1 6.1 %collective-permute-start.5 = (f32[6,4,256]{2,1,0:T(4,128)S(1)}, f32[6,4,256]{2,1,0:T(4,128)S(1)}, u32[]{:S(2)}, u32[]{:S(2)}) collective-permute-start(f32[6,4,256]{2,1,0:T(4,128)S(1)} %get-tuple-element.20), channel_id=1, source_target_pairs={{0,3},{1,2},{2,1},{3,0},{4,7},{5,6},{6,5},{7,4},{8,11},{9,10},{10,... | collective-permute-start | bytes 73736 | tf_op jit(solution)/shard_map/ppermute | solution.py:320
  13.6 2.4 %copy-start = (f32[3,1,1,2,256]{4,3,2,1,0:T(2,128)S(1)}, f32[3,1,1,2,256]{4,3,2,1,0:T(2,128)}, u32[]{:S(2)}) copy-start(f32[3,1,1,2,256]{4,3,2,1,0:T(2,128)} %speed_ref.3) | copy-start | bytes 18436
  18.3 1.7 %collective-permute-start.6 = (f32[2,4,256]{2,1,0:T(4,128)S(1)}, f32[2,4,256]{2,1,0:T(4,128)S(1)}, u32[]{:S(2)}, u32[]{:S(2)}) collective-permute-start(f32[2,4,256]{2,1,0:T(4,128)S(1)} %get-tuple-element.15.own_ref), channel_id=1, source_target_pairs={{0,8},{8,0},{16,24},{24,16},{1,9},{9,1},{17,25},{25,17},{2,10},{10... | collective-permute-start | bytes 24584 | tf_op jit(solution)/shard_map/ppermute | solution.py:307
  18.4 6.0 %collective-permute-start.9 = (f32[2,4,256]{2,1,0:T(4,128)S(1)}, f32[2,4,256]{2,1,0:T(4,128)S(1)}, u32[]{:S(2)}, u32[]{:S(2)}) collective-permute-start(f32[2,4,256]{2,1,0:T(4,128)S(1)} %get-tuple-element.15.own_ref), channel_id=1, source_target_pairs={{0,28},{4,24},{8,20},{12,16},{16,12},{20,8},{24,4},{28,0},{1,29},{... | collective-permute-start | bytes 24584 | tf_op jit(solution)/shard_map/ppermute | solution.py:265
  20.0 3.8 %collective-permute-start.7 = (f32[2,2,4,256]{3,2,1,0:T(4,128)S(1)}, f32[2,2,4,256]{3,2,1,0:T(4,128)S(1)}, u32[]{:S(2)}, u32[]{:S(2)}) collective-permute-start(f32[2,2,4,256]{3,2,1,0:T(4,128)S(1)} %pad_maximum_fusion.1), channel_id=1, source_target_pairs={{0,4},{4,0},{1,5},{5,1},{2,6},{6,2},{3,7},{7,3},{8,12},{12,8},{9,1... | collective-permute-start | bytes 49160 | tf_op jit(solution)/shard_map/ppermute | solution.py:310
  21.1 3.3 %collective-permute-start.8 = (f32[2,2,4,256]{3,2,1,0:T(4,128)S(1)}, f32[2,2,4,256]{3,2,1,0:T(4,128)S(1)}, u32[]{:S(2)}, u32[]{:S(2)}) collective-permute-start(f32[2,2,4,256]{3,2,1,0:T(4,128)S(1)} %pad_maximum_fusion.1), channel_id=1, source_target_pairs={{0,24},{8,16},{16,8},{24,0},{1,25},{9,17},{17,9},{25,1},{2,26},{10... | collective-permute-start | bytes 49160 | tf_op jit(solution)/shard_map/ppermute | solution.py:311
  24.4 4.6 %collective-permute-start.10 = (f32[6,4,256]{2,1,0:T(4,128)S(1)}, f32[6,4,256]{2,1,0:T(4,128)S(1)}, u32[]{:S(2)}, u32[]{:S(2)}) collective-permute-start(f32[6,4,256]{2,1,0:T(4,128)S(1)} %get-tuple-element.19), channel_id=1, source_target_pairs={{0,1},{1,0},{2,3},{3,2},{4,5},{5,4},{6,7},{7,6},{8,9},{9,8},{10,11... | collective-permute-start | bytes 73736 | tf_op jit(solution)/shard_map/ppermute | solution.py:321
  25.2 5.6 %collective-permute-start.11 = (f32[6,4,256]{2,1,0:T(4,128)S(1)}, f32[6,4,256]{2,1,0:T(4,128)S(1)}, u32[]{:S(2)}, u32[]{:S(2)}) collective-permute-start(f32[6,4,256]{2,1,0:T(4,128)S(1)} %get-tuple-element.18), channel_id=1, source_target_pairs={{0,3},{1,2},{2,1},{3,0},{4,7},{5,6},{6,5},{7,4},{8,11},{9,10},{10,... | collective-permute-start | bytes 73736 | tf_op jit(solution)/shard_map/ppermute | solution.py:320

commit v11 on v9

--- a/solution.py
+++ b/solution.py
@@ -88,21 +88,20 @@
     return jnp.concatenate([list_ref[2 * chunk], list_ref[2 * chunk + 1]], axis=1)[0:4]
 
 
-def fill(near_ref, sum_ref, list_ref, entries):
+def fill(list_ref, entries, chunks):
     half = list_ref.shape[-1]
     lane = lax.broadcasted_iota(jnp.int32, (8, half), 1)
     list_ref[...] = jnp.zeros_like(list_ref)
     place = jnp.int32(0)
     held = {}
+    heads = []
     for number, (ref, index, offset) in enumerate(entries):
         packed = ref[index]
         head, tail = shifted(packed[:, :half], offset), shifted(packed[:, half:], offset)
         if number == len(entries) - 1 and number % 2 == 0:
             list_ref[0] = jnp.concatenate([head, jnp.zeros_like(head)], axis=0)
         else:
-            distance, summed = source_rows(head)
-            near_ref[:, number * half : (number + 1) * half] = distance
-            sum_ref[:, number * half : (number + 1) * half] = summed
+            heads.append(head)
         held[number] = tail
     if len(entries) % 2:
         place = place + half
@@ -123,48 +122,34 @@
         place = place + length
         tile_rows = jnp.where(turn + length >= half, jnp.where(lane < turn, tail, 0.0), upto)
     list_ref[lax.div(place, half)] = tile_rows
-    done = (len(entries) // 2) * 2 * half
-    for chunk in range((near_ref.shape[1] - done) // (2 * half)):
-        distance, summed = source_rows(list_chunk(list_ref, chunk))
-        near_ref[:, done + chunk * 2 * half : done + (chunk + 1) * 2 * half] = distance
-        sum_ref[:, done + chunk * 2 * half : done + (chunk + 1) * 2 * half] = summed
-    return place
-
-
-def gathered(target, nears, sums):
-    highs, lows = [], []
-    for near in nears:
-        high, low = pair_weight(target, near)
-        highs.append(high)
-        lows.append(low)
-    rows = jnp.concatenate(sums, axis=1)
-    return contract(jnp.concatenate(highs + lows, axis=1), jnp.concatenate([rows, rows], axis=1))
-
-
-def sums_over(targets, totals, near_ref, sum_ref, list_ref, length, sources, tiles):
+    first = [source_rows(jnp.concatenate(heads[at : at + 2], axis=1)) for at in range(0, len(heads), 2)]
+    packed = [source_rows(list_chunk(list_ref, chunk)) for chunk in range(chunks)]
+    return first, packed, place
+
+
+def gathered(target, sources):
+    weights, rows = [], []
+    for near, summed in sources:
+        weights += pair_weight(target, near)
+        rows += [summed, summed]
+    return contract(jnp.concatenate(weights, axis=1), jnp.concatenate(rows, axis=1))
+
+
+def sums_over(targets, totals, list_ref, entries, chunks):
     wide = 2 * list_ref.shape[-1]
-    steps = near_ref.shape[1] // (tiles * wide)
-
-    def step(number, totals):
-        nears, sums = [], []
-        for tile in range(tiles):
-            lanes = pl.ds(pl.multiple_of((number * tiles + tile) * wide, wide), wide)
-            nears.append(near_ref[:, lanes])
-            sums.append(sum_ref[:, lanes])
-        return tuple(total + gathered(target, nears, sums) for target, total in zip(targets, totals))
-
-    totals = step(0, totals) if steps == 1 else lax.fori_loop(0, steps, step, tuple(totals))
-    done = steps * tiles - sources // 2
+    first, packed, length = fill(list_ref, entries, chunks)
+    totals = [total + gathered(target, first) for target, total in zip(targets, totals)]
+    totals = tuple(total + gathered(target, packed) for target, total in zip(targets, totals))
 
     def rest(number, totals):
-        near, summed = source_rows(list_chunk(list_ref, number))
-        return tuple(total + gathered(target, [near], [summed]) for target, total in zip(targets, totals))
-
-    return lax.fori_loop(done, jnp.maximum(lax.div(length + (wide - 1), wide), done), rest, tuple(totals))
+        sources = [source_rows(list_chunk(list_ref, number))]
+        return tuple(total + gathered(target, sources) for target, total in zip(targets, totals))
+
+    return lax.fori_loop(chunks, jnp.maximum(lax.div(length + (wide - 1), wide), chunks), rest, totals)
 
 
 def plane_kernel(size_y, *refs):
-    planes, (target_ref, total_ref, near_ref, sum_ref, list_ref) = refs[:-5], refs[-5:]
+    planes, (target_ref, total_ref, list_ref) = refs[:-3], refs[-3:]
     own_ref = planes[0]
     for z in range(2):
         target_ref[z] = target_rows(shifted(own_ref[z], (0, 0, z)))
@@ -172,37 +157,34 @@
     for ref, shifts in zip(planes, y_shifts(size_y)):
         for y in shifts:
             entries += [(ref, z, (0, y, z)) for z in range(2)]
-    length = fill(near_ref, sum_ref, list_ref, entries)
     zero = jnp.zeros(total_ref.shape[1:], F32)
     targets = [target_ref[z] for z in range(2)]
-    totals = sums_over(targets, (zero, zero), near_ref, sum_ref, list_ref, length, len(entries), 5)
+    totals = sums_over(targets, (zero, zero), list_ref, entries, 2)
     for z in range(2):
         total_ref[z] = totals[z]
 
 
 def slab_kernel(size_y, target_ref, before_ref, near_x_ref, *refs):
-    far_refs, (total_ref, near_ref, sum_ref, list_ref) = refs[:-4], refs[-4:]
+    far_refs, (total_ref, list_ref) = refs[:-2], refs[-2:]
     entries = []
     for plane, shifts in enumerate(y_shifts(size_y)):
         for y in shifts:
             entries += [(near_x_ref, (plane, z), (ahead("gx"), y, z)) for z in range(2)]
             entries += [(far_refs[plane - 1], z, (-ahead("gx"), y, z)) for z in range(2)]
-    length = fill(near_ref, sum_ref, list_ref, entries)
     targets = [target_ref[z] for z in range(2)]
-    totals = sums_over(targets, (before_ref[0], before_ref[1]), near_ref, sum_ref, list_ref, length, len(entries), 9)
+    totals = sums_over(targets, (before_ref[0], before_ref[1]), list_ref, entries, 3)
     for z in range(2):
         total_ref[z] = totals[z]
 
 
-def complete(size_y, first, z, speed_ref, own_ref, target_ref, before_ref, source_ref, near_ref, sum_ref, list_ref):
+def complete(size_y, first, z, speed_ref, own_ref, target_ref, before_ref, source_ref, list_ref):
     entries = []
     for column, x in enumerate((0, ahead("gx"), -ahead("gx"))):
         for plane, shifts in enumerate(y_shifts(size_y)):
             planes = len(y_shifts(size_y))
             index = column * planes + (plane if column < 2 else (plane - 1) % planes)
             entries += [(source_ref, index, (x, y, 3 * z - 1)) for y in shifts]
-    length = fill(near_ref, sum_ref, list_ref, entries)
-    (total,) = sums_over([target_ref[z]], (before_ref[z],), near_ref, sum_ref, list_ref, length, len(entries), 7)
+    (total,) = sums_over([target_ref[z]], (before_ref[z],), list_ref, entries, 3)
     total = total.T
     total = (total[0:8] + total[8:16] + total[16:24])[0:4]
     own = own_ref[z]
@@ -221,19 +203,19 @@
     return (1 + ahead("gz")) // 2
 
 
-def near_kernel(size_y, first, speed_ref, own_ref, target_ref, before_ref, source_ref, bin_ref, near_ref, sum_ref, list_ref):
+def near_kernel(size_y, first, speed_ref, own_ref, target_ref, before_ref, source_ref, bin_ref, list_ref):
     place, speed = complete(
-        size_y, first, near_side(), speed_ref, own_ref, target_ref, before_ref, source_ref, near_ref, sum_ref, list_ref
+        size_y, first, near_side(), speed_ref, own_ref, target_ref, before_ref, source_ref, list_ref
     )
     bin_ref[0] = place
     bin_ref[1] = speed
 
 
-def far_kernel(size_y, first, last, keep_ref, bin_ref, speed_ref, own_ref, target_ref, before_ref, source_ref, place_out, speed_out, near_ref, sum_ref, list_ref):
+def far_kernel(size_y, first, last, keep_ref, bin_ref, speed_ref, own_ref, target_ref, before_ref, source_ref, place_out, speed_out, list_ref):
     other = near_side()
     z = 1 - other
     place, speed = complete(
-        size_y, first, z, speed_ref, own_ref, target_ref, before_ref, source_ref, near_ref, sum_ref, list_ref
+        size_y, first, z, speed_ref, own_ref, target_ref, before_ref, source_ref, list_ref
     )
     if not last:
         place_out[z] = place
@@ -266,7 +248,7 @@
     return lax.ppermute(value, ("gx", "gy"), pairs)
 
 
-def call(kernel, inputs, outputs, sources, targets, slots, chunks):
+def call(kernel, inputs, outputs, sources, targets, slots):
     half = slots // 2
     heads = sources // 2 * 2
     return pl.pallas_call(
@@ -275,8 +257,6 @@
         in_specs=[VMEM] * len(inputs),
         out_specs=tuple(VMEM for _ in outputs),
         scratch_shapes=[
-            pltpu.VMEM((48, heads * half + chunks * slots), BF16),
-            pltpu.VMEM((32, heads * half + chunks * slots), BF16),
             pltpu.VMEM((heads + 4, 8, half), F32),
         ],
         compiler_params=pltpu.CompilerParams(vmem_limit_bytes=24 * 1024 * 1024),
@@ -313,7 +293,7 @@
             functools.partial(plane_kernel, size_y),
             planes,
             (jax.ShapeDtypeStruct((2, slots, 48), BF16), running),
-            6, 2, slots, 2,
+            6, 2, slots,
         )
         slab = jnp.concatenate([plane, near_x] + [value[None] for value in far_planes], axis=0)
         near, far = swaps("gz")
@@ -323,20 +303,20 @@
             functools.partial(slab_kernel, size_y),
             [targets, total, near_x] + far_planes,
             (running,),
-            12, 2, slots, 3,
+            12, 2, slots,
         )
         state = [speed, packed, targets, total]
         (half_done,) = call(
             functools.partial(near_kernel, size_y, first),
             state + [near_z],
             (bins,),
-            9, 1, slots, 3,
+            9, 1, slots,
         )
         packed, speed = call(
             functools.partial(far_kernel, size_y, first, last),
             [keep, half_done] + state + [far_z],
             (full, full) if last else (bins, bins),
-            9, 1, slots, 3,
+            9, 1, slots,
         )
     return packed, speed
 

time: 30.7 us -> 31.1 us (1.013)
  Pallas kernels: 12.2 us -> 12.7 us
    pallas_call x8, Pallas kernels: 12.2 us -> 12.7 us  [call(): pl.pallas_call(kernel, out_shape=outputs, in_specs=[VMEM] * len(inputs),...]
where the time goes in v11:
time: 31.1 us; the launch traced here: 30.9 us
  starting transfers between devices  14.1 us (45%)
  Pallas kernels  12.7 us (41%)
  waiting for transfers between devices  2.42 us (8%)
  between operations  0.82 us (3%)
  local copies, waits for them, and re-layouts  0.72 us (2%)
    pallas_call x8, Pallas kernels, call(): pl.pallas_call(kernel, out_shape=outputs, in_specs=[VMEM] * len(inputs),...  12.7 us
    ppermute x2, starting transfers between devices, on_device(): planes = [packed] + [lax.ppermute(packed, 'gy', path) for path in paths]  4.32 us
    ppermute x2, starting transfers between devices, on_device(): lax.ppermute(lax.dynamic_index_in_dim(slab, upper, 1, False), 'gz', far)  4.05 us
    ppermute x2, starting transfers between devices, on_device(): lax.ppermute(lax.dynamic_index_in_dim(slab, 1 - upper, 1, False), 'gz', n...  2.38 us
    ppermute x2, starting transfers between devices, on_device(): lax.ppermute(packed, 'gx', far)  2.03 us
    ppermute x2, starting transfers between devices, across(): return lax.ppermute(value, ('gx', 'gy'), pairs)  1.22 us
    ppermute x2, waiting for transfers between devices, across(): return lax.ppermute(value, ('gx', 'gy'), pairs)  0.96 us
    ppermute x2, waiting for transfers between devices, on_device(): planes = [packed] + [lax.ppermute(packed, 'gy', path) for path in paths]  0.81 us
  transfers between devices with their start and end apart: 12, of which 5 were waited for; matrix products, arithmetic and copies ran while one was open for 0% of the time, Pallas kernels for 31%

profile of v11, /device:TPU:0, one launch (start us, length us, event | category | flops | bytes accessed | tf_op | source)
XLA Modules:
  0.0 30.9 jit_solution(14050952411415117445)
XLA Ops:
  0.6 0.0 copy-start.2
  0.6 0.0 copy-start.3
  0.6 0.0 copy-start.1
  0.7 0.6 %copy-done.2 = s32[1,1,2]{2,1,0:T(1,128)S(1)} copy-done((s32[1,1,2]{2,1,0:T(1,128)S(1)}, s32[1,1,2]{2,1,0:T(1,128)}, u32[]{:S(2)}) %copy-start.2) | copy-done | bytes 32
  1.3 0.1 compare_select_fusion
  1.4 0.0 copy-done.3
  1.4 0.1 fusion
  1.4 0.0 copy-done.1
  1.5 3.0 %collective-permute-start = (f32[2,4,256]{2,1,0:T(4,128)S(1)}, f32[2,4,256]{2,1,0:T(4,128)S(1)}, u32[]{:S(2)}, u32[]{:S(2)}) collective-permute-start(f32[2,4,256]{2,1,0:T(4,128)S(1)} %get-tuple-element.11.refs_0_.own_ref), channel_id=1, source_target_pairs={{0,4},{4,0},{1,5},{5,1},{2,6},{6,2},{3,7},{7,3},{8,12},{12,8},{9,1... | collective-permute-start | bytes 24584 | tf_op jit(solution)/shard_map/ppermute | solution.py:287
  4.5 0.6 %collective-permute-start.2 = (f32[2,4,256]{2,1,0:T(4,128)S(1)}, f32[2,4,256]{2,1,0:T(4,128)S(1)}, u32[]{:S(2)}, u32[]{:S(2)}) collective-permute-start(f32[2,4,256]{2,1,0:T(4,128)S(1)} %get-tuple-element.11.refs_0_.own_ref), channel_id=1, source_target_pairs={{0,28},{4,24},{8,20},{12,16},{16,12},{20,8},{24,4},{28,0},{1,29},{... | collective-permute-start | bytes 24584 | tf_op jit(solution)/shard_map/ppermute | solution.py:248
  5.1 0.7 %collective-permute-start.3 = (f32[2,4,256]{2,1,0:T(4,128)S(1)}, f32[2,4,256]{2,1,0:T(4,128)S(1)}, u32[]{:S(2)}, u32[]{:S(2)}) collective-permute-start(f32[2,4,256]{2,1,0:T(4,128)S(1)} %get-tuple-element.11.refs_0_.own_ref), channel_id=1, source_target_pairs={{0,24},{8,16},{16,8},{24,0},{1,25},{9,17},{17,9},{25,1},{2,26},{10... | collective-permute-start | bytes 24584 | tf_op jit(solution)/shard_map/ppermute | solution.py:289
  5.8 0.4 %collective-permute-done.refs_1_ = f32[2,4,256]{2,1,0:T(4,128)S(1)} collective-permute-done((f32[2,4,256]{2,1,0:T(4,128)S(1)}, f32[2,4,256]{2,1,0:T(4,128)S(1)}, u32[]{:S(2)}, u32[]{:S(2)}) %collective-permute-start) | collective-permute-done | bytes 8224 | tf_op jit(solution)/shard_map/ppermute | solution.py:287
  6.1 0.1 collective-permute-start.1
  6.2 1.4 %shard_map.63 = (bf16[2,256,48]{2,1,0:T(8,128)(2,1)S(1)}, f32[2,256,32]{2,1,0:T(8,128)S(1)}) custom-call(f32[2,4,256]{2,1,0:T(4,128)S(1)} %get-tuple-element.11.refs_0_.own_ref, f32[2,4,256]{2,1,0:T(4,128)S(1)} %collective-permute-done.refs_1_), custom_call_target="tpu_custom_call" | custom-call | flops 786432000 | bytes 262144 | tf_op jit(solution)/shard_map/pallas_call | solution.py:254
  7.6 0.0 collective-permute-done.1.near_x_ref
  7.6 0.9 %collective-permute-done.2.refs_0_ = f32[2,4,256]{2,1,0:T(4,128)S(1)} collective-permute-done((f32[2,4,256]{2,1,0:T(4,128)S(1)}, f32[2,4,256]{2,1,0:T(4,128)S(1)}, u32[]{:S(2)}, u32[]{:S(2)}) %collective-permute-start.2) | collective-permute-done | bytes 8224 | tf_op jit(solution)/shard_map/ppermute | solution.py:248
  8.5 0.0 collective-permute-done.3.refs_1_
  8.5 1.6 %collective-permute-start.4 = (f32[6,4,256]{2,1,0:T(4,128)S(1)}, f32[6,4,256]{2,1,0:T(4,128)S(1)}, u32[]{:S(2)}, u32[]{:S(2)}) collective-permute-start(f32[6,4,256]{2,1,0:T(4,128)S(1)} %get-tuple-element.21), channel_id=1, source_target_pairs={{0,1},{1,0},{2,3},{3,2},{4,5},{5,4},{6,7},{7,6},{8,9},{9,8},{10,11... | collective-permute-start | bytes 73736 | tf_op jit(solution)/shard_map/ppermute | solution.py:301
  10.1 2.5 %collective-permute-start.5 = (f32[6,4,256]{2,1,0:T(4,128)S(1)}, f32[6,4,256]{2,1,0:T(4,128)S(1)}, u32[]{:S(2)}, u32[]{:S(2)}) collective-permute-start(f32[6,4,256]{2,1,0:T(4,128)S(1)} %get-tuple-element.20), channel_id=1, source_target_pairs={{0,3},{1,2},{2,1},{3,0},{4,7},{5,6},{6,5},{7,4},{8,11},{9,10},{10,... | collective-permute-start | bytes 73736 | tf_op jit(solution)/shard_map/ppermute | solution.py:300
  12.6 0.0 copy-start
  12.6 2.1 %shard_map.64.before_ref = f32[2,256,32]{2,1,0:T(8,128)S(1)} custom-call(bf16[2,256,48]{2,1,0:T(8,128)(2,1)S(1)} %get-tuple-element.12.target_ref, f32[2,256,32]{2,1,0:T(8,128)S(1)} %get-tuple-element.13.before_ref, f32[2,2,4,256]{3,2,1,0:T(4,128)S(1)} %collective-permute-done.1.near_x_ref, f32[2,4,256]{2,1,0:T(4,128)S(1)} %collective-permute-done.2.refs_0_, ...), custom_call_target="tpu_custom_call" | custom-call | flops 1572864000 | bytes 262144 | tf_op jit(solution)/shard_map/pallas_call | solution.py:254
  14.7 0.0 collective-permute-done.4.source_ref
  14.7 0.0 copy-done
  14.8 1.3 %shard_map.65.bin_ref = f32[2,4,256]{2,1,0:T(4,128)S(1)} custom-call(f32[3,1,1,2,256]{4,3,2,1,0:T(2,128)S(1)} %copy-done, f32[2,4,256]{2,1,0:T(4,128)S(1)} %get-tuple-element.11.refs_0_.own_ref, bf16[2,256,48]{2,1,0:T(8,128)(2,1)S(1)} %get-tuple-element.12.target_ref, f32[2,256,32]{2,1,0:T(8,128)S(1)} %shard_map.64.before_ref, ...), custom_call_target="tpu_custom_call" | custom-call | flops 589824000 | bytes 262144 | tf_op jit(solution)/shard_map/pallas_call | solution.py:254
  16.0 0.0 collective-permute-done.5.source_ref
  16.1 1.3 %shard_map.66 = (f32[2,4,256]{2,1,0:T(4,128)S(1)}, f32[2,4,256]{2,1,0:T(4,128)S(1)}) custom-call(f32[2,4,256]{2,1,0:T(4,128)S(1)} %get-tuple-element.10.keep_ref, f32[2,4,256]{2,1,0:T(4,128)S(1)} %shard_map.65.bin_ref, f32[3,1,1,2,256]{4,3,2,1,0:T(2,128)S(1)} %copy-done, f32[2,4,256]{2,1,0:T(4,128)S(1)} %get-tuple-element.11.refs_0_.own_ref, ...), custom_call_target="tpu_custom_call" | custom-call | flops 589824000 | bytes 262144 | tf_op jit(solution)/shard_map/pallas_call | solution.py:254
  17.4 1.3 %collective-permute-start.6 = (f32[2,4,256]{2,1,0:T(4,128)S(1)}, f32[2,4,256]{2,1,0:T(4,128)S(1)}, u32[]{:S(2)}, u32[]{:S(2)}) collective-permute-start(f32[2,4,256]{2,1,0:T(4,128)S(1)} %get-tuple-element.15.refs_0_.own_ref), channel_id=1, source_target_pairs={{0,4},{4,0},{1,5},{5,1},{2,6},{6,2},{3,7},{7,3},{8,12},{12,8},{9,1... | collective-permute-start | bytes 24584 | tf_op jit(solution)/shard_map/ppermute | solution.py:287
  18.6 0.6 %collective-permute-start.8 = (f32[2,4,256]{2,1,0:T(4,128)S(1)}, f32[2,4,256]{2,1,0:T(4,128)S(1)}, u32[]{:S(2)}, u32[]{:S(2)}) collective-permute-start(f32[2,4,256]{2,1,0:T(4,128)S(1)} %get-tuple-element.15.refs_0_.own_ref), channel_id=1, source_target_pairs={{0,28},{4,24},{8,20},{12,16},{16,12},{20,8},{24,4},{28,0},{1,29},{... | collective-permute-start | bytes 24584 | tf_op jit(solution)/shard_map/ppermute | solution.py:248
  19.3 1.4 %collective-permute-start.9 = (f32[2,4,256]{2,1,0:T(4,128)S(1)}, f32[2,4,256]{2,1,0:T(4,128)S(1)}, u32[]{:S(2)}, u32[]{:S(2)}) collective-permute-start(f32[2,4,256]{2,1,0:T(4,128)S(1)} %get-tuple-element.15.refs_0_.own_ref), channel_id=1, source_target_pairs={{0,24},{8,16},{16,8},{24,0},{1,25},{9,17},{17,9},{25,1},{2,26},{10... | collective-permute-start | bytes 24584 | tf_op jit(solution)/shard_map/ppermute | solution.py:289
  20.6 0.4 %collective-permute-done.6.refs_1_ = f32[2,4,256]{2,1,0:T(4,128)S(1)} collective-permute-done((f32[2,4,256]{2,1,0:T(4,128)S(1)}, f32[2,4,256]{2,1,0:T(4,128)S(1)}, u32[]{:S(2)}, u32[]{:S(2)}) %collective-permute-start.6) | collective-permute-done | bytes 8224 | tf_op jit(solution)/shard_map/ppermute | solution.py:287
  21.1 0.0 collective-permute-start.7
  21.1 1.4 %shard_map.67 = (bf16[2,256,48]{2,1,0:T(8,128)(2,1)S(1)}, f32[2,256,32]{2,1,0:T(8,128)S(1)}) custom-call(f32[2,4,256]{2,1,0:T(4,128)S(1)} %get-tuple-element.15.refs_0_.own_ref, f32[2,4,256]{2,1,0:T(4,128)S(1)} %collective-permute-done.6.refs_1_), custom_call_target="tpu_custom_call" | custom-call | flops 786432000 | bytes 262144 | tf_op jit(solution)/shard_map/pallas_call | solution.py:254
  22.5 0.0 collective-permute-done.7.near_x_ref
  22.5 0.1 collective-permute-done.8.refs_0_
  22.6 0.0 collective-permute-done.9.refs_1_
  22.7 0.7 %collective-permute-start.10 = (f32[6,4,256]{2,1,0:T(4,128)S(1)}, f32[6,4,256]{2,1,0:T(4,128)S(1)}, u32[]{:S(2)}, u32[]{:S(2)}) collective-permute-start(f32[6,4,256]{2,1,0:T(4,128)S(1)} %get-tuple-element.19), channel_id=1, source_target_pairs={{0,1},{1,0},{2,3},{3,2},{4,5},{5,4},{6,7},{7,6},{8,9},{9,8},{10,11... | collective-permute-start | bytes 73736 | tf_op jit(solution)/shard_map/ppermute | solution.py:301
  23.4 1.6 %collective-permute-start.11 = (f32[6,4,256]{2,1,0:T(4,128)S(1)}, f32[6,4,256]{2,1,0:T(4,128)S(1)}, u32[]{:S(2)}, u32[]{:S(2)}) collective-permute-start(f32[6,4,256]{2,1,0:T(4,128)S(1)} %get-tuple-element.18), channel_id=1, source_target_pairs={{0,3},{1,2},{2,1},{3,0},{4,7},{5,6},{6,5},{7,4},{8,11},{9,10},{10,... | collective-permute-start | bytes 73736 | tf_op jit(solution)/shard_map/ppermute | solution.py:300
  25.0 2.1 %shard_map.68.before_ref = f32[2,256,32]{2,1,0:T(8,128)S(1)} custom-call(bf16[2,256,48]{2,1,0:T(8,128)(2,1)S(1)} %get-tuple-element.16.target_ref, f32[2,256,32]{2,1,0:T(8,128)S(1)} %get-tuple-element.17.before_ref, f32[2,2,4,256]{3,2,1,0:T(4,128)S(1)} %collective-permute-done.7.near_x_ref, f32[2,4,256]{2,1,0:T(4,128)S(1)} %collective-permute-done.8.refs_0_, ...), custom_call_target="tpu_custom_call" | custom-call | flops 1572864000 | bytes 262144 | tf_op jit(solution)/shard_map/pallas_call | solution.py:254
  27.1 0.0 collective-permute-done.10.source_ref
  27.1 1.3 %shard_map.69.bin_ref = f32[2,4,256]{2,1,0:T(4,128)S(1)} custom-call(f32[2,4,256]{2,1,0:T(4,128)S(1)} %get-tuple-element.14.speed_ref, f32[2,4,256]{2,1,0:T(4,128)S(1)} %get-tuple-element.15.refs_0_.own_ref, bf16[2,256,48]{2,1,0:T(8,128)(2,1)S(1)} %get-tuple-element.16.target_ref, f32[2,256,32]{2,1,0:T(8,128)S(1)} %shard_map.68.before_ref, ...), custom_call_target="tpu_custom_call" | custom-call | flops 589824000 | bytes 262144 | tf_op jit(solution)/shard_map/pallas_call | solution.py:254
  28.4 0.6 %collective-permute-done.11.source_ref = f32[6,4,256]{2,1,0:T(4,128)S(1)} collective-permute-done((f32[6,4,256]{2,1,0:T(4,128)S(1)}, f32[6,4,256]{2,1,0:T(4,128)S(1)}, u32[]{:S(2)}, u32[]{:S(2)}) %collective-permute-start.11) | collective-permute-done | bytes 24608 | tf_op jit(solution)/shard_map/ppermute | solution.py:300
  29.0 1.9 %shard_map.70 = (f32[3,1,1,2,256]{4,3,2,1,0:T(2,128)}, f32[3,1,1,2,256]{4,3,2,1,0:T(2,128)}) custom-call(f32[2,4,256]{2,1,0:T(4,128)S(1)} %get-tuple-element.10.keep_ref, f32[2,4,256]{2,1,0:T(4,128)S(1)} %shard_map.69.bin_ref, f32[2,4,256]{2,1,0:T(4,128)S(1)} %get-tuple-element.14.speed_ref, f32[2,4,256]{2,1,0:T(4,128)S(1)} %get-tuple-element.15.refs_0_.own_ref, ...), custom_call_target="tpu_custom_call" | custom-call | flops 589824000 | bytes 262144 | tf_op jit(solution)/shard_map/pallas_call | solution.py:254
  (16 shorter events, 0.1 us)
Async XLA Ops:
  0.6 0.7 %copy-start.2 = (s32[1,1,2]{2,1,0:T(1,128)S(1)}, s32[1,1,2]{2,1,0:T(1,128)}, u32[]{:S(2)}) copy-start(s32[1,1,2]{2,1,0:T(1,128)} %param.7) | copy-start | bytes 28
  0.6 0.7 %copy-start.3 = (f32[1,1,2,256]{3,2,1,0:T(2,128)S(1)}, f32[1,1,2,256]{3,2,1,0:T(2,128)}, u32[]{:S(2)}) copy-start(f32[1,1,2,256]{3,2,1,0:T(2,128)} %param.6) | copy-start | bytes 6148
  0.6 0.8 %copy-start.1 = (f32[3,1,1,2,256]{4,3,2,1,0:T(2,128)S(1)}, f32[3,1,1,2,256]{4,3,2,1,0:T(2,128)}, u32[]{:S(2)}) copy-start(f32[3,1,1,2,256]{4,3,2,1,0:T(2,128)} %param.4) | copy-start | bytes 18436
  1.5 4.7 %collective-permute-start = (f32[2,4,256]{2,1,0:T(4,128)S(1)}, f32[2,4,256]{2,1,0:T(4,128)S(1)}, u32[]{:S(2)}, u32[]{:S(2)}) collective-permute-start(f32[2,4,256]{2,1,0:T(4,128)S(1)} %get-tuple-element.11.refs_0_.own_ref), channel_id=1, source_target_pairs={{0,4},{4,0},{1,5},{5,1},{2,6},{6,2},{3,7},{7,3},{8,12},{12,8},{9,1... | collective-permute-start | bytes 24584 | tf_op jit(solution)/shard_map/ppermute | solution.py:287
  4.5 4.0 %collective-permute-start.2 = (f32[2,4,256]{2,1,0:T(4,128)S(1)}, f32[2,4,256]{2,1,0:T(4,128)S(1)}, u32[]{:S(2)}, u32[]{:S(2)}) collective-permute-start(f32[2,4,256]{2,1,0:T(4,128)S(1)} %get-tuple-element.11.refs_0_.own_ref), channel_id=1, source_target_pairs={{0,28},{4,24},{8,20},{12,16},{16,12},{20,8},{24,4},{28,0},{1,29},{... | collective-permute-start | bytes 24584 | tf_op jit(solution)/shard_map/ppermute | solution.py:248
  5.1 3.4 %collective-permute-start.3 = (f32[2,4,256]{2,1,0:T(4,128)S(1)}, f32[2,4,256]{2,1,0:T(4,128)S(1)}, u32[]{:S(2)}, u32[]{:S(2)}) collective-permute-start(f32[2,4,256]{2,1,0:T(4,128)S(1)} %get-tuple-element.11.refs_0_.own_ref), channel_id=1, source_target_pairs={{0,24},{8,16},{16,8},{24,0},{1,25},{9,17},{17,9},{25,1},{2,26},{10... | collective-permute-start | bytes 24584 | tf_op jit(solution)/shard_map/ppermute | solution.py:289
  6.1 1.5 %collective-permute-start.1 = (f32[2,2,4,256]{3,2,1,0:T(4,128)S(1)}, f32[2,2,4,256]{3,2,1,0:T(4,128)S(1)}, u32[]{:S(2)}, u32[]{:S(2)}) collective-permute-start(f32[2,2,4,256]{3,2,1,0:T(4,128)S(1)} %pad_maximum_fusion), channel_id=1, source_target_pairs={{0,8},{8,0},{16,24},{24,16},{1,9},{9,1},{17,25},{25,17},{2,10},{10... | collective-permute-start | bytes 49160 | tf_op jit(solution)/shard_map/ppermute | solution.py:291
  8.5 6.2 %collective-permute-start.4 = (f32[6,4,256]{2,1,0:T(4,128)S(1)}, f32[6,4,256]{2,1,0:T(4,128)S(1)}, u32[]{:S(2)}, u32[]{:S(2)}) collective-permute-start(f32[6,4,256]{2,1,0:T(4,128)S(1)} %get-tuple-element.21), channel_id=1, source_target_pairs={{0,1},{1,0},{2,3},{3,2},{4,5},{5,4},{6,7},{7,6},{8,9},{9,8},{10,11... | collective-permute-start | bytes 73736 | tf_op jit(solution)/shard_map/ppermute | solution.py:301
  10.1 5.9 %collective-permute-start.5 = (f32[6,4,256]{2,1,0:T(4,128)S(1)}, f32[6,4,256]{2,1,0:T(4,128)S(1)}, u32[]{:S(2)}, u32[]{:S(2)}) collective-permute-start(f32[6,4,256]{2,1,0:T(4,128)S(1)} %get-tuple-element.20), channel_id=1, source_target_pairs={{0,3},{1,2},{2,1},{3,0},{4,7},{5,6},{6,5},{7,4},{8,11},{9,10},{10,... | collective-permute-start | bytes 73736 | tf_op jit(solution)/shard_map/ppermute | solution.py:300
  12.6 2.1 %copy-start = (f32[3,1,1,2,256]{4,3,2,1,0:T(2,128)S(1)}, f32[3,1,1,2,256]{4,3,2,1,0:T(2,128)}, u32[]{:S(2)}) copy-start(f32[3,1,1,2,256]{4,3,2,1,0:T(2,128)} %speed_ref.3) | copy-start | bytes 18436
  17.4 3.7 %collective-permute-start.6 = (f32[2,4,256]{2,1,0:T(4,128)S(1)}, f32[2,4,256]{2,1,0:T(4,128)S(1)}, u32[]{:S(2)}, u32[]{:S(2)}) collective-permute-start(f32[2,4,256]{2,1,0:T(4,128)S(1)} %get-tuple-element.15.refs_0_.own_ref), channel_id=1, source_target_pairs={{0,4},{4,0},{1,5},{5,1},{2,6},{6,2},{3,7},{7,3},{8,12},{12,8},{9,1... | collective-permute-start | bytes 24584 | tf_op jit(solution)/shard_map/ppermute | solution.py:287
  18.6 4.0 %collective-permute-start.8 = (f32[2,4,256]{2,1,0:T(4,128)S(1)}, f32[2,4,256]{2,1,0:T(4,128)S(1)}, u32[]{:S(2)}, u32[]{:S(2)}) collective-permute-start(f32[2,4,256]{2,1,0:T(4,128)S(1)} %get-tuple-element.15.refs_0_.own_ref), channel_id=1, source_target_pairs={{0,28},{4,24},{8,20},{12,16},{16,12},{20,8},{24,4},{28,0},{1,29},{... | collective-permute-start | bytes 24584 | tf_op jit(solution)/shard_map/ppermute | solution.py:248
  19.3 3.4 %collective-permute-start.9 = (f32[2,4,256]{2,1,0:T(4,128)S(1)}, f32[2,4,256]{2,1,0:T(4,128)S(1)}, u32[]{:S(2)}, u32[]{:S(2)}) collective-permute-start(f32[2,4,256]{2,1,0:T(4,128)S(1)} %get-tuple-element.15.refs_0_.own_ref), channel_id=1, source_target_pairs={{0,24},{8,16},{16,8},{24,0},{1,25},{9,17},{17,9},{25,1},{2,26},{10... | collective-permute-start | bytes 24584 | tf_op jit(solution)/shard_map/ppermute | solution.py:289
  21.1 1.4 %collective-permute-start.7 = (f32[2,2,4,256]{3,2,1,0:T(4,128)S(1)}, f32[2,2,4,256]{3,2,1,0:T(4,128)S(1)}, u32[]{:S(2)}, u32[]{:S(2)}) collective-permute-start(f32[2,2,4,256]{3,2,1,0:T(4,128)S(1)} %pad_maximum_fusion.1), channel_id=1, source_target_pairs={{0,8},{8,0},{16,24},{24,16},{1,9},{9,1},{17,25},{25,17},{2,10},{10... | collective-permute-start | bytes 49160 | tf_op jit(solution)/shard_map/ppermute | solution.py:291
  22.7 4.4 %collective-permute-start.10 = (f32[6,4,256]{2,1,0:T(4,128)S(1)}, f32[6,4,256]{2,1,0:T(4,128)S(1)}, u32[]{:S(2)}, u32[]{:S(2)}) collective-permute-start(f32[6,4,256]{2,1,0:T(4,128)S(1)} %get-tuple-element.19), channel_id=1, source_target_pairs={{0,1},{1,0},{2,3},{3,2},{4,5},{5,4},{6,7},{7,6},{8,9},{9,8},{10,11... | collective-permute-start | bytes 73736 | tf_op jit(solution)/shard_map/ppermute | solution.py:301
  23.4 5.6 %collective-permute-start.11 = (f32[6,4,256]{2,1,0:T(4,128)S(1)}, f32[6,4,256]{2,1,0:T(4,128)S(1)}, u32[]{:S(2)}, u32[]{:S(2)}) collective-permute-start(f32[6,4,256]{2,1,0:T(4,128)S(1)} %get-tuple-element.18), channel_id=1, source_target_pairs={{0,3},{1,2},{2,1},{3,0},{4,7},{5,6},{6,5},{7,4},{8,11},{9,10},{10,... | collective-permute-start | bytes 73736 | tf_op jit(solution)/shard_map/ppermute | solution.py:300

commit v12 on v11

--- a/solution.py
+++ b/solution.py
@@ -138,8 +138,7 @@
 def sums_over(targets, totals, list_ref, entries, chunks):
     wide = 2 * list_ref.shape[-1]
     first, packed, length = fill(list_ref, entries, chunks)
-    totals = [total + gathered(target, first) for target, total in zip(targets, totals)]
-    totals = tuple(total + gathered(target, packed) for target, total in zip(targets, totals))
+    totals = tuple(total + gathered(target, first + packed) for target, total in zip(targets, totals))
 
     def rest(number, totals):
         sources = [source_rows(list_chunk(list_ref, number))]

time: 31.1 us -> 30.7 us (0.987)
  Pallas kernels: 12.7 us -> 12.3 us
    pallas_call x8, Pallas kernels: 12.7 us -> 12.3 us  [call(): pl.pallas_call(kernel, out_shape=outputs, in_specs=[VMEM] * len(inputs),...]
where the time goes in v12:
time: 30.7 us; the launch traced here: 30.5 us
  starting transfers between devices  14.1 us (46%)
  Pallas kernels  12.3 us (40%)
  waiting for transfers between devices  2.41 us (8%)
  between operations  0.82 us (3%)
  local copies, waits for them, and re-layouts  0.72 us (2%)
    pallas_call x8, Pallas kernels, call(): pl.pallas_call(kernel, out_shape=outputs, in_specs=[VMEM] * len(inputs),...  12.3 us
    ppermute x2, starting transfers between devices, on_device(): planes = [packed] + [lax.ppermute(packed, 'gy', path) for path in paths]  4.28 us
    ppermute x2, starting transfers between devices, on_device(): lax.ppermute(lax.dynamic_index_in_dim(slab, upper, 1, False), 'gz', far)  4.09 us
    ppermute x2, starting transfers between devices, on_device(): lax.ppermute(lax.dynamic_index_in_dim(slab, 1 - upper, 1, False), 'gz', n...  2.39 us
    ppermute x2, starting transfers between devices, on_device(): lax.ppermute(packed, 'gx', far)  2.03 us
    ppermute x2, starting transfers between devices, across(): return lax.ppermute(value, ('gx', 'gy'), pairs)  1.25 us
    ppermute x2, waiting for transfers between devices, across(): return lax.ppermute(value, ('gx', 'gy'), pairs)  0.95 us
    ppermute x2, waiting for transfers between devices, on_device(): planes = [packed] + [lax.ppermute(packed, 'gy', path) for path in paths]  0.81 us
  transfers between devices with their start and end apart: 12, of which 5 were waited for; matrix products, arithmetic and copies ran while one was open for 0% of the time, Pallas kernels for 31%

profile of v12, /device:TPU:0, one launch (start us, length us, event | category | flops | bytes accessed | tf_op | source)
XLA Modules:
  0.0 30.5 jit_solution(869701168385534049)
XLA Ops:
  0.6 0.0 copy-start.2
  0.6 0.0 copy-start.3
  0.6 0.0 copy-start.1
  0.7 0.6 %copy-done.2 = s32[1,1,2]{2,1,0:T(1,128)S(1)} copy-done((s32[1,1,2]{2,1,0:T(1,128)S(1)}, s32[1,1,2]{2,1,0:T(1,128)}, u32[]{:S(2)}) %copy-start.2) | copy-done | bytes 32
  1.3 0.1 compare_select_fusion
  1.4 0.0 copy-done.3
  1.4 0.1 fusion
  1.4 0.0 copy-done.1
  1.5 3.0 %collective-permute-start = (f32[2,4,256]{2,1,0:T(4,128)S(1)}, f32[2,4,256]{2,1,0:T(4,128)S(1)}, u32[]{:S(2)}, u32[]{:S(2)}) collective-permute-start(f32[2,4,256]{2,1,0:T(4,128)S(1)} %get-tuple-element.11.refs_0_.own_ref), channel_id=1, source_target_pairs={{0,4},{4,0},{1,5},{5,1},{2,6},{6,2},{3,7},{7,3},{8,12},{12,8},{9,1... | collective-permute-start | bytes 24584 | tf_op jit(solution)/shard_map/ppermute | solution.py:286
  4.5 0.6 %collective-permute-start.2 = (f32[2,4,256]{2,1,0:T(4,128)S(1)}, f32[2,4,256]{2,1,0:T(4,128)S(1)}, u32[]{:S(2)}, u32[]{:S(2)}) collective-permute-start(f32[2,4,256]{2,1,0:T(4,128)S(1)} %get-tuple-element.11.refs_0_.own_ref), channel_id=1, source_target_pairs={{0,28},{4,24},{8,20},{12,16},{16,12},{20,8},{24,4},{28,0},{1,29},{... | collective-permute-start | bytes 24584 | tf_op jit(solution)/shard_map/ppermute | solution.py:247
  5.1 0.7 %collective-permute-start.3 = (f32[2,4,256]{2,1,0:T(4,128)S(1)}, f32[2,4,256]{2,1,0:T(4,128)S(1)}, u32[]{:S(2)}, u32[]{:S(2)}) collective-permute-start(f32[2,4,256]{2,1,0:T(4,128)S(1)} %get-tuple-element.11.refs_0_.own_ref), channel_id=1, source_target_pairs={{0,24},{8,16},{16,8},{24,0},{1,25},{9,17},{17,9},{25,1},{2,26},{10... | collective-permute-start | bytes 24584 | tf_op jit(solution)/shard_map/ppermute | solution.py:288
  5.8 0.4 %collective-permute-done.refs_1_ = f32[2,4,256]{2,1,0:T(4,128)S(1)} collective-permute-done((f32[2,4,256]{2,1,0:T(4,128)S(1)}, f32[2,4,256]{2,1,0:T(4,128)S(1)}, u32[]{:S(2)}, u32[]{:S(2)}) %collective-permute-start) | collective-permute-done | bytes 8224 | tf_op jit(solution)/shard_map/ppermute | solution.py:286
  6.1 0.1 collective-permute-start.1
  6.2 1.4 %shard_map.63 = (bf16[2,256,48]{2,1,0:T(8,128)(2,1)S(1)}, f32[2,256,32]{2,1,0:T(8,128)S(1)}) custom-call(f32[2,4,256]{2,1,0:T(4,128)S(1)} %get-tuple-element.11.refs_0_.own_ref, f32[2,4,256]{2,1,0:T(4,128)S(1)} %collective-permute-done.refs_1_), custom_call_target="tpu_custom_call" | custom-call | flops 786432000 | bytes 262144 | tf_op jit(solution)/shard_map/pallas_call | solution.py:253
  7.6 0.0 collective-permute-done.1.near_x_ref
  7.6 0.9 %collective-permute-done.2.refs_0_ = f32[2,4,256]{2,1,0:T(4,128)S(1)} collective-permute-done((f32[2,4,256]{2,1,0:T(4,128)S(1)}, f32[2,4,256]{2,1,0:T(4,128)S(1)}, u32[]{:S(2)}, u32[]{:S(2)}) %collective-permute-start.2) | collective-permute-done | bytes 8224 | tf_op jit(solution)/shard_map/ppermute | solution.py:247
  8.5 0.0 collective-permute-done.3.refs_1_
  8.5 1.6 %collective-permute-start.4 = (f32[6,4,256]{2,1,0:T(4,128)S(1)}, f32[6,4,256]{2,1,0:T(4,128)S(1)}, u32[]{:S(2)}, u32[]{:S(2)}) collective-permute-start(f32[6,4,256]{2,1,0:T(4,128)S(1)} %get-tuple-element.21), channel_id=1, source_target_pairs={{0,1},{1,0},{2,3},{3,2},{4,5},{5,4},{6,7},{7,6},{8,9},{9,8},{10,11... | collective-permute-start | bytes 73736 | tf_op jit(solution)/shard_map/ppermute | solution.py:300
  10.1 2.5 %collective-permute-start.5 = (f32[6,4,256]{2,1,0:T(4,128)S(1)}, f32[6,4,256]{2,1,0:T(4,128)S(1)}, u32[]{:S(2)}, u32[]{:S(2)}) collective-permute-start(f32[6,4,256]{2,1,0:T(4,128)S(1)} %get-tuple-element.20), channel_id=1, source_target_pairs={{0,3},{1,2},{2,1},{3,0},{4,7},{5,6},{6,5},{7,4},{8,11},{9,10},{10,... | collective-permute-start | bytes 73736 | tf_op jit(solution)/shard_map/ppermute | solution.py:299
  12.6 0.0 copy-start
  12.6 2.2 %shard_map.64.before_ref = f32[2,256,32]{2,1,0:T(8,128)S(1)} custom-call(bf16[2,256,48]{2,1,0:T(8,128)(2,1)S(1)} %get-tuple-element.12.target_ref, f32[2,256,32]{2,1,0:T(8,128)S(1)} %get-tuple-element.13.before_ref, f32[2,2,4,256]{3,2,1,0:T(4,128)S(1)} %collective-permute-done.1.near_x_ref, f32[2,4,256]{2,1,0:T(4,128)S(1)} %collective-permute-done.2.refs_0_, ...), custom_call_target="tpu_custom_call" | custom-call | flops 1572864000 | bytes 262144 | tf_op jit(solution)/shard_map/pallas_call | solution.py:253
  14.8 0.0 collective-permute-done.4.source_ref
  14.8 0.0 copy-done
  14.8 1.2 %shard_map.65.bin_ref = f32[2,4,256]{2,1,0:T(4,128)S(1)} custom-call(f32[3,1,1,2,256]{4,3,2,1,0:T(2,128)S(1)} %copy-done, f32[2,4,256]{2,1,0:T(4,128)S(1)} %get-tuple-element.11.refs_0_.own_ref, bf16[2,256,48]{2,1,0:T(8,128)(2,1)S(1)} %get-tuple-element.12.target_ref, f32[2,256,32]{2,1,0:T(8,128)S(1)} %shard_map.64.before_ref, ...), custom_call_target="tpu_custom_call" | custom-call | flops 589824000 | bytes 262144 | tf_op jit(solution)/shard_map/pallas_call | solution.py:253
  16.0 0.0 collective-permute-done.5.source_ref
  16.0 1.1 %shard_map.66 = (f32[2,4,256]{2,1,0:T(4,128)S(1)}, f32[2,4,256]{2,1,0:T(4,128)S(1)}) custom-call(f32[2,4,256]{2,1,0:T(4,128)S(1)} %get-tuple-element.10.keep_ref, f32[2,4,256]{2,1,0:T(4,128)S(1)} %shard_map.65.bin_ref, f32[3,1,1,2,256]{4,3,2,1,0:T(2,128)S(1)} %copy-done, f32[2,4,256]{2,1,0:T(4,128)S(1)} %get-tuple-element.11.refs_0_.own_ref, ...), custom_call_target="tpu_custom_call" | custom-call | flops 589824000 | bytes 262144 | tf_op jit(solution)/shard_map/pallas_call | solution.py:253
  17.2 1.3 %collective-permute-start.6 = (f32[2,4,256]{2,1,0:T(4,128)S(1)}, f32[2,4,256]{2,1,0:T(4,128)S(1)}, u32[]{:S(2)}, u32[]{:S(2)}) collective-permute-start(f32[2,4,256]{2,1,0:T(4,128)S(1)} %get-tuple-element.15.refs_0_.own_ref), channel_id=1, source_target_pairs={{0,4},{4,0},{1,5},{5,1},{2,6},{6,2},{3,7},{7,3},{8,12},{12,8},{9,1... | collective-permute-start | bytes 24584 | tf_op jit(solution)/shard_map/ppermute | solution.py:286
  18.4 0.7 %collective-permute-start.8 = (f32[2,4,256]{2,1,0:T(4,128)S(1)}, f32[2,4,256]{2,1,0:T(4,128)S(1)}, u32[]{:S(2)}, u32[]{:S(2)}) collective-permute-start(f32[2,4,256]{2,1,0:T(4,128)S(1)} %get-tuple-element.15.refs_0_.own_ref), channel_id=1, source_target_pairs={{0,28},{4,24},{8,20},{12,16},{16,12},{20,8},{24,4},{28,0},{1,29},{... | collective-permute-start | bytes 24584 | tf_op jit(solution)/shard_map/ppermute | solution.py:247
  19.1 1.4 %collective-permute-start.9 = (f32[2,4,256]{2,1,0:T(4,128)S(1)}, f32[2,4,256]{2,1,0:T(4,128)S(1)}, u32[]{:S(2)}, u32[]{:S(2)}) collective-permute-start(f32[2,4,256]{2,1,0:T(4,128)S(1)} %get-tuple-element.15.refs_0_.own_ref), channel_id=1, source_target_pairs={{0,24},{8,16},{16,8},{24,0},{1,25},{9,17},{17,9},{25,1},{2,26},{10... | collective-permute-start | bytes 24584 | tf_op jit(solution)/shard_map/ppermute | solution.py:288
  20.4 0.4 %collective-permute-done.6.refs_1_ = f32[2,4,256]{2,1,0:T(4,128)S(1)} collective-permute-done((f32[2,4,256]{2,1,0:T(4,128)S(1)}, f32[2,4,256]{2,1,0:T(4,128)S(1)}, u32[]{:S(2)}, u32[]{:S(2)}) %collective-permute-start.6) | collective-permute-done | bytes 8224 | tf_op jit(solution)/shard_map/ppermute | solution.py:286
  20.9 0.0 collective-permute-start.7
  20.9 1.4 %shard_map.67 = (bf16[2,256,48]{2,1,0:T(8,128)(2,1)S(1)}, f32[2,256,32]{2,1,0:T(8,128)S(1)}) custom-call(f32[2,4,256]{2,1,0:T(4,128)S(1)} %get-tuple-element.15.refs_0_.own_ref, f32[2,4,256]{2,1,0:T(4,128)S(1)} %collective-permute-done.6.refs_1_), custom_call_target="tpu_custom_call" | custom-call | flops 786432000 | bytes 262144 | tf_op jit(solution)/shard_map/pallas_call | solution.py:253
  22.3 0.0 collective-permute-done.7.near_x_ref
  22.3 0.1 collective-permute-done.8.refs_0_
  22.4 0.0 collective-permute-done.9.refs_1_
  22.4 0.8 %collective-permute-start.10 = (f32[6,4,256]{2,1,0:T(4,128)S(1)}, f32[6,4,256]{2,1,0:T(4,128)S(1)}, u32[]{:S(2)}, u32[]{:S(2)}) collective-permute-start(f32[6,4,256]{2,1,0:T(4,128)S(1)} %get-tuple-element.19), channel_id=1, source_target_pairs={{0,1},{1,0},{2,3},{3,2},{4,5},{5,4},{6,7},{7,6},{8,9},{9,8},{10,11... | collective-permute-start | bytes 73736 | tf_op jit(solution)/shard_map/ppermute | solution.py:300
  23.2 1.6 %collective-permute-start.11 = (f32[6,4,256]{2,1,0:T(4,128)S(1)}, f32[6,4,256]{2,1,0:T(4,128)S(1)}, u32[]{:S(2)}, u32[]{:S(2)}) collective-permute-start(f32[6,4,256]{2,1,0:T(4,128)S(1)} %get-tuple-element.18), channel_id=1, source_target_pairs={{0,3},{1,2},{2,1},{3,0},{4,7},{5,6},{6,5},{7,4},{8,11},{9,10},{10,... | collective-permute-start | bytes 73736 | tf_op jit(solution)/shard_map/ppermute | solution.py:299
  24.8 2.2 %shard_map.68.before_ref = f32[2,256,32]{2,1,0:T(8,128)S(1)} custom-call(bf16[2,256,48]{2,1,0:T(8,128)(2,1)S(1)} %get-tuple-element.16.target_ref, f32[2,256,32]{2,1,0:T(8,128)S(1)} %get-tuple-element.17.before_ref, f32[2,2,4,256]{3,2,1,0:T(4,128)S(1)} %collective-permute-done.7.near_x_ref, f32[2,4,256]{2,1,0:T(4,128)S(1)} %collective-permute-done.8.refs_0_, ...), custom_call_target="tpu_custom_call" | custom-call | flops 1572864000 | bytes 262144 | tf_op jit(solution)/shard_map/pallas_call | solution.py:253
  27.0 0.0 collective-permute-done.10.source_ref
  27.0 1.1 %shard_map.69.bin_ref = f32[2,4,256]{2,1,0:T(4,128)S(1)} custom-call(f32[2,4,256]{2,1,0:T(4,128)S(1)} %get-tuple-element.14.speed_ref, f32[2,4,256]{2,1,0:T(4,128)S(1)} %get-tuple-element.15.refs_0_.own_ref, bf16[2,256,48]{2,1,0:T(8,128)(2,1)S(1)} %get-tuple-element.16.target_ref, f32[2,256,32]{2,1,0:T(8,128)S(1)} %shard_map.68.before_ref, ...), custom_call_target="tpu_custom_call" | custom-call | flops 589824000 | bytes 262144 | tf_op jit(solution)/shard_map/pallas_call | solution.py:253
  28.2 0.6 %collective-permute-done.11.source_ref = f32[6,4,256]{2,1,0:T(4,128)S(1)} collective-permute-done((f32[6,4,256]{2,1,0:T(4,128)S(1)}, f32[6,4,256]{2,1,0:T(4,128)S(1)}, u32[]{:S(2)}, u32[]{:S(2)}) %collective-permute-start.11) | collective-permute-done | bytes 24608 | tf_op jit(solution)/shard_map/ppermute | solution.py:299
  28.8 1.7 %shard_map.70 = (f32[3,1,1,2,256]{4,3,2,1,0:T(2,128)}, f32[3,1,1,2,256]{4,3,2,1,0:T(2,128)}) custom-call(f32[2,4,256]{2,1,0:T(4,128)S(1)} %get-tuple-element.10.keep_ref, f32[2,4,256]{2,1,0:T(4,128)S(1)} %shard_map.69.bin_ref, f32[2,4,256]{2,1,0:T(4,128)S(1)} %get-tuple-element.14.speed_ref, f32[2,4,256]{2,1,0:T(4,128)S(1)} %get-tuple-element.15.refs_0_.own_ref, ...), custom_call_target="tpu_custom_call" | custom-call | flops 589824000 | bytes 262144 | tf_op jit(solution)/shard_map/pallas_call | solution.py:253
  (16 shorter events, 0.1 us)
Async XLA Ops:
  0.6 0.7 %copy-start.2 = (s32[1,1,2]{2,1,0:T(1,128)S(1)}, s32[1,1,2]{2,1,0:T(1,128)}, u32[]{:S(2)}) copy-start(s32[1,1,2]{2,1,0:T(1,128)} %param.7) | copy-start | bytes 28
  0.6 0.7 %copy-start.3 = (f32[1,1,2,256]{3,2,1,0:T(2,128)S(1)}, f32[1,1,2,256]{3,2,1,0:T(2,128)}, u32[]{:S(2)}) copy-start(f32[1,1,2,256]{3,2,1,0:T(2,128)} %param.6) | copy-start | bytes 6148
  0.6 0.8 %copy-start.1 = (f32[3,1,1,2,256]{4,3,2,1,0:T(2,128)S(1)}, f32[3,1,1,2,256]{4,3,2,1,0:T(2,128)}, u32[]{:S(2)}) copy-start(f32[3,1,1,2,256]{4,3,2,1,0:T(2,128)} %param.4) | copy-start | bytes 18436
  1.5 4.7 %collective-permute-start = (f32[2,4,256]{2,1,0:T(4,128)S(1)}, f32[2,4,256]{2,1,0:T(4,128)S(1)}, u32[]{:S(2)}, u32[]{:S(2)}) collective-permute-start(f32[2,4,256]{2,1,0:T(4,128)S(1)} %get-tuple-element.11.refs_0_.own_ref), channel_id=1, source_target_pairs={{0,4},{4,0},{1,5},{5,1},{2,6},{6,2},{3,7},{7,3},{8,12},{12,8},{9,1... | collective-permute-start | bytes 24584 | tf_op jit(solution)/shard_map/ppermute | solution.py:286
  4.5 4.0 %collective-permute-start.2 = (f32[2,4,256]{2,1,0:T(4,128)S(1)}, f32[2,4,256]{2,1,0:T(4,128)S(1)}, u32[]{:S(2)}, u32[]{:S(2)}) collective-permute-start(f32[2,4,256]{2,1,0:T(4,128)S(1)} %get-tuple-element.11.refs_0_.own_ref), channel_id=1, source_target_pairs={{0,28},{4,24},{8,20},{12,16},{16,12},{20,8},{24,4},{28,0},{1,29},{... | collective-permute-start | bytes 24584 | tf_op jit(solution)/shard_map/ppermute | solution.py:247
  5.1 3.4 %collective-permute-start.3 = (f32[2,4,256]{2,1,0:T(4,128)S(1)}, f32[2,4,256]{2,1,0:T(4,128)S(1)}, u32[]{:S(2)}, u32[]{:S(2)}) collective-permute-start(f32[2,4,256]{2,1,0:T(4,128)S(1)} %get-tuple-element.11.refs_0_.own_ref), channel_id=1, source_target_pairs={{0,24},{8,16},{16,8},{24,0},{1,25},{9,17},{17,9},{25,1},{2,26},{10... | collective-permute-start | bytes 24584 | tf_op jit(solution)/shard_map/ppermute | solution.py:288
  6.1 1.4 %collective-permute-start.1 = (f32[2,2,4,256]{3,2,1,0:T(4,128)S(1)}, f32[2,2,4,256]{3,2,1,0:T(4,128)S(1)}, u32[]{:S(2)}, u32[]{:S(2)}) collective-permute-start(f32[2,2,4,256]{3,2,1,0:T(4,128)S(1)} %pad_maximum_fusion), channel_id=1, source_target_pairs={{0,8},{8,0},{16,24},{24,16},{1,9},{9,1},{17,25},{25,17},{2,10},{10... | collective-permute-start | bytes 49160 | tf_op jit(solution)/shard_map/ppermute | solution.py:290
  8.5 6.3 %collective-permute-start.4 = (f32[6,4,256]{2,1,0:T(4,128)S(1)}, f32[6,4,256]{2,1,0:T(4,128)S(1)}, u32[]{:S(2)}, u32[]{:S(2)}) collective-permute-start(f32[6,4,256]{2,1,0:T(4,128)S(1)} %get-tuple-element.21), channel_id=1, source_target_pairs={{0,1},{1,0},{2,3},{3,2},{4,5},{5,4},{6,7},{7,6},{8,9},{9,8},{10,11... | collective-permute-start | bytes 73736 | tf_op jit(solution)/shard_map/ppermute | solution.py:300
  10.1 5.9 %collective-permute-start.5 = (f32[6,4,256]{2,1,0:T(4,128)S(1)}, f32[6,4,256]{2,1,0:T(4,128)S(1)}, u32[]{:S(2)}, u32[]{:S(2)}) collective-permute-start(f32[6,4,256]{2,1,0:T(4,128)S(1)} %get-tuple-element.20), channel_id=1, source_target_pairs={{0,3},{1,2},{2,1},{3,0},{4,7},{5,6},{6,5},{7,4},{8,11},{9,10},{10,... | collective-permute-start | bytes 73736 | tf_op jit(solution)/shard_map/ppermute | solution.py:299
  12.6 2.2 %copy-start = (f32[3,1,1,2,256]{4,3,2,1,0:T(2,128)S(1)}, f32[3,1,1,2,256]{4,3,2,1,0:T(2,128)}, u32[]{:S(2)}) copy-start(f32[3,1,1,2,256]{4,3,2,1,0:T(2,128)} %speed_ref.3) | copy-start | bytes 18436
  17.2 3.7 %collective-permute-start.6 = (f32[2,4,256]{2,1,0:T(4,128)S(1)}, f32[2,4,256]{2,1,0:T(4,128)S(1)}, u32[]{:S(2)}, u32[]{:S(2)}) collective-permute-start(f32[2,4,256]{2,1,0:T(4,128)S(1)} %get-tuple-element.15.refs_0_.own_ref), channel_id=1, source_target_pairs={{0,4},{4,0},{1,5},{5,1},{2,6},{6,2},{3,7},{7,3},{8,12},{12,8},{9,1... | collective-permute-start | bytes 24584 | tf_op jit(solution)/shard_map/ppermute | solution.py:286
  18.4 4.0 %collective-permute-start.8 = (f32[2,4,256]{2,1,0:T(4,128)S(1)}, f32[2,4,256]{2,1,0:T(4,128)S(1)}, u32[]{:S(2)}, u32[]{:S(2)}) collective-permute-start(f32[2,4,256]{2,1,0:T(4,128)S(1)} %get-tuple-element.15.refs_0_.own_ref), channel_id=1, source_target_pairs={{0,28},{4,24},{8,20},{12,16},{16,12},{20,8},{24,4},{28,0},{1,29},{... | collective-permute-start | bytes 24584 | tf_op jit(solution)/shard_map/ppermute | solution.py:247
  19.1 3.3 %collective-permute-start.9 = (f32[2,4,256]{2,1,0:T(4,128)S(1)}, f32[2,4,256]{2,1,0:T(4,128)S(1)}, u32[]{:S(2)}, u32[]{:S(2)}) collective-permute-start(f32[2,4,256]{2,1,0:T(4,128)S(1)} %get-tuple-element.15.refs_0_.own_ref), channel_id=1, source_target_pairs={{0,24},{8,16},{16,8},{24,0},{1,25},{9,17},{17,9},{25,1},{2,26},{10... | collective-permute-start | bytes 24584 | tf_op jit(solution)/shard_map/ppermute | solution.py:288
  20.9 1.4 %collective-permute-start.7 = (f32[2,2,4,256]{3,2,1,0:T(4,128)S(1)}, f32[2,2,4,256]{3,2,1,0:T(4,128)S(1)}, u32[]{:S(2)}, u32[]{:S(2)}) collective-permute-start(f32[2,2,4,256]{3,2,1,0:T(4,128)S(1)} %pad_maximum_fusion.1), channel_id=1, source_target_pairs={{0,8},{8,0},{16,24},{24,16},{1,9},{9,1},{17,25},{25,17},{2,10},{10... | collective-permute-start | bytes 49160 | tf_op jit(solution)/shard_map/ppermute | solution.py:290
  22.4 4.6 %collective-permute-start.10 = (f32[6,4,256]{2,1,0:T(4,128)S(1)}, f32[6,4,256]{2,1,0:T(4,128)S(1)}, u32[]{:S(2)}, u32[]{:S(2)}) collective-permute-start(f32[6,4,256]{2,1,0:T(4,128)S(1)} %get-tuple-element.19), channel_id=1, source_target_pairs={{0,1},{1,0},{2,3},{3,2},{4,5},{5,4},{6,7},{7,6},{8,9},{9,8},{10,11... | collective-permute-start | bytes 73736 | tf_op jit(solution)/shard_map/ppermute | solution.py:300
  23.2 5.6 %collective-permute-start.11 = (f32[6,4,256]{2,1,0:T(4,128)S(1)}, f32[6,4,256]{2,1,0:T(4,128)S(1)}, u32[]{:S(2)}, u32[]{:S(2)}) collective-permute-start(f32[6,4,256]{2,1,0:T(4,128)S(1)} %get-tuple-element.18), channel_id=1, source_target_pairs={{0,3},{1,2},{2,1},{3,0},{4,7},{5,6},{6,5},{7,4},{8,11},{9,10},{10,... | collective-permute-start | bytes 73736 | tf_op jit(solution)/shard_map/ppermute | solution.py:299
